TPU v7x, 512 devices: a whole 4x8x8 slice. The times are simulated.
512 devices in a mesh: dp: 16 (over z_hi, x), st: 32 (over y, z_lo, core).
Axes of the slice: x: 4, y: 8, z: 8 (z_hi: 4, z_lo: 2; z = z_hi * 2 + z_lo), core: 2. Of those that a mesh axis runs over, the one named last changes fastest.
Arguments:
- grad_out: bfloat16 [4096, 8192], P(('dp', 'st')), may hold values from -6 to 6
- w_down: bfloat16 [26624, 8192], P('st', 'dp'), may hold values from -0.0625 to 0.0625
- gate_pre: bfloat16 [4096, 26624], P('dp', 'st'), may hold values from -8 to 8
- up_pre: bfloat16 [4096, 26624], P('dp', 'st'), may hold values from -6 to 6
- rank_in: bfloat16 [4096, 128], P(('dp', 'st')), may hold values from -0.09375 to 0.09375
- rank_hidden: bfloat16 [4096, 64], P(('dp', 'st')), may hold values from -0.09375 to 0.09375
- a_down: bfloat16 [26624, 64], P('st'), may hold values from -0.75 to 0.75
- b_down: bfloat16 [64, 8192], P(None, 'st'), may hold values from -0.0625 to 0.0625
- b_in: bfloat16 [2, 64, 26624], P(None, None, 'st'), may hold values from -0.0390625 to 0.0390625
- a_in: bfloat16 [8192, 128], replicated, may hold values from -0.75 to 0.75
Outputs:
- input_grad: bfloat16 [4096, 8192], P(('dp', 'st'))
- grad_b_in: float32 [2, 64, 26624], P(None, None, 'st')
- grad_b_down: float32 [64, 8192], P(None, 'st')
All inputs are finite; a program needn't handle non-finite values.
Results may differ from a plain program's by a relative error of at most 0.009.
Values may be sent and summed in bfloat16 or wider, within the bound.
No kernel may reach another device: no remote copies, remote signals or barrier semaphores. Data moves between devices by JAX's collectives and lax.ppermute only.
A program may use at most 64 MiB of HBM per device.

v0:
```python
import jax
import jax.numpy as jnp
from jax import lax
from jax.sharding import PartitionSpec as P


def contract_last(left, right):
    return lax.dot_general(
        left, right, (((1,), (1,)), ((), ())), preferred_element_type=jnp.float32
    )


def contract_first(left, right):
    return lax.dot_general(
        left, right, (((0,), (0,)), ((), ())), preferred_element_type=jnp.float32
    )


def shards(grad_out, w_down, gate_pre, up_pre, rank_in, rank_hidden, a_down, b_down, b_in, a_in):
    rank_size = rank_hidden.shape[1]
    grad_rows = lax.all_gather(grad_out, "st", axis=0, tiled=True)
    frozen = contract_last(grad_rows, lax.all_gather(w_down, "dp", axis=1, tiled=True))
    saved_in, saved_hidden = (
        lax.all_gather(rank_in, "st", axis=0, tiled=True),
        lax.all_gather(rank_hidden, "st", axis=0, tiled=True),
    )
    band_width = b_down.shape[1]
    own_band = lax.dynamic_slice_in_dim(grad_rows, lax.axis_index("st") * band_width, band_width, 1)
    band_partial = contract_last(own_band, b_down)
    down_rank = lax.psum(band_partial, "st").astype(jnp.bfloat16)
    grad_hidden = frozen + contract_last(down_rank, a_down)
    gate_value = gate_pre.astype(jnp.float32)
    up_value = up_pre.astype(jnp.float32)
    sigmoid_gate = jax.nn.sigmoid(gate_value)
    grad_up = (grad_hidden * gate_value * sigmoid_gate).astype(jnp.bfloat16)
    grad_gate = (
        grad_hidden * up_value * sigmoid_gate * (1.0 + gate_value * (1.0 - sigmoid_gate))
    ).astype(jnp.bfloat16)
    grad_b_gate = contract_first(saved_in[:, :rank_size], grad_gate)
    grad_b_up = contract_first(saved_in[:, rank_size:], grad_up)
    partial_in = jnp.stack([grad_b_gate, grad_b_up])
    partial_down = contract_first(saved_hidden, own_band)
    grad_b_in, grad_b_down = lax.psum((partial_in, partial_down), "dp")
    rank_grad = lax.psum_scatter(
        jnp.concatenate(
            [contract_last(grad_gate, b_in[0]), contract_last(grad_up, b_in[1])], axis=1
        ),
        "st",
        scatter_dimension=0,
        tiled=True,
    ).astype(jnp.bfloat16)
    input_grad = contract_last(rank_grad, a_in).astype(jnp.bfloat16)
    return (input_grad, grad_b_in, grad_b_down)


def solution(mesh):
    placed = (
        P(("dp", "st"), None),
        P("st", "dp"),
        P("dp", "st"),
        P("dp", "st"),
        P(("dp", "st"), None),
        P(("dp", "st"), None),
        P("st", None),
        P(None, "st"),
        P(None, None, "st"),
        P(),
    )
    return jax.shard_map(
        shards,
        mesh=mesh,
        in_specs=placed,
        out_specs=(P(("dp", "st"), None), P(None, None, "st"), P(None, "st")),
        check_vma=False,
    )
```

profile of v0, /device:TPU:8, one launch (start us, length us, event | category | flops | bytes accessed | tf_op | source)
XLA Modules:
  0.0 465.7 jit_solution(10446573790304904492)
XLA Ops:
  7.2 0.7 all-gather.3.cloned.1.call-update
  8.0 0.7 all-gather.5.cloned.1.call-update
  8.7 1.3 dynamic-slice
  10.6 34.1 %all_gather.15 = bf16[256,64]{1,0:T(8,128)(2,1)S(1)} all-gather(bf16[8,64]{1,0:T(8,128)(2,1)} %param.15), channel_id=1, replica_groups=mesh['dp'=16,'st'=32] {'st'}, dimensions={0}, use_global_device_ids=true | all-gather | bytes 33792 | tf_op jit(solution)/shard_map/all_gather | solution.py:25
  44.8 32.6 %all_gather.14 = bf16[256,128]{1,0:T(8,128)(2,1)S(1)} all-gather(bf16[8,128]{1,0:T(8,128)(2,1)} %param.14), channel_id=1, replica_groups=mesh['dp'=16,'st'=32] {'st'}, dimensions={0}, use_global_device_ids=true | all-gather | bytes 67584 | tf_op jit(solution)/shard_map/all_gather | solution.py:24
  77.4 5.9 %all-gather.3.cloned.1.call-done = bf16[256,8192]{1,0:T(8,128)(2,1)} async-done(((bf16[8,8192]{1,0:T(8,128)(2,1)}), bf16[256,8192]{1,0:T(8,128)(2,1)}) %all-gather.3.cloned.1.call-update) | async-done | bytes 4194320 | tf_op jit(solution)/shard_map/all_gather | solution.py:21
  83.3 1.1 fusion.9
  84.3 106.2 %psum.21 = bf16[256,64]{1,0:T(8,128)(2,1)S(1)} all-reduce(f32[256,64]{1,0:T(8,128)S(1)} %fusion.9), channel_id=1, replica_groups=mesh['dp'=16,'st'=32] {'st'}, use_global_device_ids=true, to_apply=%region_0.0 | all-reduce | flops 16384 | bytes 98304 | tf_op jit(solution)/shard_map/psum | solution.py:30
  190.5 1.7 convolution_bitcast_fusion.2
  192.3 81.9 %all-gather.5.cloned.1.call-done = bf16[832,8192]{1,0:T(8,128)(2,1)} async-done(((bf16[832,512]{1,0:T(8,128)(2,1)}), bf16[832,8192]{1,0:T(8,128)(2,1)}) %all-gather.5.cloned.1.call-update) | async-done | bytes 13631504 | tf_op jit(solution)/shard_map/all_gather | solution.py:22
  274.1 8.1 %fusion.23 = f32[256,832]{0,1:T(8,128)S(1)} fusion(bf16[256,8192]{1,0:T(8,128)(2,1)} %all-gather.3.cloned.1.call-done, bf16[832,8192]{1,0:T(8,128)(2,1)} %all-gather.5.cloned.1.call-done), kind=kOutput, calls=%fused_computation.34 | convolution fusion | flops 3489660928 | bytes 18677760 | tf_op jit(solution)/shard_map/dot_general | solution.py:8
  282.3 0.6 fusion.5
  282.9 0.3 copy-done.1
  283.2 0.3 fusion.11
  283.5 0.3 fusion.13
  283.8 0.3 convolution_bitcast_fusion
  284.2 0.3 convolution_bitcast_fusion.1
  284.5 0.8 pad_maximum_fusion
  285.3 0.1 pad_maximum_fusion.1
  285.4 100.6 %all-reduce.6 = bf16[256,128]{1,0:T(8,128)(2,1)S(1)} all-reduce(f32[256,128]{1,0:T(8,128)S(1)} %pad_maximum_fusion.1), channel_id=2, replica_groups=mesh['dp'=16,'st'=32] {'st'}, use_global_device_ids=true, to_apply=%region_1.0.clone | all-reduce | flops 32768 | bytes 196608
  386.0 1.3 convolution_convert_fusion
  387.3 68.6 %all-reduce.5.cloned.1.call-done = (f32[2,64,832]{2,1,0:T(8,128)}, f32[64,256]{1,0:T(8,128)}) async-done(((f32[2,64,832]{2,1,0:T(8,128)}, f32[64,256]{1,0:T(8,128)}), (f32[2,64,832]{2,1,0:T(8,128)}, f32[64,256]{1,0:T(8,128)})) %all-reduce.5.cloned.1.call-update) | async-done | bytes 491536 | tf_op jit(solution)/shard_map/psum | solution.py:43
  455.9 1.8 copy.17
  457.7 1.5 copy.18
  (13 shorter events, 0.2 us)
Async XLA Ops:
  7.2 378.8 %copy-start = (bf16[8192,128]{1,0:T(8,128)(2,1)S(1)}, bf16[8192,128]{1,0:T(8,128)(2,1)}, u32[]{:S(2)}) copy-start(bf16[8192,128]{1,0:T(8,128)(2,1)} %param.19) | copy-start | bytes 6291460
  7.2 76.1 %all-gather.3.cloned.1.call-start = ((), (), s32[]{:S(2)}) async-start(), calls=%async_computation | async-start | bytes 4325376 | tf_op jit(solution)/shard_map/all_gather | solution.py:21
  7.9 266.2 %all-gather.5.cloned.1.call-start = ((), (), s32[]{:S(2)}) async-start(), calls=%async_computation.1 | async-start | bytes 14483456 | tf_op jit(solution)/shard_map/all_gather | solution.py:22
  8.7 447.2 %all-reduce.5.cloned.1.call-start = ((), (), s32[]{:S(2)}) async-start(), calls=%async_computation.2 | async-start | bytes 1048576 | tf_op jit(solution)/shard_map/psum | solution.py:43
  192.3 90.0 %copy-start.2 = (bf16[256,832]{0,1:T(8,128)(2,1)S(1)}, bf16[256,832]{0,1:T(8,128)(2,1)}, u32[]{:S(2)}) copy-start(bf16[256,832]{0,1:T(8,128)(2,1)} %param.12) | copy-start | bytes 1277956
  192.3 90.0 %copy-start.3 = (bf16[256,832]{0,1:T(8,128)(2,1)S(1)}, bf16[256,832]{0,1:T(8,128)(2,1)}, u32[]{:S(2)}) copy-start(bf16[256,832]{0,1:T(8,128)(2,1)} %param.13) | copy-start | bytes 1277956
  192.3 90.0 %copy-start.4 = (bf16[832,64]{0,1:T(8,128)(2,1)S(1)}, bf16[832,64]{0,1:T(8,128)(2,1)}, u32[]{:S(2)}) copy-start(bf16[832,64]{0,1:T(8,128)(2,1)} %param.16) | copy-start | bytes 319492
  282.2 0.9 copy-start.1
Sparse Core Ops, SparseCore 0:
  10.2 73.0 all-gather.2
  86.3 187.8 all-gather.4
  285.4 170.4 all-reduce.4
where the time goes:
time: 466 us
  blocking collectives  274 us (59%)
  waiting for transfers between devices  158 us (34%)
  between operations  14.5 us (3%)
  matrix products  14 us (3%)
  local copies, waits for them, and re-layouts  4.89 us (1%)
    psum x1, blocking collectives, shards(): down_rank = lax.psum(band_partial, 'st').astype(jnp.bfloat16)  106 us
    unnamed x1, blocking collectives  101 us
    all_gather x1, waiting for transfers between devices, shards(): lax.all_gather(w_down, 'dp', axis=1, tiled=True)  81.9 us
    psum x1, waiting for transfers between devices, shards(): grad_b_in, grad_b_down = lax.psum((partial_in, partial_down), 'dp')  68.6 us
    all_gather x1, blocking collectives, shards(): lax.all_gather(rank_hidden, 'st', axis=0, tiled=True)  34.1 us
    all_gather x1, blocking collectives, shards(): lax.all_gather(rank_in, 'st', axis=0, tiled=True)  32.6 us
    dot_general x6, matrix products, contract_last(): lax.dot_general(left, right, (((1,), (1,)), ((), ())), preferred_element_...  11.7 us
  transfers between devices with their start and end apart: 3, of which 3 were waited for; matrix products, arithmetic and copies ran while one was open for 1% of the time, Pallas kernels for 0%

commit v1 on v0

v1 whole, which is shorter than its diff:
```python
import jax
import jax.numpy as jnp
import numpy as np
from jax import lax
from jax.sharding import Mesh, PartitionSpec as P

AXES = ("zh", "x", "yh", "yl", "zl", "c")
SIZES = (4, 4, 4, 2, 2, 2)
Y = ("yh", "yl")
DP = ("zh", "x")
ST = ("yh", "yl", "zl", "c")
TOKEN_ORDER = ("c", "yh", "yl", "zl")
F32, BF16 = jnp.float32, jnp.bfloat16


def contract_last(left, right):
    return lax.dot_general(left, right, (((1,), (1,)), ((), ())), preferred_element_type=F32)


def contract_first(left, right):
    return lax.dot_general(left, right, (((0,), (0,)), ((), ())), preferred_element_type=F32)


def exchange(blocks, axes):
    return lax.all_to_all(blocks, axes, 0, 0, tiled=True)


def spread(block, axes, count):
    return exchange(jnp.broadcast_to(block[None], (count,) + block.shape), axes)


def band_pairs():
    index = np.arange(512).reshape(SIZES)
    pairs = []
    for zh in range(4):
        for x in range(4):
            for yh in range(4):
                for yl in range(2):
                    for zl in range(2):
                        for c in range(2):
                            pairs.append((int(index[yh, x, zh, yl, zl, c]), int(index[zh, x, yh, yl, zl, c])))
    return pairs


def shards(grad_out, w_down, gate_pre, up_pre, rank_in, rank_hidden, a_down, b_down, b_in, a_in):
    quarters = grad_out.reshape(8, 4, 2048).transpose(1, 0, 2)
    to_z = jnp.broadcast_to(quarters[:, None], (4, 2, 8, 2048)).reshape(8, 8, 2048)
    from_z = exchange(to_z, ("zh", "zl")).reshape(4, 16, 2048)
    from_y = lax.all_gather(from_z, Y, axis=1, tiled=True)
    grad_rows = lax.all_gather(from_y, "c", axis=1, tiled=True)
    w_blocks = spread(w_down, "x", 4)
    own_band = lax.ppermute(b_down, AXES, band_pairs())
    bands = spread(own_band, ("yl", "zl", "c"), 8).transpose(1, 0, 2).reshape(64, 2048)
    weights = w_blocks.transpose(1, 0, 2).reshape(832, 2048).astype(F32)
    weights = (weights + jnp.dot(a_down, bands, preferred_element_type=F32)).astype(BF16)
    ranks = jnp.concatenate([rank_in, rank_hidden], axis=1)
    ranks = spread(spread(ranks, "zh", 4), TOKEN_ORDER, 32)
    ranks = ranks.transpose(1, 0, 2, 3).reshape(4, 256, 192)
    saved_in = lax.dynamic_index_in_dim(ranks, lax.axis_index("zh"), 0, False)[:, :128]
    saved_hidden = ranks[:, :, 128:].reshape(1024, 64)
    rows = grad_rows.reshape(1024, 2048)
    partial = contract_last(rows, weights).astype(BF16).reshape(4, 256, 832)
    grad_hidden = jnp.sum(exchange(partial, "zh").astype(F32), axis=0)

    def by_token(saved):
        return saved.reshape(16, 2, 8, 832).transpose(1, 0, 2, 3).reshape(256, 832).astype(F32)

    gate_value, up_value = by_token(gate_pre), by_token(up_pre)
    sigmoid_gate = jax.nn.sigmoid(gate_value)
    grad_up = (grad_hidden * gate_value * sigmoid_gate).astype(BF16)
    grad_gate = (
        grad_hidden * up_value * sigmoid_gate * (1.0 + gate_value * (1.0 - sigmoid_gate))
    ).astype(BF16)
    partial_in = jnp.concatenate(
        [contract_first(saved_in[:, :64], grad_gate), contract_first(saved_in[:, 64:], grad_up)], axis=0
    )
    station = lax.axis_index(ST)
    band = lax.dynamic_slice_in_dim(rows, (station % 8) * 256, 256, 1)
    partial_down = contract_first(saved_hidden, band)
    partial_down = jnp.where(station // 8 == lax.axis_index("zh"), partial_down, 0.0)
    sums = jnp.concatenate([partial_in.reshape(16, 8, 832), partial_down.reshape(16, 8, 128)], axis=2)
    sums = jnp.sum(exchange(sums.astype(BF16), DP).astype(F32), axis=0).astype(BF16)
    sums = spread(sums, DP, 16).astype(F32)
    grad_b_in = sums[:, :, :832].reshape(2, 64, 832)
    grad_b_down = sums[:, :, 832:].reshape(64, 256)
    rank_partial = jnp.concatenate(
        [contract_last(grad_gate, b_in[0]), contract_last(grad_up, b_in[1])], axis=1
    )
    rank_grad = jnp.sum(exchange(rank_partial.reshape(32, 8, 128), TOKEN_ORDER), axis=0).astype(BF16)
    input_grad = contract_last(rank_grad, a_in).astype(BF16)
    return (input_grad, grad_b_in, grad_b_down)


def solution(mesh):
    fine = Mesh(mesh.devices.reshape(SIZES), AXES)
    placed = (
        P(AXES, None),
        P(ST, DP),
        P(DP, ST),
        P(DP, ST),
        P(AXES, None),
        P(AXES, None),
        P(ST, None),
        P(None, ST),
        P(None, None, ST),
        P(),
    )
    return jax.shard_map(
        shards,
        mesh=fine,
        in_specs=placed,
        out_specs=(P(AXES, None), P(None, None, ST), P(None, ST)),
        check_vma=False,
    )
```

time: 466 us -> 291 us (0.62)
  blocking collectives: 274 us -> 49.4 us
  starting transfers between devices: 0.11 us -> 46.2 us
  waiting for transfers between devices: 158 us -> 128 us
  local copies, waits for them, and re-layouts: 4.89 us -> 25 us
  other arithmetic: 0.9 us -> 9.77 us
    psum x1 -> x0, blocking collectives: 106 us -> none  [shards(): down_rank = lax.psum(band_partial, 'st').astype(jnp.bfloat16)]
    unnamed x1 -> x0, blocking collectives: 101 us -> none
    all_to_all x0 -> x6, waiting for transfers between devices: none -> 88.4 us  [exchange(): return lax.all_to_all(blocks, axes, 0, 0, tiled=True)]
    psum x1 -> x0, waiting for transfers between devices: 68.6 us -> none  [shards(): grad_b_in, grad_b_down = lax.psum((partial_in, partial_down), 'dp')]
    all_gather x2 -> x0, blocking collectives: 66.8 us -> none  [the longest x1 34.1 us: shards(): lax.all_gather(rank_hidden, 'st', axis=0, tiled=True)]
    all_to_all x0 -> x3, blocking collectives: none -> 49.4 us  [exchange(): return lax.all_to_all(blocks, axes, 0, 0, tiled=True)]
    all_gather x2, waiting for transfers between devices: 87.7 us -> 39.6 us  [the longest x1 39.6 us: shards(): from_y = lax.all_gather(from_z, Y, axis=1, tiled=True)]
    all_to_all x0 -> x6, starting transfers between devices: none -> 44.7 us  [exchange(): return lax.all_to_all(blocks, axes, 0, 0, tiled=True)]
  transfers between devices with their start and end apart: 3 -> 9, of which waited for: 3 -> 6; matrix products, arithmetic and copies ran while one was open for 1% -> 13% of each run, Pallas kernels for 0% -> 0%
where the time goes in v1:
time: 291 us; the launch traced here: 290 us
  waiting for transfers between devices  128 us (44%)
  blocking collectives  49.4 us (17%)
  starting transfers between devices  46.2 us (16%)
  local copies, waits for them, and re-layouts  25 us (9%)
  matrix products  17.2 us (6%)
  between operations  14.3 us (5%)
  other arithmetic  9.77 us (3%)
    all_to_all x6, waiting for transfers between devices, exchange(): return lax.all_to_all(blocks, axes, 0, 0, tiled=True)  88.4 us
    all_to_all x3, blocking collectives, exchange(): return lax.all_to_all(blocks, axes, 0, 0, tiled=True)  49.4 us
    all_to_all x6, starting transfers between devices, exchange(): return lax.all_to_all(blocks, axes, 0, 0, tiled=True)  44.7 us
    all_gather x1, waiting for transfers between devices, shards(): from_y = lax.all_gather(from_z, Y, axis=1, tiled=True)  39.6 us
    dot_general x4, matrix products, contract_last(): lax.dot_general(left, right, (((1,), (1,)), ((), ())), preferred_element_...  13.6 us
    convert_element_type x4, local copies, waits for them, and re-layouts, by_token(): saved.reshape(16, 2, 8, 832).transpose(1, 0, 2, 3).reshape(256, 832)  6.75 us
  transfers between devices with their start and end apart: 9, of which 6 were waited for; matrix products, arithmetic and copies ran while one was open for 13% of the time, Pallas kernels for 0%

profile of v1, /device:TPU:8, one launch (start us, length us, event | category | flops | bytes accessed | tf_op | source)
XLA Modules:
  0.0 289.9 jit_solution(17156225377883607982)
XLA Ops:
  8.3 22.1 %all_to_all.45 = bf16[8,8,2048]{2,1,0:T(8,128)(2,1)} all-to-all(bf16[8,8,2048]{2,1,0:T(8,128)(2,1)S(1)} %bitcast.100), channel_id=1, replica_groups=mesh['zh'=4,'x'=4,'yh'=4,'yl'=2,'zl'=2,'c'=2] {'zh','zl'}, dimensions={0} | all-to-all | bytes 524288 | tf_op jit(solution)/shard_map/all_to_all | solution.py:25
  30.5 39.6 %all-gather.3.cloned.1.call-done = bf16[4,128,2048]{2,1,0:T(8,128)(2,1)} async-done(((bf16[4,16,2048]{2,1,0:T(8,128)(2,1)}), bf16[4,128,2048]{2,1,0:T(8,128)(2,1)}) %all-gather.3.cloned.1.call-update) | async-done | bytes 2097168 | tf_op jit(solution)/shard_map/all_gather | solution.py:49
  72.3 17.7 %all_to_all.46 = bf16[4,8,192]{2,1,0:T(8,128)(2,1)S(1)} all-to-all(bf16[4,8,192]{2,1,0:T(8,128)(2,1)S(1)} %broadcast_in_dim.18), channel_id=1, replica_groups=mesh['zh'=4,'x'=4,'yh'=4,'yl'=2,'zl'=2,'c'=2] {'zh'}, dimensions={0} | all-to-all | bytes 24576 | tf_op jit(solution)/shard_map/all_to_all | solution.py:25
  89.9 9.7 %all_to_all.47 = bf16[8,64,256]{2,1,0:T(8,128)(2,1)S(1)} all-to-all(bf16[8,64,256]{2,1,0:T(8,128)(2,1)S(1)} %broadcast_in_dim.16), channel_id=1, replica_groups=mesh['zh'=4,'x'=4,'yh'=4,'yl'=2,'zl'=2,'c'=2] {'yl','zl','c'}, dimensions={0} | all-to-all | bytes 524288 | tf_op jit(solution)/shard_map/all_to_all | solution.py:25
  101.6 4.7 %all-to-all-start = ((bf16[4,832,512]{2,1,0:T(8,128)(2,1)}), bf16[4,832,512]{2,1,0:T(8,128)(2,1)}, u32[]{:S(2)}, u32[]{:S(2)}) async-start(bf16[4,832,512]{2,1,0:T(8,128)(2,1)} %broadcast_in_dim.15), calls=%async_computation | async-start | bytes 6815744 | tf_op jit(solution)/shard_map/all_to_all | solution.py:25
  106.3 40.6 %all-to-all-done = bf16[4,832,512]{2,1,0:T(8,128)(2,1)} async-done(((bf16[4,832,512]{2,1,0:T(8,128)(2,1)}), bf16[4,832,512]{2,1,0:T(8,128)(2,1)}, u32[]{:S(2)}, u32[]{:S(2)}) %all-to-all-start) | async-done | bytes 3407904 | tf_op jit(solution)/shard_map/all_to_all | solution.py:25
  147.8 6.2 %all-to-all-start.6 = ((bf16[32,4,8,192]{3,2,1,0:T(8,128)(2,1)}), bf16[32,4,8,192]{3,2,1,0:T(8,128)(2,1)S(1)}, u32[]{:S(2)}, u32[]{:S(2)}) async-start(bf16[32,4,8,192]{3,2,1,0:T(8,128)(2,1)} %broadcast_in_dim.19), calls=%async_computation.6 | async-start | bytes 1048576 | tf_op jit(solution)/shard_map/all_to_all | solution.py:25
  154.0 2.9 %convert_bitcast_fusion = f32[4,104,8,512]{3,2,1,0:T(8,128)S(1)} fusion(bf16[4,832,512]{2,1,0:T(8,128)(2,1)} %all-to-all-done), kind=kLoop, calls=%fused_computation.1 | loop fusion | flops 1703936 | bytes 10223616
  157.0 3.7 %copy.35 = f32[4,104,8,512]{3,2,0,1:T(8,128)} copy(f32[4,104,8,512]{3,2,1,0:T(8,128)S(1)} %convert_bitcast_fusion) | data formatting | bytes 13631488 | tf_op jit(solution)/shard_map/convert_element_type | solution.py:54
  160.6 9.9 %convolution_convert_fusion.1 = bf16[832,1024]{1,0:T(8,128)(2,1)} fusion(bf16[1024,2048]{1,0:T(8,128)(2,1)} %bitcast.104, f32[832,2048]{1,0:T(8,128)} %bitcast.85, bf16[832,64]{0,1:T(8,128)(2,1)S(1)} %copy-done.8, bf16[64,2048]{1,0:T(8,128)(2,1)S(1)} %bitcast.102), kind=kOutput, calls=%fused_computation.4 | convolution fusion | flops 3712024576 | bytes 13082624 | tf_op jit(solution)/shard_map/dot_general | solution.py:17
  170.6 2.8 copy.42
  173.4 4.4 %all-to-all-start.3 = ((bf16[4,256,832]{1,2,0:T(8,128)(2,1)}), bf16[4,256,832]{1,2,0:T(8,128)(2,1)}, u32[]{:S(2)}, u32[]{:S(2)}) async-start(bf16[4,256,832]{1,2,0:T(8,128)(2,1)} %bitcast.86), calls=%async_computation.3 | async-start | bytes 3407872 | tf_op jit(solution)/shard_map/all_to_all | solution.py:25
  180.3 2.4 copy.30
  183.7 2.4 copy.29
  188.2 18.6 %all-to-all-done.3 = bf16[4,256,832]{1,2,0:T(8,128)(2,1)} async-done(((bf16[4,256,832]{1,2,0:T(8,128)(2,1)}), bf16[4,256,832]{1,2,0:T(8,128)(2,1)}, u32[]{:S(2)}, u32[]{:S(2)}) %all-to-all-start.3) | async-done | bytes 1703968 | tf_op jit(solution)/shard_map/all_to_all | solution.py:25
  206.8 2.7 convert_reduce_fusion
  209.5 2.4 copy.22
  211.9 2.5 fusion.6
  217.6 17.0 %all-to-all-start.7 = ((bf16[16,8,960]{2,1,0:T(8,128)(2,1)}), bf16[16,8,960]{2,1,0:T(8,128)(2,1)S(1)}, u32[]{:S(2)}, u32[]{:S(2)}) async-start(bf16[16,8,960]{2,1,0:T(8,128)(2,1)} %pad_maximum_fusion), calls=%async_computation.7 | async-start | bytes 524288 | tf_op jit(solution)/shard_map/all_to_all | solution.py:25
  237.7 8.9 %all-to-all-done.7 = bf16[16,8,960]{2,1,0:T(8,128)(2,1)S(1)} async-done(((bf16[16,8,960]{2,1,0:T(8,128)(2,1)}), bf16[16,8,960]{2,1,0:T(8,128)(2,1)S(1)}, u32[]{:S(2)}, u32[]{:S(2)}) %all-to-all-start.7) | async-done | bytes 245792 | tf_op jit(solution)/shard_map/all_to_all | solution.py:25
  246.6 8.9 %all-to-all-start.4 = ((f32[32,8,128]{2,1,0:T(8,128)}), f32[32,8,128]{2,1,0:T(8,128)S(1)}, u32[]{:S(2)}, u32[]{:S(2)}) async-start(f32[32,8,128]{2,1,0:T(8,128)} %bitcast.17), calls=%async_computation.4 | async-start | bytes 262144 | tf_op jit(solution)/shard_map/all_to_all | solution.py:25
  255.6 8.8 %all-to-all-done.4 = f32[32,8,128]{2,1,0:T(8,128)S(1)} async-done(((f32[32,8,128]{2,1,0:T(8,128)}), f32[32,8,128]{2,1,0:T(8,128)S(1)}, u32[]{:S(2)}, u32[]{:S(2)}) %all-to-all-start.4) | async-done | bytes 131104 | tf_op jit(solution)/shard_map/all_to_all | solution.py:25
  265.1 3.5 %all-to-all-start.8 = ((bf16[16,8,960]{2,1,0:T(8,128)(2,1)}), bf16[16,8,960]{2,1,0:T(8,128)(2,1)S(1)}, u32[]{:S(2)}, u32[]{:S(2)}) async-start(bf16[16,8,960]{2,1,0:T(8,128)(2,1)} %broadcast_in_dim.22), calls=%async_computation.8 | async-start | bytes 524288 | tf_op jit(solution)/shard_map/all_to_all | solution.py:25
  270.0 11.6 %all-to-all-done.8 = bf16[16,8,960]{2,1,0:T(8,128)(2,1)S(1)} async-done(((bf16[16,8,960]{2,1,0:T(8,128)(2,1)}), bf16[16,8,960]{2,1,0:T(8,128)(2,1)S(1)}, u32[]{:S(2)}, u32[]{:S(2)}) %all-to-all-start.8) | async-done | bytes 245792 | tf_op jit(solution)/shard_map/all_to_all | solution.py:25
  (57 shorter events, 21.7 us)
Async XLA Ops:
  7.2 261.5 %copy-start = (bf16[8192,128]{1,0:T(8,128)(2,1)S(1)}, bf16[8192,128]{1,0:T(8,128)(2,1)}, u32[]{:S(2)}) copy-start(bf16[8192,128]{1,0:T(8,128)(2,1)} %param.19) | copy-start | bytes 6291460
  7.2 92.4 %copy-start.5 = (bf16[832,512]{1,0:T(8,128)(2,1)S(1)}, bf16[832,512]{1,0:T(8,128)(2,1)}, u32[]{:S(2)}) copy-start(bf16[832,512]{1,0:T(8,128)(2,1)} %param.11) | copy-start | bytes 2555908
  7.2 62.9 %all-gather.3.cloned.1.call-start = ((), (), s32[]{:S(2)}) async-start(), calls=%async_computation.9 | async-start | bytes 2359296 | tf_op jit(solution)/shard_map/all_gather | solution.py:49
  30.5 130.2 %all-gather.5.cloned.1.call-start = ((), (), s32[]{:S(2)}) async-start(), calls=%async_computation.10 | async-start | bytes 6291456 | tf_op jit(solution)/shard_map/all_gather | solution.py:50
  70.1 19.8 %collective-permute-start = (bf16[64,256]{1,0:T(8,128)(2,1)}, bf16[64,256]{1,0:T(8,128)(2,1)S(1)}, u32[]{:S(2)}, u32[]{:S(2)}) collective-permute-start(bf16[64,256]{1,0:T(8,128)(2,1)} %param.17), channel_id=1, source_target_pairs={{0,0},{1,1},{2,2},{3,3},{4,4},{5,5},{6,6},{7,7},{128,8},{129,9},{1... | collective-permute-start | bytes 98312 | tf_op jit(solution)/shard_map/ppermute | solution.py:52
  101.6 45.3 %all-to-all-start = ((bf16[4,832,512]{2,1,0:T(8,128)(2,1)}), bf16[4,832,512]{2,1,0:T(8,128)(2,1)}, u32[]{:S(2)}, u32[]{:S(2)}) async-start(bf16[4,832,512]{2,1,0:T(8,128)(2,1)} %broadcast_in_dim.15), calls=%async_computation | async-start | bytes 6815744 | tf_op jit(solution)/shard_map/all_to_all | solution.py:25
  147.8 25.6 %all-to-all-start.6 = ((bf16[32,4,8,192]{3,2,1,0:T(8,128)(2,1)}), bf16[32,4,8,192]{3,2,1,0:T(8,128)(2,1)S(1)}, u32[]{:S(2)}, u32[]{:S(2)}) async-start(bf16[32,4,8,192]{3,2,1,0:T(8,128)(2,1)} %broadcast_in_dim.19), calls=%async_computation.6 | async-start | bytes 1048576 | tf_op jit(solution)/shard_map/all_to_all | solution.py:25
  157.0 3.7 %copy-start.8 = (bf16[832,64]{0,1:T(8,128)(2,1)S(1)}, bf16[832,64]{0,1:T(8,128)(2,1)}, u32[]{:S(2)}) copy-start(bf16[832,64]{0,1:T(8,128)(2,1)} %param.16) | copy-start | bytes 319492
  170.6 7.3 %copy-start.6 = (bf16[256,832]{0,1:T(8,128)(2,1)S(1)}, bf16[256,832]{0,1:T(8,128)(2,1)}, u32[]{:S(2)}) copy-start(bf16[256,832]{0,1:T(8,128)(2,1)} %param.12) | copy-start | bytes 1277956
  173.4 33.4 %all-to-all-start.3 = ((bf16[4,256,832]{1,2,0:T(8,128)(2,1)}), bf16[4,256,832]{1,2,0:T(8,128)(2,1)}, u32[]{:S(2)}, u32[]{:S(2)}) async-start(bf16[4,256,832]{1,2,0:T(8,128)(2,1)} %bitcast.86), calls=%async_computation.3 | async-start | bytes 3407872 | tf_op jit(solution)/shard_map/all_to_all | solution.py:25
  211.9 4.4 %copy-start.1 = (f32[256,832]{0,1:T(8,128)S(1)}, f32[256,832]{0,1:T(8,128)}, u32[]{:S(2)}) copy-start(f32[256,832]{0,1:T(8,128)} %convert_reduce_fusion) | copy-start | bytes 2555908
  211.9 4.4 %copy-start.3 = (f32[256,832]{0,1:T(8,128)S(1)}, f32[256,832]{0,1:T(8,128)}, u32[]{:S(2)}) copy-start(f32[256,832]{0,1:T(8,128)} %copy.30) | copy-start | bytes 2555908
  211.9 4.4 %copy-start.4 = (f32[256,832]{0,1:T(8,128)S(1)}, f32[256,832]{0,1:T(8,128)}, u32[]{:S(2)}) copy-start(f32[256,832]{0,1:T(8,128)} %copy.29) | copy-start | bytes 2555908
  211.9 4.4 %copy-start.7 = (bf16[256,192]{1,0:T(8,128)(2,1)S(1)}, bf16[256,192]{1,0:T(8,128)(2,1)}, u32[]{:S(2)}) copy-start(bf16[256,192]{1,0:T(8,128)(2,1)} %dynamic-slice_bitcast_fusion) | copy-start | bytes 294916
  216.3 18.3 %copy-start.2 = (bf16[2,16,8,832]{3,2,1,0:T(8,128)(2,1)S(1)}, bf16[2,16,8,832]{3,2,1,0:T(8,128)(2,1)}, u32[]{:S(2)}) copy-start(bf16[2,16,8,832]{3,2,1,0:T(8,128)(2,1)} %get-tuple-element.4) | copy-start | bytes 1277956
  217.6 29.0 %all-to-all-start.7 = ((bf16[16,8,960]{2,1,0:T(8,128)(2,1)}), bf16[16,8,960]{2,1,0:T(8,128)(2,1)S(1)}, u32[]{:S(2)}, u32[]{:S(2)}) async-start(bf16[16,8,960]{2,1,0:T(8,128)(2,1)} %pad_maximum_fusion), calls=%async_computation.7 | async-start | bytes 524288 | tf_op jit(solution)/shard_map/all_to_all | solution.py:25
  246.6 17.8 %all-to-all-start.4 = ((f32[32,8,128]{2,1,0:T(8,128)}), f32[32,8,128]{2,1,0:T(8,128)S(1)}, u32[]{:S(2)}, u32[]{:S(2)}) async-start(f32[32,8,128]{2,1,0:T(8,128)} %bitcast.17), calls=%async_computation.4 | async-start | bytes 262144 | tf_op jit(solution)/shard_map/all_to_all | solution.py:25
  265.1 16.5 %all-to-all-start.8 = ((bf16[16,8,960]{2,1,0:T(8,128)(2,1)}), bf16[16,8,960]{2,1,0:T(8,128)(2,1)S(1)}, u32[]{:S(2)}, u32[]{:S(2)}) async-start(bf16[16,8,960]{2,1,0:T(8,128)(2,1)} %broadcast_in_dim.22), calls=%async_computation.8 | async-start | bytes 524288 | tf_op jit(solution)/shard_map/all_to_all | solution.py:25
Sparse Core Ops, SparseCore 0:
  30.6 39.4 all-gather.2
  72.2 21.1 all-gather.4

commit v2 on v1

v2 whole, which is shorter than its diff:
```python
import jax
import jax.numpy as jnp
import numpy as np
from jax import lax
from jax.experimental import pallas as pl
from jax.experimental.pallas import tpu as pltpu
from jax.sharding import Mesh, PartitionSpec as P

AXES = ("zh", "x", "yh", "yl", "zl", "c")
SIZES = (4, 4, 4, 2, 2, 2)
Y = ("yh", "yl")
DP = ("zh", "x")
ST = ("yh", "yl", "zl", "c")
TOKEN_ORDER = ("c", "yh", "yl", "zl")
F32, BF16 = jnp.float32, jnp.bfloat16
VMEM = pl.BlockSpec(memory_space=pltpu.VMEM)
PARAMS = pltpu.CompilerParams(vmem_limit_bytes=56 * 2**20)


def contract_last(left, right):
    return lax.dot_general(left, right, (((1,), (1,)), ((), ())), preferred_element_type=F32)


def contract_first(left, right):
    return lax.dot_general(left, right, (((0,), (0,)), ((), ())), preferred_element_type=F32)


def exchange(blocks, axes):
    return lax.all_to_all(blocks, axes, 0, 0, tiled=True)


def spread(block, axes, count):
    return exchange(jnp.broadcast_to(block[None], (count,) + block.shape), axes)


def swap_cores(array):
    return lax.ppermute(array, "c", [(0, 1), (1, 0)])


def band_pairs():
    index = np.arange(512).reshape(SIZES)
    pairs = []
    for zh in range(4):
        for x in range(4):
            for yh in range(4):
                for yl in range(2):
                    for zl in range(2):
                        for c in range(2):
                            source = index[yh, yl * 2 + zl, zh, x // 2, x % 2, c]
                            pairs.append((int(source), int(index[zh, x, yh, yl, zl, c])))
    return pairs


def partial_hidden(rows, weights, a_down):
    rows = rows[:, :2048].reshape(512, 4, 512)
    total = lax.dot_general(weights, rows, (((0, 2), (1, 2)), ((), ())), preferred_element_type=F32)
    rank = total[832:].astype(BF16)
    whole = total[:832] + jnp.dot(a_down, rank, preferred_element_type=F32)
    return whole.astype(BF16).reshape(832, 4, 128).transpose(1, 0, 2)


def adapter_terms(parts_ref, gate_ref, up_ref, saved_ref, b_gate_ref, b_up_ref):
    grad_hidden = jnp.sum(parts_ref[...].astype(F32), axis=0)
    grad_gate = (grad_hidden * gate_ref[...]).astype(BF16)
    grad_up = (grad_hidden * up_ref[...]).astype(BF16)
    rank = jnp.dot(b_gate_ref[...], grad_gate, preferred_element_type=F32)
    rank = rank + jnp.dot(b_up_ref[...], grad_up, preferred_element_type=F32)
    into_gate = contract_last(saved_ref[:64, :], grad_gate)
    into_up = contract_last(saved_ref[64:, :], grad_up)
    return rank.T, into_gate, into_up


def own_kernel(parts_ref, gate_ref, up_ref, saved_ref, b_gate_ref, b_up_ref, rank_ref, sums_ref):
    rank, into_gate, into_up = adapter_terms(parts_ref, gate_ref, up_ref, saved_ref, b_gate_ref, b_up_ref)
    rank_ref[...] = rank
    sums_ref[:64, :] = into_gate
    sums_ref[64:, :] = into_up


def other_kernel(
    core_ref, parts_ref, gate_ref, up_ref, saved_ref, b_gate_ref, b_up_ref, own_rank_ref, own_sums_ref, down_ref, rank_ref, sums_ref
):
    rank, into_gate, into_up = adapter_terms(parts_ref, gate_ref, up_ref, saved_ref, b_gate_ref, b_up_ref)
    core = core_ref[0]
    rank_ref[core] = own_rank_ref[...]
    rank_ref[1 - core] = rank
    sums_ref[:, :128] = down_ref[...]
    sums_ref[:64, 128:] = (own_sums_ref[:64, :] + into_gate).astype(BF16)
    sums_ref[64:, 128:] = (own_sums_ref[64:, :] + into_up).astype(BF16)


def own_terms(*operands):
    return pl.pallas_call(
        own_kernel,
        out_shape=(jax.ShapeDtypeStruct((128, 128), F32), jax.ShapeDtypeStruct((128, 832), F32)),
        in_specs=[VMEM] * 6,
        out_specs=(VMEM, VMEM),
        compiler_params=PARAMS,
        cost_estimate=pl.CostEstimate(flops=10**8, bytes_accessed=3 * 2**20, transcendentals=0),
    )(*operands)


def other_terms(*operands):
    return pl.pallas_call(
        other_kernel,
        out_shape=(jax.ShapeDtypeStruct((2, 128, 128), F32), jax.ShapeDtypeStruct((128, 960), BF16)),
        in_specs=[pl.BlockSpec(memory_space=pltpu.SMEM)] + [VMEM] * 9,
        out_specs=(VMEM, VMEM),
        compiler_params=PARAMS,
        cost_estimate=pl.CostEstimate(flops=10**8, bytes_accessed=3 * 2**20, transcendentals=0),
    )(*operands)


def factor_kernel(core_ref, gate_ref, up_ref, gate_out, up_out):
    core = core_ref[0]
    gate_rows = gate_ref[...].astype(F32).reshape(16, 2, 8, 832)
    up_rows = up_ref[...].astype(F32).reshape(16, 2, 8, 832)
    for which in range(2):
        slot = core if which == 0 else 1 - core
        gate_value = gate_rows[:, which].reshape(128, 832)
        sigmoid_gate = jax.nn.sigmoid(gate_value)
        up_out[slot] = (gate_value * sigmoid_gate).T
        slope = sigmoid_gate * (1.0 + gate_value * (1.0 - sigmoid_gate))
        gate_out[slot] = (up_rows[:, which].reshape(128, 832) * slope).T


def factors(core, gate_pre, up_pre):
    shape = jax.ShapeDtypeStruct((2, 832, 128), F32)
    return pl.pallas_call(
        factor_kernel,
        out_shape=(shape, shape),
        in_specs=[pl.BlockSpec(memory_space=pltpu.SMEM), VMEM, VMEM],
        out_specs=(VMEM, VMEM),
        compiler_params=PARAMS,
        cost_estimate=pl.CostEstimate(flops=10**7, bytes_accessed=3 * 2**20, transcendentals=256 * 832),
    )(core.reshape(1), gate_pre, up_pre)


def saved_kernel(place_ref, own_band_ref, other_band_ref, own_ranks_ref, other_ranks_ref, saved_ref, down_ref):
    down = contract_first(own_ranks_ref[:, 128:192], own_band_ref[...])
    down = down + contract_first(other_ranks_ref[:, 128:192], other_band_ref[...])
    down_ref[...] = jnp.where(place_ref[2] == 1, down, 0.0).astype(BF16)
    window = pl.ds(pl.multiple_of(place_ref[1] * 128, 128), 128)
    saved_ref[0] = own_ranks_ref[window, :128].T
    saved_ref[1] = other_ranks_ref[window, :128].T


def saved_terms(place, own_rows, other_rows):
    band = pl.BlockSpec((512, 256), lambda i, place: (0, place[0]))
    ranks = pl.BlockSpec((512, 256), lambda i, place: (0, 8))
    return pl.pallas_call(
        saved_kernel,
        grid_spec=pltpu.PrefetchScalarGridSpec(
            num_scalar_prefetch=1,
            grid=(1,),
            in_specs=[band, band, ranks, ranks],
            out_specs=(
                pl.BlockSpec((2, 128, 128), lambda i, place: (0, 0, 0)),
                pl.BlockSpec((64, 256), lambda i, place: (0, 0)),
            ),
        ),
        out_shape=(jax.ShapeDtypeStruct((2, 128, 128), BF16), jax.ShapeDtypeStruct((64, 256), BF16)),
        compiler_params=PARAMS,
        cost_estimate=pl.CostEstimate(flops=2 * 1024 * 64 * 256, bytes_accessed=2**20, transcendentals=0),
    )(place, own_rows, other_rows, own_rows, other_rows)


def shards(grad_out, w_down, gate_pre, up_pre, rank_in, rank_hidden, a_down, b_down, b_in, a_in):
    core = lax.axis_index("c")
    zh = lax.axis_index("zh")
    station = lax.axis_index(ST)

    ranks = jnp.concatenate([rank_in, rank_hidden, jnp.zeros((8, 64), BF16)], axis=1)
    quarters = grad_out.reshape(8, 4, 2048).transpose(1, 0, 2)
    quarters = jnp.concatenate([quarters, jnp.broadcast_to(ranks[None], (4, 8, 256))], axis=2)
    blocks = jnp.broadcast_to(quarters[:, None], (4, 2, 8, 2304)).reshape(8, 8, 2304)
    own_band = lax.ppermute(b_down, AXES, band_pairs())
    other_band = swap_cores(own_band)
    band_pair = jnp.where(
        core == 0, jnp.concatenate([own_band, other_band], axis=1), jnp.concatenate([other_band, own_band], axis=1)
    )
    w_here = jnp.concatenate([w_down, band_pair])
    from_z = exchange(blocks, ("zh", "zl"))
    gate_factor, up_factor = factors(core, gate_pre, up_pre)
    none = jnp.zeros((64, 832), BF16)
    b_gate, b_up = jnp.concatenate([b_in[0], none]), jnp.concatenate([none, b_in[1]])
    ready = (from_z, w_here, gate_factor, up_factor, b_gate, b_up, a_down)
    from_z, w_here, gate_factor, up_factor, b_gate, b_up, a_down = lax.optimization_barrier(ready)
    own_rows = lax.all_gather(from_z.reshape(4, 16, 2304), Y, axis=1, tiled=True).reshape(512, 2304)
    weights = spread(w_here, "x", 4)
    own_rows, weights = lax.optimization_barrier((own_rows, weights))
    other_rows = swap_cores(own_rows)

    own_parts = exchange(partial_hidden(own_rows, weights, a_down), "zh")
    other_partial = partial_hidden(other_rows, weights, a_down)
    other_parts = exchange(other_partial, "zh")

    place = jnp.stack([station % 8, zh, (station // 8 == zh).astype(jnp.int32)])
    place, _ = lax.optimization_barrier((place, other_partial))
    saved, partial_down = saved_terms(place, own_rows, other_rows)
    partial_down = partial_down.reshape(128, 128)
    own_rank, own_sums = own_terms(own_parts, gate_factor[0], up_factor[0], saved[0], b_gate, b_up)
    rank_partial, sums = other_terms(
        core.reshape(1), other_parts, gate_factor[1], up_factor[1], saved[1], b_gate, b_up, own_rank, own_sums, partial_down
    )
    sums = jnp.sum(exchange(sums.reshape(16, 8, 960), DP).astype(F32), axis=0).astype(BF16)
    rank_partial, sums = lax.optimization_barrier((rank_partial, sums))
    rank_grad = jnp.sum(exchange(rank_partial.reshape(32, 8, 128), TOKEN_ORDER), axis=0).astype(BF16)
    sums = spread(sums, DP, 16).astype(F32)
    grad_b_in = sums[:, :, 128:].reshape(2, 64, 832)
    grad_b_down = sums[:, :, :128].reshape(64, 256)
    input_grad = contract_last(rank_grad, a_in).astype(BF16)
    return (input_grad, grad_b_in, grad_b_down)


def solution(mesh):
    fine = Mesh(mesh.devices.reshape(SIZES), AXES)
    placed = (
        P(AXES, None),
        P(ST, DP),
        P(DP, ST),
        P(DP, ST),
        P(AXES, None),
        P(AXES, None),
        P(ST, None),
        P(None, ST),
        P(None, None, ST),
        P(),
    )
    return jax.shard_map(
        shards,
        mesh=fine,
        in_specs=placed,
        out_specs=(P(AXES, None), P(None, None, ST), P(None, ST)),
        check_vma=False,
    )
```

time: 291 us -> 212 us (0.73)
  waiting for transfers between devices: 128 us -> 30.7 us
  blocking collectives: 49.4 us -> 82.7 us
  Pallas kernels: 0 us -> 11.3 us
  matrix products: 17.2 us -> 6.3 us
  other arithmetic: 9.77 us -> 3.58 us
  local copies, waits for them, and re-layouts: 25 us -> 20.3 us
  starting transfers between devices: 46.2 us -> 41.6 us
    all_to_all x6 -> x4, waiting for transfers between devices: 88.4 us -> 30.7 us  [exchange(): return lax.all_to_all(blocks, axes, 0, 0, tiled=True)]
    all_gather x2 -> x1, waiting for transfers between devices: 39.6 us -> 0.01 us  [shards(): lax.all_gather(from_z.reshape(4, 16, 2304), Y, axis=1, tiled=True)]
    all_to_all x3, blocking collectives: 49.4 us -> 82.7 us  [exchange(): return lax.all_to_all(blocks, axes, 0, 0, tiled=True)]
    all_to_all x6 -> x4, starting transfers between devices: 44.7 us -> 32.4 us  [exchange(): return lax.all_to_all(blocks, axes, 0, 0, tiled=True)]
    dot_general x4 -> x1, matrix products: 13.6 us -> 1.31 us  [contract_last(): lax.dot_general(left, right, (((1,), (1,)), ((), ())), preferred_element_...]
    pallas_call x0 -> x4, Pallas kernels: none -> 11.3 us  [the longest x1 2.94 us: other_terms(): pl.pallas_call(other_kernel, out_shape=(jax.ShapeDtypeStruct((2, 128, 128...]
    convert_element_type x5 -> x0, local copies, waits for them, and re-layouts: 10.4 us -> none  [the longest x4 6.75 us: by_token(): saved.reshape(16, 2, 8, 832).transpose(1, 0, 2, 3).reshape(256, 832)]
    squeeze x1 -> x3, local copies, waits for them, and re-layouts: 0.67 us -> 4.99 us  [the longest x1 2.62 us: shards(): up_factor[0]]
  transfers between devices with their start and end apart: 9 -> 8, of which waited for: 6 -> 4; matrix products, arithmetic and copies ran while one was open for 13% -> 13% of each run, Pallas kernels for 0% -> 4%
where the time goes in v2:
time: 212 us; the launch traced here: 211 us
  blocking collectives  82.7 us (39%)
  starting transfers between devices  41.6 us (20%)
  waiting for transfers between devices  30.7 us (14%)
  local copies, waits for them, and re-layouts  20.3 us (10%)
  between operations  14.2 us (7%)
  Pallas kernels  11.3 us (5%)
  matrix products  6.3 us (3%)
  other arithmetic  3.58 us (2%)
    all_to_all x3, blocking collectives, exchange(): return lax.all_to_all(blocks, axes, 0, 0, tiled=True)  82.7 us
    all_to_all x4, starting transfers between devices, exchange(): return lax.all_to_all(blocks, axes, 0, 0, tiled=True)  32.4 us
    all_to_all x4, waiting for transfers between devices, exchange(): return lax.all_to_all(blocks, axes, 0, 0, tiled=True)  30.7 us
    ppermute x1, starting transfers between devices, shards(): own_band = lax.ppermute(b_down, AXES, band_pairs())  5.08 us
  transfers between devices with their start and end apart: 8, of which 4 were waited for; matrix products, arithmetic and copies ran while one was open for 13% of the time, Pallas kernels for 4%

profile of v2, /device:TPU:8, one launch (start us, length us, event | category | flops | bytes accessed | tf_op | source)
XLA Modules:
  0.0 210.8 jit_solution(18132138013865630597)
XLA Ops:
  7.2 5.1 %collective-permute-start = (bf16[64,256]{1,0:T(8,128)(2,1)}, bf16[64,256]{1,0:T(8,128)(2,1)S(1)}, u32[]{:S(2)}, u32[]{:S(2)}) collective-permute-start(bf16[64,256]{1,0:T(8,128)(2,1)} %param.17), channel_id=1, source_target_pairs={{0,0},{1,1},{32,2},{33,3},{64,4},{65,5},{96,6},{97,7},{128,8},{129... | collective-permute-start | bytes 98312 | tf_op jit(solution)/shard_map/ppermute | solution.py:177
  14.7 11.0 %all-to-all-start = ((bf16[8,8,2304]{2,1,0:T(8,128)(2,1)}), bf16[8,8,2304]{2,1,0:T(8,128)(2,1)S(1)}, u32[]{:S(2)}, u32[]{:S(2)}) async-start(bf16[8,8,2304]{2,1,0:T(8,128)(2,1)} %bitcast.3), calls=%async_computation | async-start | bytes 589824 | tf_op jit(solution)/shard_map/all_to_all | solution.py:29
  25.8 1.9 collective-permute-start.1
  32.1 2.9 %shard_map.121 = (f32[2,832,128]{2,1,0:T(8,128)}, f32[2,832,128]{2,1,0:T(8,128)}) custom-call(s32[1]{0:T(128)} %bitcast.core_ref, bf16[256,832]{1,0:T(8,128)(2,1)} %copy.17.gate_ref, bf16[256,832]{1,0:T(8,128)(2,1)} %copy.18.up_ref), custom_call_target="tpu_custom_call" | custom-call | flops 10000000 | bytes 3145728 | tf_op jit(solution)/shard_map/pallas_call | solution.py:129
  36.2 1.9 all-to-all-done
  39.1 45.7 %all_to_all.35 = bf16[4,896,512]{2,1,0:T(8,128)(2,1)} all-to-all(bf16[4,896,512]{2,1,0:T(8,128)(2,1)S(1)} %broadcast_in_dim.13), channel_id=1, replica_groups=mesh['zh'=4,'x'=4,'yh'=4,'yl'=2,'zl'=2,'c'=2] {'x'}, dimensions={0} | all-to-all | bytes 7340032 | tf_op jit(solution)/shard_map/all_to_all | solution.py:29
  84.7 2.2 %collective-permute-start.2 = (bf16[512,2304]{1,0:T(8,128)(2,1)}, bf16[512,2304]{1,0:T(8,128)(2,1)}, u32[]{:S(2)}, u32[]{:S(2)}) collective-permute-start(bf16[512,2304]{1,0:T(8,128)(2,1)} %bitcast.67), channel_id=1, source_target_pairs={{0,1},{1,0},{2,3},{3,2},{4,5},{5,4},{6,7},{7,6},{8,9},{9,8},{10,11... | collective-permute-start | bytes 7077896 | tf_op jit(solution)/shard_map/ppermute | solution.py:37
  86.9 1.7 slice.58
  88.7 2.1 fusion.11
  92.2 8.8 %all-to-all-start.3 = ((bf16[4,832,128]{2,1,0:T(8,128)(2,1)}), bf16[4,832,128]{2,1,0:T(8,128)(2,1)S(1)}, u32[]{:S(2)}, u32[]{:S(2)}) async-start(bf16[4,832,128]{2,1,0:T(8,128)(2,1)} %bitcast.72), calls=%async_computation.3 | async-start | bytes 1703936 | tf_op jit(solution)/shard_map/all_to_all | solution.py:29
  101.1 1.9 slice.66
  103.8 2.1 fusion.8
  107.4 11.8 %all-to-all-done.3.parts_ref = bf16[4,832,128]{2,1,0:T(8,128)(2,1)S(1)} async-done(((bf16[4,832,128]{2,1,0:T(8,128)(2,1)}), bf16[4,832,128]{2,1,0:T(8,128)(2,1)S(1)}, u32[]{:S(2)}, u32[]{:S(2)}) %all-to-all-start.3) | async-done | bytes 852000 | tf_op jit(solution)/shard_map/all_to_all | solution.py:29
  119.1 9.0 %all-to-all-start.2 = ((bf16[4,832,128]{2,1,0:T(8,128)(2,1)}), bf16[4,832,128]{2,1,0:T(8,128)(2,1)}, u32[]{:S(2)}, u32[]{:S(2)}) async-start(bf16[4,832,128]{2,1,0:T(8,128)(2,1)} %bitcast.71), calls=%async_computation.2 | async-start | bytes 1703936 | tf_op jit(solution)/shard_map/all_to_all | solution.py:29
  128.8 2.6 %slice_bitcast_fusion = (f32[832,128]{1,0:T(8,128)}, f32[832,128]{1,0:T(8,128)}, f32[832,128]{1,0:T(8,128)}, f32[832,128]{1,0:T(8,128)}) fusion(f32[2,832,128]{2,1,0:T(8,128)} %get-tuple-element.31, f32[2,832,128]{2,1,0:T(8,128)} %get-tuple-element.30), kind=kLoop, calls=%fused_computation.18 | loop fusion | bytes 3407872 | tf_op jit(solution)/shard_map/squeeze | solution.py:202
  131.4 2.7 %shard_map.122 = (bf16[2,128,128]{2,1,0:T(8,128)(2,1)}, bf16[64,256]{1,0:T(8,128)(2,1)}) custom-call(s32[3]{0:T(128)} %pad_add_fusion.place_ref, bf16[512,2304]{1,0:T(8,128)(2,1)} %bitcast.69, bf16[512,2304]{1,0:T(8,128)(2,1)} %collective-permute-done.2.other_band_ref.other_ranks_ref, bf16[512,2304]{1,0:T(8,128)(2,1)} %bitcast.70, ...), custom_call_target="tpu_custom_call" | custom-call | flops 33554432 | bytes 1048576 | tf_op jit(solution)/shard_map/pallas_call | solution.py:151
  135.5 1.4 slice_bitcast_fusion.6
  136.9 2.8 %shard_map.123 = (f32[128,128]{1,0:T(8,128)}, f32[128,832]{1,0:T(8,128)}) custom-call(bf16[4,832,128]{2,1,0:T(8,128)(2,1)} %copy-done.3, f32[832,128]{1,0:T(8,128)} %get-tuple-element.52.gate_ref, f32[832,128]{1,0:T(8,128)} %get-tuple-element.43.up_ref, bf16[128,128]{1,0:T(8,128)(2,1)} %get-tuple-element.49.saved_ref, ...), custom_call_target="tpu_custom_call" | custom-call | flops 100000000 | bytes 3145728 | tf_op jit(solution)/shard_map/pallas_call | solution.py:93
  139.7 5.5 %all-to-all-done.2.parts_ref = bf16[4,832,128]{2,1,0:T(8,128)(2,1)} async-done(((bf16[4,832,128]{2,1,0:T(8,128)(2,1)}), bf16[4,832,128]{2,1,0:T(8,128)(2,1)}, u32[]{:S(2)}, u32[]{:S(2)}) %all-to-all-start.2) | async-done | bytes 852000 | tf_op jit(solution)/shard_map/all_to_all | solution.py:29
  145.2 2.9 %shard_map.124 = (f32[2,128,128]{2,1,0:T(8,128)}, bf16[128,960]{1,0:T(8,128)(2,1)}) custom-call(s32[1]{0:T(128)} %bitcast.core_ref, bf16[4,832,128]{2,1,0:T(8,128)(2,1)} %all-to-all-done.2.parts_ref, f32[832,128]{1,0:T(8,128)} %get-tuple-element.51.gate_ref, f32[832,128]{1,0:T(8,128)} %get-tuple-element.44.up_ref, ...), custom_call_target="tpu_custom_call" | custom-call | flops 100000000 | bytes 3145728 | tf_op jit(solution)/shard_map/pallas_call | solution.py:104
  148.2 21.1 %all_to_all.36 = bf16[16,8,960]{2,1,0:T(8,128)(2,1)S(1)} all-to-all(bf16[16,8,960]{2,1,0:T(8,128)(2,1)} %bitcast.77), channel_id=1, replica_groups=mesh['zh'=4,'x'=4,'yh'=4,'yl'=2,'zl'=2,'c'=2] {'zh','x'}, dimensions={0} | all-to-all | bytes 491520 | tf_op jit(solution)/shard_map/all_to_all | solution.py:29
  169.3 15.9 %all_to_all.37 = f32[32,8,128]{2,1,0:T(8,128)S(1)} all-to-all(f32[32,8,128]{2,1,0:T(8,128)} %bitcast.79), channel_id=1, replica_groups=mesh['zh'=4,'x'=4,'yh'=4,'yl'=2,'zl'=2,'c'=2] {'c','yh','yl','zl'}, dimensions={0} | all-to-all | bytes 262144 | tf_op jit(solution)/shard_map/all_to_all | solution.py:29
  186.0 3.5 %all-to-all-start.6 = ((bf16[16,8,960]{2,1,0:T(8,128)(2,1)}), bf16[16,8,960]{2,1,0:T(8,128)(2,1)S(1)}, u32[]{:S(2)}, u32[]{:S(2)}) async-start(bf16[16,8,960]{2,1,0:T(8,128)(2,1)} %broadcast_in_dim.14), calls=%async_computation.6 | async-start | bytes 524288 | tf_op jit(solution)/shard_map/all_to_all | solution.py:29
  190.9 11.6 %all-to-all-done.6 = bf16[16,8,960]{2,1,0:T(8,128)(2,1)S(1)} async-done(((bf16[16,8,960]{2,1,0:T(8,128)(2,1)}), bf16[16,8,960]{2,1,0:T(8,128)(2,1)S(1)}, u32[]{:S(2)}, u32[]{:S(2)}) %all-to-all-start.6) | async-done | bytes 245792 | tf_op jit(solution)/shard_map/all_to_all | solution.py:29
  (49 shorter events, 18.5 us)
Async XLA Ops:
  7.2 182.4 %copy-start = (bf16[8192,128]{1,0:T(8,128)(2,1)S(1)}, bf16[8192,128]{1,0:T(8,128)(2,1)}, u32[]{:S(2)}) copy-start(bf16[8192,128]{1,0:T(8,128)(2,1)} %param.19) | copy-start | bytes 6291460
  7.2 21.5 %copy-start.6 = (bf16[256,832]{0,1:T(8,128)(2,1)S(1)}, bf16[256,832]{0,1:T(8,128)(2,1)}, u32[]{:S(2)}) copy-start(bf16[256,832]{0,1:T(8,128)(2,1)} %param.12) | copy-start | bytes 1277956
  7.2 22.5 %copy-start.7 = (bf16[256,832]{0,1:T(8,128)(2,1)S(1)}, bf16[256,832]{0,1:T(8,128)(2,1)}, u32[]{:S(2)}) copy-start(bf16[256,832]{0,1:T(8,128)(2,1)} %param.13) | copy-start | bytes 1277956
  7.2 18.6 %collective-permute-start = (bf16[64,256]{1,0:T(8,128)(2,1)}, bf16[64,256]{1,0:T(8,128)(2,1)S(1)}, u32[]{:S(2)}, u32[]{:S(2)}) collective-permute-start(bf16[64,256]{1,0:T(8,128)(2,1)} %param.17), channel_id=1, source_target_pairs={{0,0},{1,1},{32,2},{33,3},{64,4},{65,5},{96,6},{97,7},{128,8},{129... | collective-permute-start | bytes 98312 | tf_op jit(solution)/shard_map/ppermute | solution.py:177
  14.7 23.3 %all-to-all-start = ((bf16[8,8,2304]{2,1,0:T(8,128)(2,1)}), bf16[8,8,2304]{2,1,0:T(8,128)(2,1)S(1)}, u32[]{:S(2)}, u32[]{:S(2)}) async-start(bf16[8,8,2304]{2,1,0:T(8,128)(2,1)} %bitcast.3), calls=%async_computation | async-start | bytes 589824 | tf_op jit(solution)/shard_map/all_to_all | solution.py:29
  25.7 59.0 %all-gather.2.cloned.1.call-start = ((), (), s32[]{:S(2)}) async-start(), calls=%async_computation.7 | async-start | bytes 2654208 | tf_op jit(solution)/shard_map/all_gather | solution.py:189
  25.8 9.1 %collective-permute-start.1 = (bf16[64,256]{1,0:T(8,128)(2,1)S(1)}, bf16[64,256]{1,0:T(8,128)(2,1)S(1)}, u32[]{:S(2)}, u32[]{:S(2)}) collective-permute-start(bf16[64,256]{1,0:T(8,128)(2,1)S(1)} %collective-permute-done), channel_id=1, source_target_pairs={{0,1},{1,0},{2,3},{3,2},{4,5},{5,4},{6,7},{7,6},{8,9},{9,8},{10,11... | collective-permute-start | bytes 98312 | tf_op jit(solution)/shard_map/ppermute | solution.py:37
  38.0 0.7 copy-start.4
  84.7 3.9 %copy-start.1 = (bf16[4,896,512]{2,1,0:T(8,128)(2,1)S(1)}, bf16[4,896,512]{2,1,0:T(8,128)(2,1)}, u32[]{:S(2)}) copy-start(bf16[4,896,512]{2,1,0:T(8,128)(2,1)} %all_to_all.35) | copy-start | bytes 11010052
  84.7 16.4 %collective-permute-start.2 = (bf16[512,2304]{1,0:T(8,128)(2,1)}, bf16[512,2304]{1,0:T(8,128)(2,1)}, u32[]{:S(2)}, u32[]{:S(2)}) collective-permute-start(bf16[512,2304]{1,0:T(8,128)(2,1)} %bitcast.67), channel_id=1, source_target_pairs={{0,1},{1,0},{2,3},{3,2},{4,5},{5,4},{6,7},{7,6},{8,9},{9,8},{10,11... | collective-permute-start | bytes 7077896 | tf_op jit(solution)/shard_map/ppermute | solution.py:37
  88.7 2.1 copy-start.5
  92.2 26.9 %all-to-all-start.3 = ((bf16[4,832,128]{2,1,0:T(8,128)(2,1)}), bf16[4,832,128]{2,1,0:T(8,128)(2,1)S(1)}, u32[]{:S(2)}, u32[]{:S(2)}) async-start(bf16[4,832,128]{2,1,0:T(8,128)(2,1)} %bitcast.72), calls=%async_computation.3 | async-start | bytes 1703936 | tf_op jit(solution)/shard_map/all_to_all | solution.py:29
  101.1 2.7 %copy-start.2 = (bf16[4,896,512]{2,1,0:T(8,128)(2,1)S(1)}, bf16[4,896,512]{2,1,0:T(8,128)(2,1)}, u32[]{:S(2)}) copy-start(bf16[4,896,512]{2,1,0:T(8,128)(2,1)} %all_to_all.35) | copy-start | bytes 11010052
  119.1 12.3 %copy-start.3 = (bf16[4,832,128]{2,1,0:T(8,128)(2,1)}, bf16[4,832,128]{2,1,0:T(8,128)(2,1)S(1)}, u32[]{:S(2)}) copy-start(bf16[4,832,128]{2,1,0:T(8,128)(2,1)S(1)} %all-to-all-done.3.parts_ref) | copy-start | bytes 2555908
  119.1 26.1 %all-to-all-start.2 = ((bf16[4,832,128]{2,1,0:T(8,128)(2,1)}), bf16[4,832,128]{2,1,0:T(8,128)(2,1)}, u32[]{:S(2)}, u32[]{:S(2)}) async-start(bf16[4,832,128]{2,1,0:T(8,128)(2,1)} %bitcast.71), calls=%async_computation.2 | async-start | bytes 1703936 | tf_op jit(solution)/shard_map/all_to_all | solution.py:29
  186.0 16.5 %all-to-all-start.6 = ((bf16[16,8,960]{2,1,0:T(8,128)(2,1)}), bf16[16,8,960]{2,1,0:T(8,128)(2,1)S(1)}, u32[]{:S(2)}, u32[]{:S(2)}) async-start(bf16[16,8,960]{2,1,0:T(8,128)(2,1)} %broadcast_in_dim.14), calls=%async_computation.6 | async-start | bytes 524288 | tf_op jit(solution)/shard_map/all_to_all | solution.py:29
Sparse Core Ops, SparseCore 0:
  38.9 43.5 all-gather.1

commit v3 on v2

--- a/solution.py
+++ b/solution.py
@@ -11,7 +11,6 @@
 Y = ("yh", "yl")
 DP = ("zh", "x")
 ST = ("yh", "yl", "zl", "c")
-TOKEN_ORDER = ("c", "yh", "yl", "zl")
 F32, BF16 = jnp.float32, jnp.bfloat16
 VMEM = pl.BlockSpec(memory_space=pltpu.VMEM)
 PARAMS = pltpu.CompilerParams(vmem_limit_bytes=56 * 2**20)
@@ -35,6 +34,13 @@
 
 def swap_cores(array):
     return lax.ppermute(array, "c", [(0, 1), (1, 0)])
+
+
+def halve(array, dim, axis, size, bit):
+    mine = lax.axis_index(axis) // bit % 2
+    kept = lax.dynamic_index_in_dim(array, mine, dim, False)
+    sent = lax.dynamic_index_in_dim(array, 1 - mine, dim, False)
+    return kept + lax.ppermute(sent, axis, [(i, i ^ bit) for i in range(size)])
 
 
 def band_pairs():
@@ -46,7 +52,7 @@
                 for yl in range(2):
                     for zl in range(2):
                         for c in range(2):
-                            source = index[yh, yl * 2 + zl, zh, x // 2, x % 2, c]
+                            source = index[x, zl * 2 + c, zh, yh // 2, yh % 2, yl]
                             pairs.append((int(source), int(index[zh, x, yh, yl, zl, c])))
     return pairs
 
@@ -59,55 +65,34 @@
     return whole.astype(BF16).reshape(832, 4, 128).transpose(1, 0, 2)
 
 
-def adapter_terms(parts_ref, gate_ref, up_ref, saved_ref, b_gate_ref, b_up_ref):
-    grad_hidden = jnp.sum(parts_ref[...].astype(F32), axis=0)
-    grad_gate = (grad_hidden * gate_ref[...]).astype(BF16)
-    grad_up = (grad_hidden * up_ref[...]).astype(BF16)
-    rank = jnp.dot(b_gate_ref[...], grad_gate, preferred_element_type=F32)
-    rank = rank + jnp.dot(b_up_ref[...], grad_up, preferred_element_type=F32)
-    into_gate = contract_last(saved_ref[:64, :], grad_gate)
-    into_up = contract_last(saved_ref[64:, :], grad_up)
-    return rank.T, into_gate, into_up
-
-
-def own_kernel(parts_ref, gate_ref, up_ref, saved_ref, b_gate_ref, b_up_ref, rank_ref, sums_ref):
-    rank, into_gate, into_up = adapter_terms(parts_ref, gate_ref, up_ref, saved_ref, b_gate_ref, b_up_ref)
-    rank_ref[...] = rank
-    sums_ref[:64, :] = into_gate
-    sums_ref[64:, :] = into_up
-
-
-def other_kernel(
-    core_ref, parts_ref, gate_ref, up_ref, saved_ref, b_gate_ref, b_up_ref, own_rank_ref, own_sums_ref, down_ref, rank_ref, sums_ref
+def adapter_kernel(
+    parts_ref, gate_ref, up_ref, saved_ref, b_gate_ref, b_up_ref, down_ref, own_rank_ref, other_rank_ref, sums_ref
 ):
-    rank, into_gate, into_up = adapter_terms(parts_ref, gate_ref, up_ref, saved_ref, b_gate_ref, b_up_ref)
-    core = core_ref[0]
-    rank_ref[core] = own_rank_ref[...]
-    rank_ref[1 - core] = rank
+    into_gate = jnp.zeros((64, 832), F32)
+    into_up = jnp.zeros((64, 832), F32)
+    for slot, rank_ref in enumerate((own_rank_ref, other_rank_ref)):
+        grad_hidden = jnp.sum(parts_ref[:, slot].astype(F32), axis=0)
+        grad_gate = (grad_hidden * gate_ref[slot]).astype(BF16)
+        grad_up = (grad_hidden * up_ref[slot]).astype(BF16)
+        rank = jnp.dot(b_gate_ref[...], grad_gate, preferred_element_type=F32)
+        rank = rank + jnp.dot(b_up_ref[...], grad_up, preferred_element_type=F32)
+        rank_ref[...] = rank.T
+        into_gate = into_gate + contract_last(saved_ref[slot, :64, :], grad_gate)
+        into_up = into_up + contract_last(saved_ref[slot, 64:, :], grad_up)
     sums_ref[:, :128] = down_ref[...]
-    sums_ref[:64, 128:] = (own_sums_ref[:64, :] + into_gate).astype(BF16)
-    sums_ref[64:, 128:] = (own_sums_ref[64:, :] + into_up).astype(BF16)
-
-
-def own_terms(*operands):
+    sums_ref[:64, 128:] = into_gate.astype(BF16)
+    sums_ref[64:, 128:] = into_up.astype(BF16)
+
+
+def adapter_terms(*operands):
+    rank = jax.ShapeDtypeStruct((128, 128), F32)
     return pl.pallas_call(
-        own_kernel,
-        out_shape=(jax.ShapeDtypeStruct((128, 128), F32), jax.ShapeDtypeStruct((128, 832), F32)),
-        in_specs=[VMEM] * 6,
-        out_specs=(VMEM, VMEM),
+        adapter_kernel,
+        out_shape=(rank, rank, jax.ShapeDtypeStruct((128, 960), BF16)),
+        in_specs=[VMEM] * 7,
+        out_specs=(VMEM, VMEM, VMEM),
         compiler_params=PARAMS,
-        cost_estimate=pl.CostEstimate(flops=10**8, bytes_accessed=3 * 2**20, transcendentals=0),
-    )(*operands)
-
-
-def other_terms(*operands):
-    return pl.pallas_call(
-        other_kernel,
-        out_shape=(jax.ShapeDtypeStruct((2, 128, 128), F32), jax.ShapeDtypeStruct((128, 960), BF16)),
-        in_specs=[pl.BlockSpec(memory_space=pltpu.SMEM)] + [VMEM] * 9,
-        out_specs=(VMEM, VMEM),
-        compiler_params=PARAMS,
-        cost_estimate=pl.CostEstimate(flops=10**8, bytes_accessed=3 * 2**20, transcendentals=0),
+        cost_estimate=pl.CostEstimate(flops=2 * 10**8, bytes_accessed=5 * 2**20, transcendentals=0),
     )(*operands)
 
 
@@ -174,38 +159,38 @@
     quarters = grad_out.reshape(8, 4, 2048).transpose(1, 0, 2)
     quarters = jnp.concatenate([quarters, jnp.broadcast_to(ranks[None], (4, 8, 256))], axis=2)
     blocks = jnp.broadcast_to(quarters[:, None], (4, 2, 8, 2304)).reshape(8, 8, 2304)
-    own_band = lax.ppermute(b_down, AXES, band_pairs())
-    other_band = swap_cores(own_band)
-    band_pair = jnp.where(
-        core == 0, jnp.concatenate([own_band, other_band], axis=1), jnp.concatenate([other_band, own_band], axis=1)
-    )
-    w_here = jnp.concatenate([w_down, band_pair])
     from_z = exchange(blocks, ("zh", "zl"))
     gate_factor, up_factor = factors(core, gate_pre, up_pre)
     none = jnp.zeros((64, 832), BF16)
     b_gate, b_up = jnp.concatenate([b_in[0], none]), jnp.concatenate([none, b_in[1]])
-    ready = (from_z, w_here, gate_factor, up_factor, b_gate, b_up, a_down)
-    from_z, w_here, gate_factor, up_factor, b_gate, b_up, a_down = lax.optimization_barrier(ready)
-    own_rows = lax.all_gather(from_z.reshape(4, 16, 2304), Y, axis=1, tiled=True).reshape(512, 2304)
-    weights = spread(w_here, "x", 4)
-    own_rows, weights = lax.optimization_barrier((own_rows, weights))
+    b_down, b_gate, b_up = lax.optimization_barrier((b_down, b_gate, b_up))
+    own_band = lax.ppermute(b_down, AXES, band_pairs()).reshape(4, 16, 256)
+    w_copies = jnp.broadcast_to(w_down[None], (4, 832, 512))
+    from_z, w_copies = lax.optimization_barrier((from_z, w_copies))
+    own = lax.all_gather(jnp.concatenate([from_z.reshape(4, 16, 2304), own_band], axis=2), Y, axis=1, tiled=True)
+    weights = exchange(w_copies.reshape(3328, 512), "x").reshape(4, 832, 512)
+    bands = own[:, :, 2304:].reshape(4, 8, 16, 256).transpose(1, 0, 2, 3).reshape(4, 2, 64, 256)
+    bands = bands.transpose(0, 2, 1, 3).reshape(4, 64, 512)
+    own, gate_factor, up_factor, a_down = lax.optimization_barrier((own, gate_factor, up_factor, a_down))
+    own_rows = own.reshape(512, 2560)
     other_rows = swap_cores(own_rows)
-
-    own_parts = exchange(partial_hidden(own_rows, weights, a_down), "zh")
+    weights = jnp.concatenate([weights, bands], axis=1)
+    own_partial = partial_hidden(own_rows, weights, a_down)
     other_partial = partial_hidden(other_rows, weights, a_down)
-    other_parts = exchange(other_partial, "zh")
+    parts = exchange(jnp.stack([own_partial, other_partial], axis=1), "zh")
 
     place = jnp.stack([station % 8, zh, (station // 8 == zh).astype(jnp.int32)])
     place, _ = lax.optimization_barrier((place, other_partial))
     saved, partial_down = saved_terms(place, own_rows, other_rows)
     partial_down = partial_down.reshape(128, 128)
-    own_rank, own_sums = own_terms(own_parts, gate_factor[0], up_factor[0], saved[0], b_gate, b_up)
-    rank_partial, sums = other_terms(
-        core.reshape(1), other_parts, gate_factor[1], up_factor[1], saved[1], b_gate, b_up, own_rank, own_sums, partial_down
-    )
+    own_rank, other_rank, sums = adapter_terms(parts, gate_factor, up_factor, saved, b_gate, b_up, partial_down)
     sums = jnp.sum(exchange(sums.reshape(16, 8, 960), DP).astype(F32), axis=0).astype(BF16)
-    rank_partial, sums = lax.optimization_barrier((rank_partial, sums))
-    rank_grad = jnp.sum(exchange(rank_partial.reshape(32, 8, 128), TOKEN_ORDER), axis=0).astype(BF16)
+    rank_grad = (own_rank + swap_cores(other_rank)).reshape(8, 2, 8, 128)
+    rank_grad = halve(rank_grad, 1, "zl", 2, 1)
+    rank_grad = halve(rank_grad.reshape(4, 2, 8, 128), 1, "yl", 2, 1)
+    rank_grad = halve(rank_grad.reshape(2, 2, 8, 128), 1, "yh", 4, 1)
+    rank_grad = halve(rank_grad.reshape(2, 8, 128), 0, "yh", 4, 2)
+    rank_grad = rank_grad.astype(BF16)
     sums = spread(sums, DP, 16).astype(F32)
     grad_b_in = sums[:, :, 128:].reshape(2, 64, 832)
     grad_b_down = sums[:, :, :128].reshape(64, 256)

time: 212 us -> 201 us (0.948)
  blocking collectives: 82.7 us -> 0 us
  waiting for transfers between devices: 30.7 us -> 90.6 us
  starting transfers between devices: 41.6 us -> 58.1 us
  local copies, waits for them, and re-layouts: 20.3 us -> 16 us
  Pallas kernels: 11.3 us -> 9.07 us
    all_to_all x3 -> x0, blocking collectives: 82.7 us -> none  [exchange(): return lax.all_to_all(blocks, axes, 0, 0, tiled=True)]
    all_gather x1, waiting for transfers between devices: 0.01 us -> 35.3 us  [shards(): lax.all_gather(jnp.concatenate([from_z.reshape(4, 16, 2304), own_band], a...]
    all_to_all x4 -> x5, waiting for transfers between devices: 30.7 us -> 45.9 us  [exchange(): return lax.all_to_all(blocks, axes, 0, 0, tiled=True)]
    ppermute x1 -> x5, starting transfers between devices: 5.08 us -> 19.5 us  [the longest x4 12.8 us: halve(): return kept + lax.ppermute(sent, axis, [(i, i ^ bit) for i in range(size)])]
    ppermute x1 -> x5, waiting for transfers between devices: 0.01 us -> 7.92 us  [the longest x4 7.92 us: halve(): return kept + lax.ppermute(sent, axis, [(i, i ^ bit) for i in range(size)])]
    squeeze x2 -> x4, local copies, waits for them, and re-layouts: 4.01 us -> 0.03 us  [halve(): sent = lax.dynamic_index_in_dim(array, 1 - mine, dim, False)]
    all_to_all x4 -> x5, starting transfers between devices: 32.4 us -> 34.7 us  [exchange(): return lax.all_to_all(blocks, axes, 0, 0, tiled=True)]
    pallas_call x2 -> x1, Pallas kernels: 5.73 us -> 3.52 us  [adapter_terms(): pl.pallas_call(adapter_kernel, out_shape=(rank, rank, jax.ShapeDtypeStruc...]
  transfers between devices with their start and end apart: 8 -> 13, of which waited for: 4 -> 8; matrix products, arithmetic and copies ran while one was open for 13% -> 8% of each run, Pallas kernels for 4% -> 3%
where the time goes in v3:
time: 201 us; the launch traced here: 200 us
  waiting for transfers between devices  90.6 us (45%)
  starting transfers between devices  58.1 us (29%)
  local copies, waits for them, and re-layouts  16 us (8%)
  between operations  14.5 us (7%)
  Pallas kernels  9.07 us (5%)
  matrix products  6.3 us (3%)
  other arithmetic  5.47 us (3%)
    all_to_all x5, waiting for transfers between devices, exchange(): return lax.all_to_all(blocks, axes, 0, 0, tiled=True)  45.9 us
    all_gather x1, waiting for transfers between devices, shards(): lax.all_gather(jnp.concatenate([from_z.reshape(4, 16, 2304), own_band], a...  35.3 us
    all_to_all x5, starting transfers between devices, exchange(): return lax.all_to_all(blocks, axes, 0, 0, tiled=True)  34.7 us
    ppermute x4, starting transfers between devices, halve(): return kept + lax.ppermute(sent, axis, [(i, i ^ bit) for i in range(size)])  12.8 us
    ppermute x4, waiting for transfers between devices, halve(): return kept + lax.ppermute(sent, axis, [(i, i ^ bit) for i in range(size)])  7.92 us
    ppermute x1, starting transfers between devices, shards(): own_band = lax.ppermute(b_down, AXES, band_pairs()).reshape(4, 16, 256)  6.71 us
    unnamed x17, local copies, waits for them, and re-layouts  4.74 us
    dot_general x2, matrix products, partial_hidden(): lax.dot_general(weights, rows, (((0, 2), (1, 2)), ((), ())), preferred_el...  4.18 us
  transfers between devices with their start and end apart: 13, of which 8 were waited for; matrix products, arithmetic and copies ran while one was open for 8% of the time, Pallas kernels for 3%

profile of v3, /device:TPU:8, one launch (start us, length us, event | category | flops | bytes accessed | tf_op | source)
XLA Modules:
  0.0 200.1 jit_solution(4405198734227220732)
XLA Ops:
  9.8 10.3 %all-to-all-start = ((bf16[8,8,2304]{2,1,0:T(8,128)(2,1)}), bf16[8,8,2304]{2,1,0:T(8,128)(2,1)S(1)}, u32[]{:S(2)}, u32[]{:S(2)}) async-start(bf16[8,8,2304]{2,1,0:T(8,128)(2,1)} %bitcast.2), calls=%async_computation | async-start | bytes 589824 | tf_op jit(solution)/shard_map/all_to_all | solution.py:28
  22.6 6.7 %collective-permute-start = (bf16[64,256]{1,0:T(8,128)(2,1)S(1)}, bf16[64,256]{1,0:T(8,128)(2,1)S(1)}, u32[]{:S(2)}, u32[]{:S(2)}) collective-permute-start(bf16[64,256]{1,0:T(8,128)(2,1)S(1)} %copy-done.6), channel_id=1, source_target_pairs={{0,0},{32,1},{64,2},{96,3},{1,4},{33,5},{65,6},{97,7},{2,8},{34,9}... | collective-permute-start | bytes 98312 | tf_op jit(solution)/shard_map/ppermute | solution.py:167
  29.3 3.5 %all-to-all-done = bf16[8,8,2304]{2,1,0:T(8,128)(2,1)S(1)} async-done(((bf16[8,8,2304]{2,1,0:T(8,128)(2,1)}), bf16[8,8,2304]{2,1,0:T(8,128)(2,1)S(1)}, u32[]{:S(2)}, u32[]{:S(2)}) %all-to-all-start) | async-done | bytes 294944 | tf_op jit(solution)/shard_map/all_to_all | solution.py:28
  32.8 2.0 %broadcast_in_dim.13 = bf16[4,832,512]{2,1,0:T(8,128)(2,1)} broadcast(bf16[832,512]{1,0:T(8,128)(2,1)S(1)} %copy-done.2), dimensions={1,2} | broadcast | bytes 4259840 | tf_op jit(solution)/shard_map/broadcast_in_dim | solution.py:168
  35.6 4.8 %all-to-all-start.1 = ((bf16[4,832,512]{2,1,0:T(8,128)(2,1)}), bf16[4,832,512]{2,1,0:T(8,128)(2,1)}, u32[]{:S(2)}, u32[]{:S(2)}) async-start(bf16[4,832,512]{2,1,0:T(8,128)(2,1)} %broadcast_in_dim.13), calls=%async_computation.1 | async-start | bytes 6815744 | tf_op jit(solution)/shard_map/all_to_all | solution.py:28
  42.4 2.8 %shard_map.121 = (f32[2,832,128]{2,1,0:T(8,128)}, f32[2,832,128]{2,1,0:T(8,128)}) custom-call(s32[1]{0:T(128)} %bitcast.11.core_ref, bf16[256,832]{1,0:T(8,128)(2,1)} %copy.26.gate_ref, bf16[256,832]{1,0:T(8,128)(2,1)} %copy.27.up_ref), custom_call_target="tpu_custom_call" | custom-call | flops 10000000 | bytes 3145728 | tf_op jit(solution)/shard_map/pallas_call | solution.py:114
  45.2 35.3 %all-gather.2.cloned.1.call-done = bf16[4,128,2560]{2,1,0:T(8,128)(2,1)} async-done(((bf16[4,16,2560]{2,1,0:T(8,128)(2,1)}), bf16[4,128,2560]{2,1,0:T(8,128)(2,1)}) %all-gather.2.cloned.1.call-update) | async-done | bytes 2621456 | tf_op jit(solution)/shard_map/all_gather | solution.py:170
  80.5 1.9 collective-permute-start.1
  82.4 2.3 %constant_dynamic-update-slice_fusion.1 = bf16[4,896,512]{2,1,0:T(8,128)(2,1)S(1)} fusion(bf16[4,832,512]{2,1,0:T(8,128)(2,1)} %all-to-all-done.1), kind=kLoop, calls=%fused_computation.31 | loop fusion | bytes 6815744
  85.6 2.1 %fusion.8 = f32[896,512]{1,0:T(8,128)S(1)} fusion(bf16[4,896,512]{2,1,0:T(8,128)(2,1)S(1)} %constant_dynamic-update-slice_fusion, bf16[64,4,8,512]{3,2,1,0:T(8,128)(2,1)S(1)} %bitcast.88), kind=kOutput, calls=%fused_computation.12 | convolution fusion | flops 1879048192 | bytes 7602176 | tf_op jit(solution)/shard_map/dot_general | solution.py:62
  90.0 2.1 %fusion.11 = f32[896,512]{1,0:T(8,128)S(1)} fusion(bf16[4,896,512]{2,1,0:T(8,128)(2,1)S(1)} %constant_dynamic-update-slice_fusion, bf16[64,4,8,512]{3,2,1,0:T(8,128)(2,1)S(1)} %bitcast.89), kind=kOutput, calls=%fused_computation.13 | convolution fusion | flops 1879048192 | bytes 7602176 | tf_op jit(solution)/shard_map/dot_general | solution.py:62
  94.2 7.4 %all-to-all-start.2 = ((bf16[4,2,832,128]{3,2,1,0:T(8,128)(2,1)}), bf16[4,2,832,128]{3,2,1,0:T(8,128)(2,1)}, u32[]{:S(2)}, u32[]{:S(2)}) async-start(bf16[4,2,832,128]{3,2,1,0:T(8,128)(2,1)} %pad_maximum_fusion), calls=%async_computation.2 | async-start | bytes 3407872 | tf_op jit(solution)/shard_map/all_to_all | solution.py:28
  102.2 2.7 %shard_map.122 = (bf16[2,128,128]{2,1,0:T(8,128)(2,1)}, bf16[64,256]{1,0:T(8,128)(2,1)}) custom-call(s32[3]{0:T(128)} %pad_add_fusion.place_ref, bf16[512,2560]{1,0:T(8,128)(2,1)} %bitcast.85, bf16[512,2560]{1,0:T(8,128)(2,1)} %collective-permute-done.1.other_band_ref.other_ranks_ref, bf16[512,2560]{1,0:T(8,128)(2,1)} %bitcast.86, ...), custom_call_target="tpu_custom_call" | custom-call | flops 33554432 | bytes 1048576 | tf_op jit(solution)/shard_map/pallas_call | solution.py:136
  106.3 38.3 %all-to-all-done.2.parts_ref = bf16[4,2,832,128]{3,2,1,0:T(8,128)(2,1)} async-done(((bf16[4,2,832,128]{3,2,1,0:T(8,128)(2,1)}), bf16[4,2,832,128]{3,2,1,0:T(8,128)(2,1)}, u32[]{:S(2)}, u32[]{:S(2)}) %all-to-all-start.2) | async-done | bytes 1703968 | tf_op jit(solution)/shard_map/all_to_all | solution.py:28
  144.6 3.5 %shard_map.123 = (f32[128,128]{1,0:T(8,128)}, f32[128,128]{1,0:T(8,128)}, bf16[128,960]{1,0:T(8,128)(2,1)}) custom-call(bf16[4,2,832,128]{3,2,1,0:T(8,128)(2,1)} %all-to-all-done.2.parts_ref, f32[2,832,128]{2,1,0:T(8,128)} %get-tuple-element.27.gate_ref, f32[2,832,128]{2,1,0:T(8,128)} %get-tuple-element.28.up_ref, ...), custom_call_target="tpu_custom_call" | custom-call | flops 200000000 | bytes 5242880 | tf_op jit(solution)/shard_map/pallas_call | solution.py:89
  152.3 1.9 collective-permute-start.3
  154.2 5.6 %all-to-all-start.3 = ((bf16[16,8,960]{2,1,0:T(8,128)(2,1)}), bf16[16,8,960]{2,1,0:T(8,128)(2,1)S(1)}, u32[]{:S(2)}, u32[]{:S(2)}) async-start(bf16[16,8,960]{2,1,0:T(8,128)(2,1)} %bitcast.97), calls=%async_computation.3 | async-start | bytes 524288 | tf_op jit(solution)/shard_map/all_to_all | solution.py:28
  159.9 2.4 %collective-permute-start.4 = (f32[4,8,128]{2,1,0:T(8,128)S(1)}, f32[4,8,128]{2,1,0:T(8,128)S(1)}, u32[]{:S(2)}, u32[]{:S(2)}) collective-permute-start(f32[4,8,128]{2,1,0:T(8,128)S(1)} %dynamic-slice_bitcast_fusion.1), channel_id=1, source_target_pairs={{0,4},{4,0},{1,5},{5,1},{2,6},{6,2},{3,7},{7,3},{8,12},{12,8},{9,1... | collective-permute-start | bytes 49160 | tf_op jit(solution)/shard_map/ppermute | solution.py:43
  162.3 3.2 %collective-permute-done.4 = f32[4,8,128]{2,1,0:T(8,128)S(1)} collective-permute-done((f32[4,8,128]{2,1,0:T(8,128)S(1)}, f32[4,8,128]{2,1,0:T(8,128)S(1)}, u32[]{:S(2)}, u32[]{:S(2)}) %collective-permute-start.4) | collective-permute-done | bytes 16416 | tf_op jit(solution)/shard_map/ppermute | solution.py:43
  165.6 3.8 %collective-permute-start.5 = (f32[2,8,128]{2,1,0:T(8,128)S(1)}, f32[2,8,128]{2,1,0:T(8,128)S(1)}, u32[]{:S(2)}, u32[]{:S(2)}) collective-permute-start(f32[2,8,128]{2,1,0:T(8,128)S(1)} %dynamic-slice_bitcast_fusion.2), channel_id=1, source_target_pairs={{0,8},{8,0},{16,24},{24,16},{1,9},{9,1},{17,25},{25,17},{2,10},{10... | collective-permute-start | bytes 24584 | tf_op jit(solution)/shard_map/ppermute | solution.py:43
  169.5 3.1 %all-to-all-done.3 = bf16[16,8,960]{2,1,0:T(8,128)(2,1)S(1)} async-done(((bf16[16,8,960]{2,1,0:T(8,128)(2,1)}), bf16[16,8,960]{2,1,0:T(8,128)(2,1)S(1)}, u32[]{:S(2)}, u32[]{:S(2)}) %all-to-all-start.3) | async-done | bytes 245792 | tf_op jit(solution)/shard_map/all_to_all | solution.py:28
  173.3 6.6 %all-to-all-start.4 = ((bf16[16,8,960]{2,1,0:T(8,128)(2,1)}), bf16[16,8,960]{2,1,0:T(8,128)(2,1)S(1)}, u32[]{:S(2)}, u32[]{:S(2)}) async-start(bf16[16,8,960]{2,1,0:T(8,128)(2,1)} %broadcast_in_dim.14), calls=%async_computation.4 | async-start | bytes 524288 | tf_op jit(solution)/shard_map/all_to_all | solution.py:28
  179.9 4.7 %collective-permute-start.6 = (f32[8,128]{1,0:T(8,128)S(1)}, f32[8,128]{1,0:T(8,128)S(1)}, u32[]{:S(2)}, u32[]{:S(2)}) collective-permute-start(f32[8,128]{1,0:T(8,128)S(1)} %dynamic-slice_bitcast_fusion.3), channel_id=1, source_target_pairs={{0,16},{8,24},{16,0},{24,8},{1,17},{9,25},{17,1},{25,9},{2,18},{10... | collective-permute-start | bytes 12296 | tf_op jit(solution)/shard_map/ppermute | solution.py:43
  184.7 4.7 %collective-permute-done.6 = f32[8,128]{1,0:T(8,128)S(1)} collective-permute-done((f32[8,128]{1,0:T(8,128)S(1)}, f32[8,128]{1,0:T(8,128)S(1)}, u32[]{:S(2)}, u32[]{:S(2)}) %collective-permute-start.6) | collective-permute-done | bytes 4128 | tf_op jit(solution)/shard_map/ppermute | solution.py:43
  (62 shorter events, 23.8 us)
Async XLA Ops:
  7.2 182.2 %copy-start = (bf16[8192,128]{1,0:T(8,128)(2,1)S(1)}, bf16[8192,128]{1,0:T(8,128)(2,1)}, u32[]{:S(2)}) copy-start(bf16[8192,128]{1,0:T(8,128)(2,1)} %param.19) | copy-start | bytes 6291460
  7.2 15.4 %copy-start.6 = (bf16[64,256]{1,0:T(8,128)(2,1)S(1)}, bf16[64,256]{1,0:T(8,128)(2,1)}, u32[]{:S(2)}) copy-start(bf16[64,256]{1,0:T(8,128)(2,1)} %param.17) | copy-start | bytes 98308
  7.2 25.6 %copy-start.2 = (bf16[832,512]{1,0:T(8,128)(2,1)S(1)}, bf16[832,512]{1,0:T(8,128)(2,1)}, u32[]{:S(2)}) copy-start(bf16[832,512]{1,0:T(8,128)(2,1)} %param.11) | copy-start | bytes 2555908
  9.8 23.0 %all-to-all-start = ((bf16[8,8,2304]{2,1,0:T(8,128)(2,1)}), bf16[8,8,2304]{2,1,0:T(8,128)(2,1)S(1)}, u32[]{:S(2)}, u32[]{:S(2)}) async-start(bf16[8,8,2304]{2,1,0:T(8,128)(2,1)} %bitcast.2), calls=%async_computation | async-start | bytes 589824 | tf_op jit(solution)/shard_map/all_to_all | solution.py:28
  20.1 60.4 %all-gather.2.cloned.1.call-start = ((), (), s32[]{:S(2)}) async-start(), calls=%async_computation.5 | async-start | bytes 2949120 | tf_op jit(solution)/shard_map/all_gather | solution.py:170
  22.6 12.2 %collective-permute-start = (bf16[64,256]{1,0:T(8,128)(2,1)S(1)}, bf16[64,256]{1,0:T(8,128)(2,1)S(1)}, u32[]{:S(2)}, u32[]{:S(2)}) collective-permute-start(bf16[64,256]{1,0:T(8,128)(2,1)S(1)} %copy-done.6), channel_id=1, source_target_pairs={{0,0},{32,1},{64,2},{96,3},{1,4},{33,5},{65,6},{97,7},{2,8},{34,9}... | collective-permute-start | bytes 98312 | tf_op jit(solution)/shard_map/ppermute | solution.py:167
  35.6 4.9 %copy-start.4 = (bf16[256,832]{0,1:T(8,128)(2,1)S(1)}, bf16[256,832]{0,1:T(8,128)(2,1)}, u32[]{:S(2)}) copy-start(bf16[256,832]{0,1:T(8,128)(2,1)} %param.12) | copy-start | bytes 1277956
  35.6 5.8 %copy-start.5 = (bf16[256,832]{0,1:T(8,128)(2,1)S(1)}, bf16[256,832]{0,1:T(8,128)(2,1)}, u32[]{:S(2)}) copy-start(bf16[256,832]{0,1:T(8,128)(2,1)} %param.13) | copy-start | bytes 1277956
  35.6 46.8 %all-to-all-start.1 = ((bf16[4,832,512]{2,1,0:T(8,128)(2,1)}), bf16[4,832,512]{2,1,0:T(8,128)(2,1)}, u32[]{:S(2)}, u32[]{:S(2)}) async-start(bf16[4,832,512]{2,1,0:T(8,128)(2,1)} %broadcast_in_dim.13), calls=%async_computation.1 | async-start | bytes 6815744 | tf_op jit(solution)/shard_map/all_to_all | solution.py:28
  80.5 7.6 %collective-permute-start.1 = (bf16[512,2560]{1,0:T(8,128)(2,1)}, bf16[512,2560]{1,0:T(8,128)(2,1)}, u32[]{:S(2)}, u32[]{:S(2)}) collective-permute-start(bf16[512,2560]{1,0:T(8,128)(2,1)} %bitcast.84), channel_id=1, source_target_pairs={{0,1},{1,0},{2,3},{3,2},{4,5},{5,4},{6,7},{7,6},{8,9},{9,8},{10,11... | collective-permute-start | bytes 7864328 | tf_op jit(solution)/shard_map/ppermute | solution.py:36
  82.4 2.8 %copy-start.1 = (bf16[4,128,2560]{2,1,0:T(8,128)(2,1)S(1)}, bf16[4,128,2560]{2,1,0:T(8,128)(2,1)}, u32[]{:S(2)}) copy-start(bf16[4,128,2560]{2,1,0:T(8,128)(2,1)} %all-gather.2.cloned.1.call-done) | copy-start | bytes 7864324
  85.6 2.1 %copy-start.3 = (bf16[832,64]{0,1:T(8,128)(2,1)S(1)}, bf16[832,64]{0,1:T(8,128)(2,1)}, u32[]{:S(2)}) copy-start(bf16[832,64]{0,1:T(8,128)(2,1)} %param.16) | copy-start | bytes 319492
  94.2 50.4 %all-to-all-start.2 = ((bf16[4,2,832,128]{3,2,1,0:T(8,128)(2,1)}), bf16[4,2,832,128]{3,2,1,0:T(8,128)(2,1)}, u32[]{:S(2)}, u32[]{:S(2)}) async-start(bf16[4,2,832,128]{3,2,1,0:T(8,128)(2,1)} %pad_maximum_fusion), calls=%async_computation.2 | async-start | bytes 3407872 | tf_op jit(solution)/shard_map/all_to_all | solution.py:28
  148.1 3.3 %collective-permute-start.2 = (f32[128,128]{1,0:T(8,128)}, f32[128,128]{1,0:T(8,128)S(1)}, u32[]{:S(2)}, u32[]{:S(2)}) collective-permute-start(f32[128,128]{1,0:T(8,128)} %get-tuple-element.35), channel_id=1, source_target_pairs={{0,1},{1,0},{2,3},{3,2},{4,5},{5,4},{6,7},{7,6},{8,9},{9,8},{10,11... | collective-permute-start | bytes 196616 | tf_op jit(solution)/shard_map/ppermute | solution.py:36
  152.3 7.6 %collective-permute-start.3 = (f32[8,8,128]{2,1,0:T(8,128)S(1)}, f32[8,8,128]{2,1,0:T(8,128)S(1)}, u32[]{:S(2)}, u32[]{:S(2)}) collective-permute-start(f32[8,8,128]{2,1,0:T(8,128)S(1)} %dynamic-slice_bitcast_fusion), channel_id=1, source_target_pairs={{0,2},{2,0},{1,3},{3,1},{4,6},{6,4},{5,7},{7,5},{8,10},{10,8},{9,1... | collective-permute-start | bytes 98312 | tf_op jit(solution)/shard_map/ppermute | solution.py:43
  154.2 18.3 %all-to-all-start.3 = ((bf16[16,8,960]{2,1,0:T(8,128)(2,1)}), bf16[16,8,960]{2,1,0:T(8,128)(2,1)S(1)}, u32[]{:S(2)}, u32[]{:S(2)}) async-start(bf16[16,8,960]{2,1,0:T(8,128)(2,1)} %bitcast.97), calls=%async_computation.3 | async-start | bytes 524288 | tf_op jit(solution)/shard_map/all_to_all | solution.py:28
  159.9 5.6 %collective-permute-start.4 = (f32[4,8,128]{2,1,0:T(8,128)S(1)}, f32[4,8,128]{2,1,0:T(8,128)S(1)}, u32[]{:S(2)}, u32[]{:S(2)}) collective-permute-start(f32[4,8,128]{2,1,0:T(8,128)S(1)} %dynamic-slice_bitcast_fusion.1), channel_id=1, source_target_pairs={{0,4},{4,0},{1,5},{5,1},{2,6},{6,2},{3,7},{7,3},{8,12},{12,8},{9,1... | collective-permute-start | bytes 49160 | tf_op jit(solution)/shard_map/ppermute | solution.py:43
  165.6 14.3 %collective-permute-start.5 = (f32[2,8,128]{2,1,0:T(8,128)S(1)}, f32[2,8,128]{2,1,0:T(8,128)S(1)}, u32[]{:S(2)}, u32[]{:S(2)}) collective-permute-start(f32[2,8,128]{2,1,0:T(8,128)S(1)} %dynamic-slice_bitcast_fusion.2), channel_id=1, source_target_pairs={{0,8},{8,0},{16,24},{24,16},{1,9},{9,1},{17,25},{25,17},{2,10},{10... | collective-permute-start | bytes 24584 | tf_op jit(solution)/shard_map/ppermute | solution.py:43
  173.3 18.4 %all-to-all-start.4 = ((bf16[16,8,960]{2,1,0:T(8,128)(2,1)}), bf16[16,8,960]{2,1,0:T(8,128)(2,1)S(1)}, u32[]{:S(2)}, u32[]{:S(2)}) async-start(bf16[16,8,960]{2,1,0:T(8,128)(2,1)} %broadcast_in_dim.14), calls=%async_computation.4 | async-start | bytes 524288 | tf_op jit(solution)/shard_map/all_to_all | solution.py:28
  179.9 9.4 %collective-permute-start.6 = (f32[8,128]{1,0:T(8,128)S(1)}, f32[8,128]{1,0:T(8,128)S(1)}, u32[]{:S(2)}, u32[]{:S(2)}) collective-permute-start(f32[8,128]{1,0:T(8,128)S(1)} %dynamic-slice_bitcast_fusion.3), channel_id=1, source_target_pairs={{0,16},{8,24},{16,0},{24,8},{1,17},{9,25},{17,1},{25,9},{2,18},{10... | collective-permute-start | bytes 12296 | tf_op jit(solution)/shard_map/ppermute | solution.py:43
Sparse Core Ops, SparseCore 0:
  35.7 44.7 all-gather.1

commit v4 on v2

--- a/solution.py
+++ b/solution.py
@@ -11,7 +11,6 @@
 Y = ("yh", "yl")
 DP = ("zh", "x")
 ST = ("yh", "yl", "zl", "c")
-TOKEN_ORDER = ("c", "yh", "yl", "zl")
 F32, BF16 = jnp.float32, jnp.bfloat16
 VMEM = pl.BlockSpec(memory_space=pltpu.VMEM)
 PARAMS = pltpu.CompilerParams(vmem_limit_bytes=56 * 2**20)
@@ -35,6 +34,22 @@
 
 def swap_cores(array):
     return lax.ppermute(array, "c", [(0, 1), (1, 0)])
+
+
+def halve(array, dim, axis, size, bit):
+    mine = lax.axis_index(axis) // bit % 2
+    kept = lax.dynamic_index_in_dim(array, mine, dim, False)
+    sent = lax.dynamic_index_in_dim(array, 1 - mine, dim, False)
+    return kept + lax.ppermute(sent, axis, [(i, i ^ bit) for i in range(size)])
+
+
+def by_permutes(whole):
+    zh = lax.axis_index("zh")
+    parts = []
+    for step in range(4):
+        block = lax.dynamic_slice_in_dim(whole, (zh + step) % 4 * 128, 128, 1)
+        parts.append(block if step == 0 else lax.ppermute(block, "zh", [(i, (i + step) % 4) for i in range(4)]))
+    return parts
 
 
 def band_pairs():
@@ -46,9 +61,15 @@
                 for yl in range(2):
                     for zl in range(2):
                         for c in range(2):
-                            source = index[yh, yl * 2 + zl, zh, x // 2, x % 2, c]
+                            source = index[yh, x, zh, yl, zl, c]
                             pairs.append((int(source), int(index[zh, x, yh, yl, zl, c])))
     return pairs
+
+
+def join(array, axis):
+    other = lax.ppermute(array, axis, [(0, 1), (1, 0)])
+    first = lax.axis_index(axis) == 0
+    return jnp.where(first, jnp.concatenate([array, other]), jnp.concatenate([other, array]))
 
 
 def partial_hidden(rows, weights, a_down):
@@ -56,34 +77,31 @@
     total = lax.dot_general(weights, rows, (((0, 2), (1, 2)), ((), ())), preferred_element_type=F32)
     rank = total[832:].astype(BF16)
     whole = total[:832] + jnp.dot(a_down, rank, preferred_element_type=F32)
-    return whole.astype(BF16).reshape(832, 4, 128).transpose(1, 0, 2)
-
-
-def adapter_terms(parts_ref, gate_ref, up_ref, saved_ref, b_gate_ref, b_up_ref):
-    grad_hidden = jnp.sum(parts_ref[...].astype(F32), axis=0)
+    return whole.astype(BF16)
+
+
+def adapter_sums(parts, gate_ref, up_ref, saved_ref, b_gate_ref, b_up_ref):
+    grad_hidden = (parts[0].astype(F32) + parts[1].astype(F32)) + (parts[2].astype(F32) + parts[3].astype(F32))
     grad_gate = (grad_hidden * gate_ref[...]).astype(BF16)
     grad_up = (grad_hidden * up_ref[...]).astype(BF16)
     rank = jnp.dot(b_gate_ref[...], grad_gate, preferred_element_type=F32)
     rank = rank + jnp.dot(b_up_ref[...], grad_up, preferred_element_type=F32)
-    into_gate = contract_last(saved_ref[:64, :], grad_gate)
-    into_up = contract_last(saved_ref[64:, :], grad_up)
-    return rank.T, into_gate, into_up
+    return rank.T, contract_last(saved_ref[:64, :], grad_gate), contract_last(saved_ref[64:, :], grad_up)
 
 
 def own_kernel(parts_ref, gate_ref, up_ref, saved_ref, b_gate_ref, b_up_ref, rank_ref, sums_ref):
-    rank, into_gate, into_up = adapter_terms(parts_ref, gate_ref, up_ref, saved_ref, b_gate_ref, b_up_ref)
+    rank, into_gate, into_up = adapter_sums(parts_ref[...], gate_ref, up_ref, saved_ref, b_gate_ref, b_up_ref)
     rank_ref[...] = rank
     sums_ref[:64, :] = into_gate
     sums_ref[64:, :] = into_up
 
 
 def other_kernel(
-    core_ref, parts_ref, gate_ref, up_ref, saved_ref, b_gate_ref, b_up_ref, own_rank_ref, own_sums_ref, down_ref, rank_ref, sums_ref
+    a_ref, b_ref, c_ref, d_ref, gate_ref, up_ref, saved_ref, b_gate_ref, b_up_ref, own_sums_ref, down_ref, rank_ref, sums_ref
 ):
-    rank, into_gate, into_up = adapter_terms(parts_ref, gate_ref, up_ref, saved_ref, b_gate_ref, b_up_ref)
-    core = core_ref[0]
-    rank_ref[core] = own_rank_ref[...]
-    rank_ref[1 - core] = rank
+    parts = (a_ref[...], b_ref[...], c_ref[...], d_ref[...])
+    rank, into_gate, into_up = adapter_sums(parts, gate_ref, up_ref, saved_ref, b_gate_ref, b_up_ref)
+    rank_ref[...] = rank
     sums_ref[:, :128] = down_ref[...]
     sums_ref[:64, 128:] = (own_sums_ref[:64, :] + into_gate).astype(BF16)
     sums_ref[64:, 128:] = (own_sums_ref[64:, :] + into_up).astype(BF16)
@@ -103,8 +121,8 @@
 def other_terms(*operands):
     return pl.pallas_call(
         other_kernel,
-        out_shape=(jax.ShapeDtypeStruct((2, 128, 128), F32), jax.ShapeDtypeStruct((128, 960), BF16)),
-        in_specs=[pl.BlockSpec(memory_space=pltpu.SMEM)] + [VMEM] * 9,
+        out_shape=(jax.ShapeDtypeStruct((128, 128), F32), jax.ShapeDtypeStruct((128, 960), BF16)),
+        in_specs=[VMEM] * 11,
         out_specs=(VMEM, VMEM),
         compiler_params=PARAMS,
         cost_estimate=pl.CostEstimate(flops=10**8, bytes_accessed=3 * 2**20, transcendentals=0),
@@ -174,38 +192,42 @@
     quarters = grad_out.reshape(8, 4, 2048).transpose(1, 0, 2)
     quarters = jnp.concatenate([quarters, jnp.broadcast_to(ranks[None], (4, 8, 256))], axis=2)
     blocks = jnp.broadcast_to(quarters[:, None], (4, 2, 8, 2304)).reshape(8, 8, 2304)
-    own_band = lax.ppermute(b_down, AXES, band_pairs())
-    other_band = swap_cores(own_band)
-    band_pair = jnp.where(
-        core == 0, jnp.concatenate([own_band, other_band], axis=1), jnp.concatenate([other_band, own_band], axis=1)
-    )
-    w_here = jnp.concatenate([w_down, band_pair])
     from_z = exchange(blocks, ("zh", "zl"))
     gate_factor, up_factor = factors(core, gate_pre, up_pre)
     none = jnp.zeros((64, 832), BF16)
     b_gate, b_up = jnp.concatenate([b_in[0], none]), jnp.concatenate([none, b_in[1]])
-    ready = (from_z, w_here, gate_factor, up_factor, b_gate, b_up, a_down)
-    from_z, w_here, gate_factor, up_factor, b_gate, b_up, a_down = lax.optimization_barrier(ready)
-    own_rows = lax.all_gather(from_z.reshape(4, 16, 2304), Y, axis=1, tiled=True).reshape(512, 2304)
-    weights = spread(w_here, "x", 4)
-    own_rows, weights = lax.optimization_barrier((own_rows, weights))
+    w_copies = jnp.broadcast_to(w_down[None], (4, 832, 512))
+    from_z, w_copies = lax.optimization_barrier((from_z, w_copies))
+    own = lax.all_gather(from_z.reshape(4, 16, 2304), Y, axis=1, tiled=True)
+    weights = exchange(w_copies.reshape(3328, 512), "x").reshape(4, 832, 512)
+    b_down, gate_factor, up_factor = lax.optimization_barrier((b_down, gate_factor, up_factor))
+    bands = lax.ppermute(b_down, AXES, band_pairs())[None]
+    bands = join(join(join(bands, "c"), "zl"), "yl")
+    bands = bands.reshape(4, 2, 64, 256).transpose(0, 2, 1, 3).reshape(4, 64, 512)
+    own, bands, a_down, b_gate, b_up = lax.optimization_barrier((own, bands, a_down, b_gate, b_up))
+    own_rows = own.reshape(512, 2304)
     other_rows = swap_cores(own_rows)
-
-    own_parts = exchange(partial_hidden(own_rows, weights, a_down), "zh")
+    weights = jnp.concatenate([weights, bands], axis=1)
+    own_partial = partial_hidden(own_rows, weights, a_down)
+    own_parts = exchange(own_partial.reshape(832, 4, 128).transpose(1, 0, 2), "zh")
     other_partial = partial_hidden(other_rows, weights, a_down)
-    other_parts = exchange(other_partial, "zh")
+    other_parts = by_permutes(other_partial)
 
     place = jnp.stack([station % 8, zh, (station // 8 == zh).astype(jnp.int32)])
     place, _ = lax.optimization_barrier((place, other_partial))
     saved, partial_down = saved_terms(place, own_rows, other_rows)
     partial_down = partial_down.reshape(128, 128)
     own_rank, own_sums = own_terms(own_parts, gate_factor[0], up_factor[0], saved[0], b_gate, b_up)
-    rank_partial, sums = other_terms(
-        core.reshape(1), other_parts, gate_factor[1], up_factor[1], saved[1], b_gate, b_up, own_rank, own_sums, partial_down
+    other_rank, sums = other_terms(
+        *other_parts, gate_factor[1], up_factor[1], saved[1], b_gate, b_up, own_sums, partial_down
     )
     sums = jnp.sum(exchange(sums.reshape(16, 8, 960), DP).astype(F32), axis=0).astype(BF16)
-    rank_partial, sums = lax.optimization_barrier((rank_partial, sums))
-    rank_grad = jnp.sum(exchange(rank_partial.reshape(32, 8, 128), TOKEN_ORDER), axis=0).astype(BF16)
+    rank_grad = (own_rank + swap_cores(other_rank)).reshape(8, 2, 8, 128)
+    rank_grad = halve(rank_grad, 1, "zl", 2, 1)
+    rank_grad = halve(rank_grad.reshape(4, 2, 8, 128), 1, "yl", 2, 1)
+    rank_grad = halve(rank_grad.reshape(2, 2, 8, 128), 1, "yh", 4, 1)
+    rank_grad = halve(rank_grad.reshape(2, 8, 128), 0, "yh", 4, 2)
+    rank_grad = rank_grad.astype(BF16)
     sums = spread(sums, DP, 16).astype(F32)
     grad_b_in = sums[:, :, 128:].reshape(2, 64, 832)
     grad_b_down = sums[:, :, :128].reshape(64, 256)

time: 212 us -> 194 us (0.915)
  blocking collectives: 82.7 us -> 22.8 us
  starting transfers between devices: 41.6 us -> 65.5 us
  waiting for transfers between devices: 30.7 us -> 46.2 us
  local copies, waits for them, and re-layouts: 20.3 us -> 23.1 us
    all_to_all x3 -> x1, blocking collectives: 82.7 us -> 22.8 us  [exchange(): return lax.all_to_all(blocks, axes, 0, 0, tiled=True)]
    ppermute x1 -> x11, starting transfers between devices: 5.08 us -> 37.7 us  [the longest x3 15.8 us: by_permutes(): lax.ppermute(block, 'zh', [(i, (i + step) % 4) for i in range(4)])]
    ppermute x1 -> x11, waiting for transfers between devices: 0.01 us -> 29 us  [the longest x3 12.2 us: join(): other = lax.ppermute(array, axis, [(0, 1), (1, 0)])]
    all_to_all x4, waiting for transfers between devices: 30.7 us -> 4.67 us  [exchange(): return lax.all_to_all(blocks, axes, 0, 0, tiled=True)]
    all_gather x1, waiting for transfers between devices: 0.01 us -> 11.1 us  [shards(): own = lax.all_gather(from_z.reshape(4, 16, 2304), Y, axis=1, tiled=True)]
    all_to_all x4, starting transfers between devices: 32.4 us -> 24 us  [exchange(): return lax.all_to_all(blocks, axes, 0, 0, tiled=True)]
    broadcast_in_dim x0 -> x1, local copies, waits for them, and re-layouts: none -> 3.12 us  [shards(): w_copies = jnp.broadcast_to(w_down[None], (4, 832, 512))]
    unnamed x18 -> x27, local copies, waits for them, and re-layouts: 3.48 us -> 6.39 us
  transfers between devices with their start and end apart: 8 -> 18, of which waited for: 4 -> 11; matrix products, arithmetic and copies ran while one was open for 13% -> 12% of each run, Pallas kernels for 4% -> 4%
where the time goes in v4:
time: 194 us; the launch traced here: 192 us
  starting transfers between devices  65.5 us (34%)
  waiting for transfers between devices  46.2 us (24%)
  local copies, waits for them, and re-layouts  23.1 us (12%)
  blocking collectives  22.8 us (12%)
  between operations  14.7 us (8%)
  Pallas kernels  11.3 us (6%)
  matrix products  6.3 us (3%)
  other arithmetic  2.53 us (1%)
    all_to_all x4, starting transfers between devices, exchange(): return lax.all_to_all(blocks, axes, 0, 0, tiled=True)  24 us
    all_to_all x1, blocking collectives, exchange(): return lax.all_to_all(blocks, axes, 0, 0, tiled=True)  22.8 us
    ppermute x3, starting transfers between devices, by_permutes(): lax.ppermute(block, 'zh', [(i, (i + step) % 4) for i in range(4)])  15.8 us
    ppermute x4, starting transfers between devices, halve(): return kept + lax.ppermute(sent, axis, [(i, i ^ bit) for i in range(size)])  14.5 us
    ppermute x3, waiting for transfers between devices, join(): other = lax.ppermute(array, axis, [(0, 1), (1, 0)])  12.2 us
    all_gather x1, waiting for transfers between devices, shards(): own = lax.all_gather(from_z.reshape(4, 16, 2304), Y, axis=1, tiled=True)  11.1 us
    ppermute x3, waiting for transfers between devices, by_permutes(): lax.ppermute(block, 'zh', [(i, (i + step) % 4) for i in range(4)])  10 us
    ppermute x4, waiting for transfers between devices, halve(): return kept + lax.ppermute(sent, axis, [(i, i ^ bit) for i in range(size)])  6.79 us
  transfers between devices with their start and end apart: 18, of which 11 were waited for; matrix products, arithmetic and copies ran while one was open for 12% of the time, Pallas kernels for 4%

profile of v4, /device:TPU:8, one launch (start us, length us, event | category | flops | bytes accessed | tf_op | source)
XLA Modules:
  0.0 192.4 jit_solution(6646344366365187298)
XLA Ops:
  9.1 22.8 %all_to_all.26 = bf16[8,8,2304]{2,1,0:T(8,128)(2,1)} all-to-all(bf16[8,8,2304]{2,1,0:T(8,128)(2,1)S(1)} %bitcast.92), channel_id=1, replica_groups=mesh['zh'=4,'x'=4,'yh'=4,'yl'=2,'zl'=2,'c'=2] {'zh','zl'}, dimensions={0} | all-to-all | bytes 589824 | tf_op jit(solution)/shard_map/all_to_all | solution.py:28
  31.9 3.1 %broadcast_in_dim.15 = bf16[4,832,512]{2,1,0:T(8,128)(2,1)} broadcast(bf16[832,512]{1,0:T(8,128)(2,1)} %param.11), dimensions={1,2} | broadcast | bytes 4259840 | tf_op jit(solution)/shard_map/broadcast_in_dim | solution.py:199
  35.1 4.8 %all-to-all-start.1 = ((bf16[4,832,512]{2,1,0:T(8,128)(2,1)}), bf16[4,832,512]{2,1,0:T(8,128)(2,1)}, u32[]{:S(2)}, u32[]{:S(2)}) async-start(bf16[4,832,512]{2,1,0:T(8,128)(2,1)} %broadcast_in_dim.15), calls=%async_computation.1 | async-start | bytes 6815744 | tf_op jit(solution)/shard_map/all_to_all | solution.py:28
  41.9 2.9 %shard_map.121 = (f32[2,832,128]{2,1,0:T(8,128)}, f32[2,832,128]{2,1,0:T(8,128)}) custom-call(s32[1]{0:T(128)} %bitcast.4.core_ref, bf16[256,832]{1,0:T(8,128)(2,1)} %copy.18.gate_ref, bf16[256,832]{1,0:T(8,128)(2,1)} %copy.19.up_ref), custom_call_target="tpu_custom_call" | custom-call | flops 10000000 | bytes 3145728 | tf_op jit(solution)/shard_map/pallas_call | solution.py:147
  51.2 4.2 %collective-permute-done.2 = bf16[2,64,256]{2,1,0:T(8,128)(2,1)S(1)} collective-permute-done((bf16[2,64,256]{2,1,0:T(8,128)(2,1)S(1)}, bf16[2,64,256]{2,1,0:T(8,128)(2,1)S(1)}, u32[]{:S(2)}, u32[]{:S(2)}) %collective-permute-start.2) | collective-permute-done | bytes 65568 | tf_op jit(solution)/shard_map/ppermute | solution.py:70
  59.1 6.8 %collective-permute-done.3 = bf16[4,64,256]{2,1,0:T(8,128)(2,1)S(1)} collective-permute-done((bf16[4,64,256]{2,1,0:T(8,128)(2,1)S(1)}, bf16[4,64,256]{2,1,0:T(8,128)(2,1)S(1)}, u32[]{:S(2)}, u32[]{:S(2)}) %collective-permute-start.3) | collective-permute-done | bytes 131104 | tf_op jit(solution)/shard_map/ppermute | solution.py:70
  66.4 11.1 %all-gather.2.cloned.1.call-done = bf16[4,128,2304]{2,1,0:T(8,128)(2,1)} async-done(((bf16[4,16,2304]{2,1,0:T(8,128)(2,1)}), bf16[4,128,2304]{2,1,0:T(8,128)(2,1)}) %all-gather.2.cloned.1.call-update) | async-done | bytes 2359312 | tf_op jit(solution)/shard_map/all_gather | solution.py:201
  88.5 7.2 %all-to-all-start.2 = ((bf16[4,832,128]{2,1,0:T(8,128)(2,1)}), bf16[4,832,128]{2,1,0:T(8,128)(2,1)S(1)}, u32[]{:S(2)}, u32[]{:S(2)}) async-start(bf16[4,832,128]{2,1,0:T(8,128)(2,1)} %bitcast.88), calls=%async_computation.2 | async-start | bytes 1703936 | tf_op jit(solution)/shard_map/all_to_all | solution.py:28
  102.5 4.8 %collective-permute-start.5 = (bf16[832,128]{1,0:T(8,128)(2,1)}, bf16[832,128]{1,0:T(8,128)(2,1)}, u32[]{:S(2)}, u32[]{:S(2)}) collective-permute-start(bf16[832,128]{1,0:T(8,128)(2,1)} %get-tuple-element.47), channel_id=1, source_target_pairs={{0,128},{128,256},{256,384},{384,0},{1,129},{129,257},{257,385},{3... | collective-permute-start | bytes 638984 | tf_op jit(solution)/shard_map/ppermute | solution.py:51
  107.3 5.5 %collective-permute-start.6 = (bf16[832,128]{1,0:T(8,128)(2,1)S(1)}, bf16[832,128]{1,0:T(8,128)(2,1)}, u32[]{:S(2)}, u32[]{:S(2)}) collective-permute-start(bf16[832,128]{1,0:T(8,128)(2,1)S(1)} %get-tuple-element.46), channel_id=1, source_target_pairs={{0,256},{128,384},{256,0},{384,128},{1,257},{129,385},{257,1},{385... | collective-permute-start | bytes 638984 | tf_op jit(solution)/shard_map/ppermute | solution.py:51
  112.8 5.5 %collective-permute-start.7 = (bf16[832,128]{1,0:T(8,128)(2,1)S(1)}, bf16[832,128]{1,0:T(8,128)(2,1)}, u32[]{:S(2)}, u32[]{:S(2)}) collective-permute-start(bf16[832,128]{1,0:T(8,128)(2,1)S(1)} %get-tuple-element.45), channel_id=1, source_target_pairs={{0,384},{128,0},{256,128},{384,256},{1,385},{129,1},{257,129},{385... | collective-permute-start | bytes 638984 | tf_op jit(solution)/shard_map/ppermute | solution.py:51
  118.3 2.7 %shard_map.122 = (bf16[2,128,128]{2,1,0:T(8,128)(2,1)}, bf16[64,256]{1,0:T(8,128)(2,1)}) custom-call(s32[3]{0:T(128)} %pad_add_fusion.place_ref, bf16[512,2304]{1,0:T(8,128)(2,1)} %bitcast.85, bf16[512,2304]{1,0:T(8,128)(2,1)} %collective-permute-done.4.other_band_ref.other_ranks_ref, bf16[512,2304]{1,0:T(8,128)(2,1)} %bitcast.86, ...), custom_call_target="tpu_custom_call" | custom-call | flops 33554432 | bytes 1048576 | tf_op jit(solution)/shard_map/pallas_call | solution.py:169
  124.7 2.8 %shard_map.123 = (f32[128,128]{1,0:T(8,128)}, f32[128,832]{1,0:T(8,128)}) custom-call(bf16[4,832,128]{2,1,0:T(8,128)(2,1)} %copy-done.2, f32[832,128]{1,0:T(8,128)} %get-tuple-element.53.gate_ref, f32[832,128]{1,0:T(8,128)} %get-tuple-element.42.up_ref, bf16[128,128]{1,0:T(8,128)(2,1)} %get-tuple-element.52.saved_ref, ...), custom_call_target="tpu_custom_call" | custom-call | flops 100000000 | bytes 3145728 | tf_op jit(solution)/shard_map/pallas_call | solution.py:111
  127.6 9.9 %collective-permute-done.7.d_ref = bf16[832,128]{1,0:T(8,128)(2,1)} collective-permute-done((bf16[832,128]{1,0:T(8,128)(2,1)S(1)}, bf16[832,128]{1,0:T(8,128)(2,1)}, u32[]{:S(2)}, u32[]{:S(2)}) %collective-permute-start.7) | collective-permute-done | bytes 213024 | tf_op jit(solution)/shard_map/ppermute | solution.py:51
  137.5 2.9 %shard_map.124 = (f32[128,128]{1,0:T(8,128)}, bf16[128,960]{1,0:T(8,128)(2,1)}) custom-call(bf16[832,128]{1,0:T(8,128)(2,1)} %get-tuple-element.48.a_ref, bf16[832,128]{1,0:T(8,128)(2,1)} %collective-permute-done.5.b_ref, bf16[832,128]{1,0:T(8,128)(2,1)} %collective-permute-done.6.c_ref, bf16[832,128]{1,0:T(8,128)(2,1)} %collective-permute-done.7.d_ref, ...), custom_call_target="tpu_custom_call" | custom-call | flops 100000000 | bytes 3145728 | tf_op jit(solution)/shard_map/pallas_call | solution.py:122
  143.9 3.3 %collective-permute-start.9 = (f32[8,8,128]{2,1,0:T(8,128)S(1)}, f32[8,8,128]{2,1,0:T(8,128)S(1)}, u32[]{:S(2)}, u32[]{:S(2)}) collective-permute-start(f32[8,8,128]{2,1,0:T(8,128)S(1)} %dynamic-slice_bitcast_fusion), channel_id=1, source_target_pairs={{0,2},{2,0},{1,3},{3,1},{4,6},{6,4},{5,7},{7,5},{8,10},{10,8},{9,1... | collective-permute-start | bytes 98312 | tf_op jit(solution)/shard_map/ppermute | solution.py:43
  147.2 6.1 %all-to-all-start.3 = ((bf16[16,8,960]{2,1,0:T(8,128)(2,1)}), bf16[16,8,960]{2,1,0:T(8,128)(2,1)S(1)}, u32[]{:S(2)}, u32[]{:S(2)}) async-start(bf16[16,8,960]{2,1,0:T(8,128)(2,1)} %bitcast.98), calls=%async_computation.3 | async-start | bytes 524288 | tf_op jit(solution)/shard_map/all_to_all | solution.py:28
  153.4 2.7 %collective-permute-start.10 = (f32[4,8,128]{2,1,0:T(8,128)S(1)}, f32[4,8,128]{2,1,0:T(8,128)S(1)}, u32[]{:S(2)}, u32[]{:S(2)}) collective-permute-start(f32[4,8,128]{2,1,0:T(8,128)S(1)} %dynamic-slice_bitcast_fusion.1), channel_id=1, source_target_pairs={{0,4},{4,0},{1,5},{5,1},{2,6},{6,2},{3,7},{7,3},{8,12},{12,8},{9,1... | collective-permute-start | bytes 49160 | tf_op jit(solution)/shard_map/ppermute | solution.py:43
  156.1 2.9 %collective-permute-done.10 = f32[4,8,128]{2,1,0:T(8,128)S(1)} collective-permute-done((f32[4,8,128]{2,1,0:T(8,128)S(1)}, f32[4,8,128]{2,1,0:T(8,128)S(1)}, u32[]{:S(2)}, u32[]{:S(2)}) %collective-permute-start.10) | collective-permute-done | bytes 16416 | tf_op jit(solution)/shard_map/ppermute | solution.py:43
  159.0 3.0 %collective-permute-start.11 = (f32[2,8,128]{2,1,0:T(8,128)S(1)}, f32[2,8,128]{2,1,0:T(8,128)S(1)}, u32[]{:S(2)}, u32[]{:S(2)}) collective-permute-start(f32[2,8,128]{2,1,0:T(8,128)S(1)} %dynamic-slice_bitcast_fusion.2), channel_id=1, source_target_pairs={{0,8},{8,0},{16,24},{24,16},{1,9},{9,1},{17,25},{25,17},{2,10},{10... | collective-permute-start | bytes 24584 | tf_op jit(solution)/shard_map/ppermute | solution.py:43
  162.1 3.8 %all-to-all-done.3 = bf16[16,8,960]{2,1,0:T(8,128)(2,1)S(1)} async-done(((bf16[16,8,960]{2,1,0:T(8,128)(2,1)}), bf16[16,8,960]{2,1,0:T(8,128)(2,1)S(1)}, u32[]{:S(2)}, u32[]{:S(2)}) %all-to-all-start.3) | async-done | bytes 245792 | tf_op jit(solution)/shard_map/all_to_all | solution.py:28
  166.6 5.9 %all-to-all-start.4 = ((bf16[16,8,960]{2,1,0:T(8,128)(2,1)}), bf16[16,8,960]{2,1,0:T(8,128)(2,1)S(1)}, u32[]{:S(2)}, u32[]{:S(2)}) async-start(bf16[16,8,960]{2,1,0:T(8,128)(2,1)} %broadcast_in_dim.17), calls=%async_computation.4 | async-start | bytes 524288 | tf_op jit(solution)/shard_map/all_to_all | solution.py:28
  172.5 5.5 %collective-permute-start.12 = (f32[8,128]{1,0:T(8,128)S(1)}, f32[8,128]{1,0:T(8,128)S(1)}, u32[]{:S(2)}, u32[]{:S(2)}) collective-permute-start(f32[8,128]{1,0:T(8,128)S(1)} %dynamic-slice_bitcast_fusion.3), channel_id=1, source_target_pairs={{0,16},{8,24},{16,0},{24,8},{1,17},{9,25},{17,1},{25,9},{2,18},{10... | collective-permute-start | bytes 12296 | tf_op jit(solution)/shard_map/ppermute | solution.py:43
  178.0 3.9 %collective-permute-done.12 = f32[8,128]{1,0:T(8,128)S(1)} collective-permute-done((f32[8,128]{1,0:T(8,128)S(1)}, f32[8,128]{1,0:T(8,128)S(1)}, u32[]{:S(2)}, u32[]{:S(2)}) %collective-permute-start.12) | collective-permute-done | bytes 4128 | tf_op jit(solution)/shard_map/ppermute | solution.py:43
  (87 shorter events, 43.6 us)
Async XLA Ops:
  7.2 174.8 %copy-start = (bf16[8192,128]{1,0:T(8,128)(2,1)S(1)}, bf16[8192,128]{1,0:T(8,128)(2,1)}, u32[]{:S(2)}) copy-start(bf16[8192,128]{1,0:T(8,128)(2,1)} %param.19) | copy-start | bytes 6291460
  7.2 70.3 %all-gather.2.cloned.1.call-start = ((), (), s32[]{:S(2)}) async-start(), calls=%async_computation.5 | async-start | bytes 2654208 | tf_op jit(solution)/shard_map/all_gather | solution.py:201
  35.0 4.9 %copy-start.6 = (bf16[256,832]{0,1:T(8,128)(2,1)S(1)}, bf16[256,832]{0,1:T(8,128)(2,1)}, u32[]{:S(2)}) copy-start(bf16[256,832]{0,1:T(8,128)(2,1)} %param.12) | copy-start | bytes 1277956
  35.1 5.9 %copy-start.7 = (bf16[256,832]{0,1:T(8,128)(2,1)S(1)}, bf16[256,832]{0,1:T(8,128)(2,1)}, u32[]{:S(2)}) copy-start(bf16[256,832]{0,1:T(8,128)(2,1)} %param.13) | copy-start | bytes 1277956
  35.1 46.9 %all-to-all-start.1 = ((bf16[4,832,512]{2,1,0:T(8,128)(2,1)}), bf16[4,832,512]{2,1,0:T(8,128)(2,1)}, u32[]{:S(2)}, u32[]{:S(2)}) async-start(bf16[4,832,512]{2,1,0:T(8,128)(2,1)} %broadcast_in_dim.15), calls=%async_computation.1 | async-start | bytes 6815744 | tf_op jit(solution)/shard_map/all_to_all | solution.py:28
  39.9 17.7 %copy-start.8 = (bf16[2,64,832]{2,1,0:T(8,128)(2,1)S(1)}, bf16[2,64,832]{2,1,0:T(8,128)(2,1)}, u32[]{:S(2)}) copy-start(bf16[2,64,832]{2,1,0:T(8,128)(2,1)} %param.18) | copy-start | bytes 638980
  44.7 34.8 %copy-start.5 = (f32[2,832,128]{2,1,0:T(8,128)S(1)}, f32[2,832,128]{2,1,0:T(8,128)}, u32[]{:S(2)}) copy-start(f32[2,832,128]{2,1,0:T(8,128)} %get-tuple-element.30) | copy-start | bytes 2555908
  44.7 0.8 collective-permute-start
  45.6 3.1 %collective-permute-start.1 = (bf16[1,64,256]{2,1,0:T(8,128)(2,1)S(1)}, bf16[1,64,256]{2,1,0:T(8,128)(2,1)S(1)}, u32[]{:S(2)}, u32[]{:S(2)}) collective-permute-start(bf16[1,64,256]{2,1,0:T(8,128)(2,1)S(1)} %bitcast.104), channel_id=1, source_target_pairs={{0,1},{1,0},{2,3},{3,2},{4,5},{5,4},{6,7},{7,6},{8,9},{9,8},{10,11... | collective-permute-start | bytes 98312 | tf_op jit(solution)/shard_map/ppermute | solution.py:70
  48.7 6.7 %collective-permute-start.2 = (bf16[2,64,256]{2,1,0:T(8,128)(2,1)S(1)}, bf16[2,64,256]{2,1,0:T(8,128)(2,1)S(1)}, u32[]{:S(2)}, u32[]{:S(2)}) collective-permute-start(bf16[2,64,256]{2,1,0:T(8,128)(2,1)S(1)} %maximum_select_fusion.2), channel_id=1, source_target_pairs={{0,2},{2,0},{1,3},{3,1},{4,6},{6,4},{5,7},{7,5},{8,10},{10,8},{9,1... | collective-permute-start | bytes 196616 | tf_op jit(solution)/shard_map/ppermute | solution.py:70
  55.4 10.5 %collective-permute-start.3 = (bf16[4,64,256]{2,1,0:T(8,128)(2,1)S(1)}, bf16[4,64,256]{2,1,0:T(8,128)(2,1)S(1)}, u32[]{:S(2)}, u32[]{:S(2)}) collective-permute-start(bf16[4,64,256]{2,1,0:T(8,128)(2,1)S(1)} %maximum_select_fusion.1), channel_id=1, source_target_pairs={{0,4},{4,0},{1,5},{5,1},{2,6},{6,2},{3,7},{7,3},{8,12},{12,8},{9,1... | collective-permute-start | bytes 393224 | tf_op jit(solution)/shard_map/ppermute | solution.py:70
  77.5 18.9 %collective-permute-start.4 = (bf16[512,2304]{1,0:T(8,128)(2,1)}, bf16[512,2304]{1,0:T(8,128)(2,1)}, u32[]{:S(2)}, u32[]{:S(2)}) collective-permute-start(bf16[512,2304]{1,0:T(8,128)(2,1)} %bitcast.84), channel_id=1, source_target_pairs={{0,1},{1,0},{2,3},{3,2},{4,5},{5,4},{6,7},{7,6},{8,9},{9,8},{10,11... | collective-permute-start | bytes 7077896 | tf_op jit(solution)/shard_map/ppermute | solution.py:36
  88.5 35.3 %all-to-all-start.2 = ((bf16[4,832,128]{2,1,0:T(8,128)(2,1)}), bf16[4,832,128]{2,1,0:T(8,128)(2,1)S(1)}, u32[]{:S(2)}, u32[]{:S(2)}) async-start(bf16[4,832,128]{2,1,0:T(8,128)(2,1)} %bitcast.88), calls=%async_computation.2 | async-start | bytes 1703936 | tf_op jit(solution)/shard_map/all_to_all | solution.py:28
  102.5 25.0 %collective-permute-start.5 = (bf16[832,128]{1,0:T(8,128)(2,1)}, bf16[832,128]{1,0:T(8,128)(2,1)}, u32[]{:S(2)}, u32[]{:S(2)}) collective-permute-start(bf16[832,128]{1,0:T(8,128)(2,1)} %get-tuple-element.47), channel_id=1, source_target_pairs={{0,128},{128,256},{256,384},{384,0},{1,129},{129,257},{257,385},{3... | collective-permute-start | bytes 638984 | tf_op jit(solution)/shard_map/ppermute | solution.py:51
  107.3 20.3 %collective-permute-start.6 = (bf16[832,128]{1,0:T(8,128)(2,1)S(1)}, bf16[832,128]{1,0:T(8,128)(2,1)}, u32[]{:S(2)}, u32[]{:S(2)}) collective-permute-start(bf16[832,128]{1,0:T(8,128)(2,1)S(1)} %get-tuple-element.46), channel_id=1, source_target_pairs={{0,256},{128,384},{256,0},{384,128},{1,257},{129,385},{257,1},{385... | collective-permute-start | bytes 638984 | tf_op jit(solution)/shard_map/ppermute | solution.py:51
  112.8 24.7 %collective-permute-start.7 = (bf16[832,128]{1,0:T(8,128)(2,1)S(1)}, bf16[832,128]{1,0:T(8,128)(2,1)}, u32[]{:S(2)}, u32[]{:S(2)}) collective-permute-start(bf16[832,128]{1,0:T(8,128)(2,1)S(1)} %get-tuple-element.45), channel_id=1, source_target_pairs={{0,384},{128,0},{256,128},{384,256},{1,385},{129,1},{257,129},{385... | collective-permute-start | bytes 638984 | tf_op jit(solution)/shard_map/ppermute | solution.py:51
  127.5 16.3 %copy-start.10 = (f32[128,128]{1,0:T(8,128)S(1)}, f32[128,128]{1,0:T(8,128)}, u32[]{:S(2)}) copy-start(f32[128,128]{1,0:T(8,128)} %get-tuple-element.36) | copy-start | bytes 196612
  140.5 3.3 %collective-permute-start.8 = (f32[128,128]{1,0:T(8,128)}, f32[128,128]{1,0:T(8,128)S(1)}, u32[]{:S(2)}, u32[]{:S(2)}) collective-permute-start(f32[128,128]{1,0:T(8,128)} %get-tuple-element.39), channel_id=1, source_target_pairs={{0,1},{1,0},{2,3},{3,2},{4,5},{5,4},{6,7},{7,6},{8,9},{9,8},{10,11... | collective-permute-start | bytes 196616 | tf_op jit(solution)/shard_map/ppermute | solution.py:36
  143.9 9.5 %collective-permute-start.9 = (f32[8,8,128]{2,1,0:T(8,128)S(1)}, f32[8,8,128]{2,1,0:T(8,128)S(1)}, u32[]{:S(2)}, u32[]{:S(2)}) collective-permute-start(f32[8,8,128]{2,1,0:T(8,128)S(1)} %dynamic-slice_bitcast_fusion), channel_id=1, source_target_pairs={{0,2},{2,0},{1,3},{3,1},{4,6},{6,4},{5,7},{7,5},{8,10},{10,8},{9,1... | collective-permute-start | bytes 98312 | tf_op jit(solution)/shard_map/ppermute | solution.py:43
  147.2 18.6 %all-to-all-start.3 = ((bf16[16,8,960]{2,1,0:T(8,128)(2,1)}), bf16[16,8,960]{2,1,0:T(8,128)(2,1)S(1)}, u32[]{:S(2)}, u32[]{:S(2)}) async-start(bf16[16,8,960]{2,1,0:T(8,128)(2,1)} %bitcast.98), calls=%async_computation.3 | async-start | bytes 524288 | tf_op jit(solution)/shard_map/all_to_all | solution.py:28
  153.4 5.6 %collective-permute-start.10 = (f32[4,8,128]{2,1,0:T(8,128)S(1)}, f32[4,8,128]{2,1,0:T(8,128)S(1)}, u32[]{:S(2)}, u32[]{:S(2)}) collective-permute-start(f32[4,8,128]{2,1,0:T(8,128)S(1)} %dynamic-slice_bitcast_fusion.1), channel_id=1, source_target_pairs={{0,4},{4,0},{1,5},{5,1},{2,6},{6,2},{3,7},{7,3},{8,12},{12,8},{9,1... | collective-permute-start | bytes 49160 | tf_op jit(solution)/shard_map/ppermute | solution.py:43
  159.0 13.5 %collective-permute-start.11 = (f32[2,8,128]{2,1,0:T(8,128)S(1)}, f32[2,8,128]{2,1,0:T(8,128)S(1)}, u32[]{:S(2)}, u32[]{:S(2)}) collective-permute-start(f32[2,8,128]{2,1,0:T(8,128)S(1)} %dynamic-slice_bitcast_fusion.2), channel_id=1, source_target_pairs={{0,8},{8,0},{16,24},{24,16},{1,9},{9,1},{17,25},{25,17},{2,10},{10... | collective-permute-start | bytes 24584 | tf_op jit(solution)/shard_map/ppermute | solution.py:43
  166.6 17.5 %all-to-all-start.4 = ((bf16[16,8,960]{2,1,0:T(8,128)(2,1)}), bf16[16,8,960]{2,1,0:T(8,128)(2,1)S(1)}, u32[]{:S(2)}, u32[]{:S(2)}) async-start(bf16[16,8,960]{2,1,0:T(8,128)(2,1)} %broadcast_in_dim.17), calls=%async_computation.4 | async-start | bytes 524288 | tf_op jit(solution)/shard_map/all_to_all | solution.py:28
  172.5 9.4 %collective-permute-start.12 = (f32[8,128]{1,0:T(8,128)S(1)}, f32[8,128]{1,0:T(8,128)S(1)}, u32[]{:S(2)}, u32[]{:S(2)}) collective-permute-start(f32[8,128]{1,0:T(8,128)S(1)} %dynamic-slice_bitcast_fusion.3), channel_id=1, source_target_pairs={{0,16},{8,24},{16,0},{24,8},{1,17},{9,25},{17,1},{25,9},{2,18},{10... | collective-permute-start | bytes 12296 | tf_op jit(solution)/shard_map/ppermute | solution.py:43
  (6 other events, 15.4 us)
Sparse Core Ops, SparseCore 0:
  35.2 42.2 all-gather.1

commit v5 on v4

--- a/solution.py
+++ b/solution.py
@@ -89,27 +89,27 @@
     return rank.T, contract_last(saved_ref[:64, :], grad_gate), contract_last(saved_ref[64:, :], grad_up)
 
 
-def own_kernel(parts_ref, gate_ref, up_ref, saved_ref, b_gate_ref, b_up_ref, rank_ref, sums_ref):
+def first_kernel(parts_ref, gate_ref, up_ref, saved_ref, b_gate_ref, b_up_ref, rank_ref, sums_ref):
     rank, into_gate, into_up = adapter_sums(parts_ref[...], gate_ref, up_ref, saved_ref, b_gate_ref, b_up_ref)
     rank_ref[...] = rank
     sums_ref[:64, :] = into_gate
     sums_ref[64:, :] = into_up
 
 
-def other_kernel(
-    a_ref, b_ref, c_ref, d_ref, gate_ref, up_ref, saved_ref, b_gate_ref, b_up_ref, own_sums_ref, down_ref, rank_ref, sums_ref
+def last_kernel(
+    a_ref, b_ref, c_ref, d_ref, gate_ref, up_ref, saved_ref, b_gate_ref, b_up_ref, first_ref, down_ref, rank_ref, sums_ref
 ):
     parts = (a_ref[...], b_ref[...], c_ref[...], d_ref[...])
     rank, into_gate, into_up = adapter_sums(parts, gate_ref, up_ref, saved_ref, b_gate_ref, b_up_ref)
     rank_ref[...] = rank
     sums_ref[:, :128] = down_ref[...]
-    sums_ref[:64, 128:] = (own_sums_ref[:64, :] + into_gate).astype(BF16)
-    sums_ref[64:, 128:] = (own_sums_ref[64:, :] + into_up).astype(BF16)
-
-
-def own_terms(*operands):
-    return pl.pallas_call(
-        own_kernel,
+    sums_ref[:64, 128:] = (first_ref[:64, :] + into_gate).astype(BF16)
+    sums_ref[64:, 128:] = (first_ref[64:, :] + into_up).astype(BF16)
+
+
+def first_terms(*operands):
+    return pl.pallas_call(
+        first_kernel,
         out_shape=(jax.ShapeDtypeStruct((128, 128), F32), jax.ShapeDtypeStruct((128, 832), F32)),
         in_specs=[VMEM] * 6,
         out_specs=(VMEM, VMEM),
@@ -118,9 +118,9 @@
     )(*operands)
 
 
-def other_terms(*operands):
-    return pl.pallas_call(
-        other_kernel,
+def last_terms(*operands):
+    return pl.pallas_call(
+        last_kernel,
         out_shape=(jax.ShapeDtypeStruct((128, 128), F32), jax.ShapeDtypeStruct((128, 960), BF16)),
         in_specs=[VMEM] * 11,
         out_specs=(VMEM, VMEM),
@@ -129,38 +129,42 @@
     )(*operands)
 
 
-def factor_kernel(core_ref, gate_ref, up_ref, gate_out, up_out):
-    core = core_ref[0]
+def factor_kernel(core_ref, gate_ref, up_ref, own_gate_ref, own_up_ref, other_gate_ref, other_up_ref):
     gate_rows = gate_ref[...].astype(F32).reshape(16, 2, 8, 832)
     up_rows = up_ref[...].astype(F32).reshape(16, 2, 8, 832)
-    for which in range(2):
-        slot = core if which == 0 else 1 - core
-        gate_value = gate_rows[:, which].reshape(128, 832)
+    first = core_ref[0] == 0
+
+    def tokens(rows, own):
+        zero, one = rows[:, 0].reshape(128, 832), rows[:, 1].reshape(128, 832)
+        return jnp.where(first, zero, one) if own else jnp.where(first, one, zero)
+
+    for own, gate_out, up_out in ((True, own_gate_ref, own_up_ref), (False, other_gate_ref, other_up_ref)):
+        gate_value = tokens(gate_rows, own)
         sigmoid_gate = jax.nn.sigmoid(gate_value)
-        up_out[slot] = (gate_value * sigmoid_gate).T
+        up_out[...] = (gate_value * sigmoid_gate).T
         slope = sigmoid_gate * (1.0 + gate_value * (1.0 - sigmoid_gate))
-        gate_out[slot] = (up_rows[:, which].reshape(128, 832) * slope).T
+        gate_out[...] = (tokens(up_rows, own) * slope).T
 
 
 def factors(core, gate_pre, up_pre):
-    shape = jax.ShapeDtypeStruct((2, 832, 128), F32)
+    shape = jax.ShapeDtypeStruct((832, 128), F32)
     return pl.pallas_call(
         factor_kernel,
-        out_shape=(shape, shape),
+        out_shape=(shape,) * 4,
         in_specs=[pl.BlockSpec(memory_space=pltpu.SMEM), VMEM, VMEM],
-        out_specs=(VMEM, VMEM),
+        out_specs=(VMEM,) * 4,
         compiler_params=PARAMS,
         cost_estimate=pl.CostEstimate(flops=10**7, bytes_accessed=3 * 2**20, transcendentals=256 * 832),
     )(core.reshape(1), gate_pre, up_pre)
 
 
-def saved_kernel(place_ref, own_band_ref, other_band_ref, own_ranks_ref, other_ranks_ref, saved_ref, down_ref):
+def saved_kernel(place_ref, own_band_ref, other_band_ref, own_ranks_ref, other_ranks_ref, own_saved_ref, other_saved_ref, down_ref):
     down = contract_first(own_ranks_ref[:, 128:192], own_band_ref[...])
     down = down + contract_first(other_ranks_ref[:, 128:192], other_band_ref[...])
     down_ref[...] = jnp.where(place_ref[2] == 1, down, 0.0).astype(BF16)
     window = pl.ds(pl.multiple_of(place_ref[1] * 128, 128), 128)
-    saved_ref[0] = own_ranks_ref[window, :128].T
-    saved_ref[1] = other_ranks_ref[window, :128].T
+    own_saved_ref[...] = own_ranks_ref[window, :128].T
+    other_saved_ref[...] = other_ranks_ref[window, :128].T
 
 
 def saved_terms(place, own_rows, other_rows):
@@ -173,11 +177,16 @@
             grid=(1,),
             in_specs=[band, band, ranks, ranks],
             out_specs=(
-                pl.BlockSpec((2, 128, 128), lambda i, place: (0, 0, 0)),
+                pl.BlockSpec((128, 128), lambda i, place: (0, 0)),
+                pl.BlockSpec((128, 128), lambda i, place: (0, 0)),
                 pl.BlockSpec((64, 256), lambda i, place: (0, 0)),
             ),
         ),
-        out_shape=(jax.ShapeDtypeStruct((2, 128, 128), BF16), jax.ShapeDtypeStruct((64, 256), BF16)),
+        out_shape=(
+            jax.ShapeDtypeStruct((128, 128), BF16),
+            jax.ShapeDtypeStruct((128, 128), BF16),
+            jax.ShapeDtypeStruct((64, 256), BF16),
+        ),
         compiler_params=PARAMS,
         cost_estimate=pl.CostEstimate(flops=2 * 1024 * 64 * 256, bytes_accessed=2**20, transcendentals=0),
     )(place, own_rows, other_rows, own_rows, other_rows)
@@ -193,14 +202,14 @@
     quarters = jnp.concatenate([quarters, jnp.broadcast_to(ranks[None], (4, 8, 256))], axis=2)
     blocks = jnp.broadcast_to(quarters[:, None], (4, 2, 8, 2304)).reshape(8, 8, 2304)
     from_z = exchange(blocks, ("zh", "zl"))
-    gate_factor, up_factor = factors(core, gate_pre, up_pre)
+    own_gate, own_up, other_gate, other_up = factors(core, gate_pre, up_pre)
     none = jnp.zeros((64, 832), BF16)
     b_gate, b_up = jnp.concatenate([b_in[0], none]), jnp.concatenate([none, b_in[1]])
     w_copies = jnp.broadcast_to(w_down[None], (4, 832, 512))
-    from_z, w_copies = lax.optimization_barrier((from_z, w_copies))
+    _, w_copies = lax.optimization_barrier((from_z, w_copies))
     own = lax.all_gather(from_z.reshape(4, 16, 2304), Y, axis=1, tiled=True)
     weights = exchange(w_copies.reshape(3328, 512), "x").reshape(4, 832, 512)
-    b_down, gate_factor, up_factor = lax.optimization_barrier((b_down, gate_factor, up_factor))
+    b_down, own_gate, own_up, other_gate, other_up = lax.optimization_barrier((b_down, own_gate, own_up, other_gate, other_up))
     bands = lax.ppermute(b_down, AXES, band_pairs())[None]
     bands = join(join(join(bands, "c"), "zl"), "yl")
     bands = bands.reshape(4, 2, 64, 256).transpose(0, 2, 1, 3).reshape(4, 64, 512)
@@ -215,11 +224,11 @@
 
     place = jnp.stack([station % 8, zh, (station // 8 == zh).astype(jnp.int32)])
     place, _ = lax.optimization_barrier((place, other_partial))
-    saved, partial_down = saved_terms(place, own_rows, other_rows)
+    own_saved, other_saved, partial_down = saved_terms(place, own_rows, other_rows)
     partial_down = partial_down.reshape(128, 128)
-    own_rank, own_sums = own_terms(own_parts, gate_factor[0], up_factor[0], saved[0], b_gate, b_up)
-    other_rank, sums = other_terms(
-        *other_parts, gate_factor[1], up_factor[1], saved[1], b_gate, b_up, own_sums, partial_down
+    own_rank, first = first_terms(own_parts, own_gate, own_up, own_saved, b_gate, b_up)
+    other_rank, sums = last_terms(
+        *other_parts, other_gate, other_up, other_saved, b_gate, b_up, first, partial_down
     )
     sums = jnp.sum(exchange(sums.reshape(16, 8, 960), DP).astype(F32), axis=0).astype(BF16)
     rank_grad = (own_rank + swap_cores(other_rank)).reshape(8, 2, 8, 128)

time: 194 us -> 188 us (0.969)
  local copies, waits for them, and re-layouts: 23.1 us -> 18.1 us
    all_to_all x4, waiting for transfers between devices: 4.67 us -> 9.2 us  [exchange(): return lax.all_to_all(blocks, axes, 0, 0, tiled=True)]
    squeeze x2 -> x0, local copies, waits for them, and re-layouts: 3.8 us -> none  [the longest x1 2.4 us: shards(): up_factor[1]]
    ppermute x3, waiting for transfers between devices: 10 us -> 6.71 us  [by_permutes(): lax.ppermute(block, 'zh', [(i, (i + step) % 4) for i in range(4)])]
  transfers between devices with their start and end apart: 18 -> 18, of which waited for: 11 -> 12; matrix products, arithmetic and copies ran while one was open for 12% -> 11% of each run, Pallas kernels for 4% -> 4%
where the time goes in v5:
time: 188 us; the launch traced here: 187 us
  starting transfers between devices  66.8 us (36%)
  waiting for transfers between devices  44.9 us (24%)
  blocking collectives  22.8 us (12%)
  local copies, waits for them, and re-layouts  18.1 us (10%)
  between operations  14.6 us (8%)
  Pallas kernels  11.1 us (6%)
  matrix products  6.31 us (3%)
  other arithmetic  2.62 us (1%)
    all_to_all x4, starting transfers between devices, exchange(): return lax.all_to_all(blocks, axes, 0, 0, tiled=True)  24.6 us
    all_to_all x1, blocking collectives, exchange(): return lax.all_to_all(blocks, axes, 0, 0, tiled=True)  22.8 us
    ppermute x3, starting transfers between devices, by_permutes(): lax.ppermute(block, 'zh', [(i, (i + step) % 4) for i in range(4)])  15.8 us
    ppermute x4, starting transfers between devices, halve(): return kept + lax.ppermute(sent, axis, [(i, i ^ bit) for i in range(size)])  15.1 us
    ppermute x3, waiting for transfers between devices, join(): other = lax.ppermute(array, axis, [(0, 1), (1, 0)])  11.8 us
    all_gather x1, waiting for transfers between devices, shards(): own = lax.all_gather(from_z.reshape(4, 16, 2304), Y, axis=1, tiled=True)  9.87 us
    all_to_all x4, waiting for transfers between devices, exchange(): return lax.all_to_all(blocks, axes, 0, 0, tiled=True)  9.2 us
    ppermute x3, starting transfers between devices, join(): other = lax.ppermute(array, axis, [(0, 1), (1, 0)])  6.81 us
  transfers between devices with their start and end apart: 18, of which 12 were waited for; matrix products, arithmetic and copies ran while one was open for 11% of the time, Pallas kernels for 4%

profile of v5, /device:TPU:8, one launch (start us, length us, event | category | flops | bytes accessed | tf_op | source)
XLA Modules:
  0.0 187.2 jit_solution(5918125117369240369)
XLA Ops:
  9.2 22.8 %all_to_all.26 = bf16[8,8,2304]{2,1,0:T(8,128)(2,1)} all-to-all(bf16[8,8,2304]{2,1,0:T(8,128)(2,1)S(1)} %bitcast.80), channel_id=1, replica_groups=mesh['zh'=4,'x'=4,'yh'=4,'yl'=2,'zl'=2,'c'=2] {'zh','zl'}, dimensions={0} | all-to-all | bytes 589824 | tf_op jit(solution)/shard_map/all_to_all | solution.py:28
  34.1 4.8 %all-to-all-start.1 = ((bf16[4,832,512]{2,1,0:T(8,128)(2,1)}), bf16[4,832,512]{2,1,0:T(8,128)(2,1)}, u32[]{:S(2)}, u32[]{:S(2)}) async-start(bf16[4,832,512]{2,1,0:T(8,128)(2,1)} %broadcast_in_dim.15), calls=%async_computation.1 | async-start | bytes 6815744 | tf_op jit(solution)/shard_map/all_to_all | solution.py:28
  40.9 2.7 %shard_map.121 = (f32[832,128]{1,0:T(8,128)}, f32[832,128]{1,0:T(8,128)}, f32[832,128]{1,0:T(8,128)}, f32[832,128]{1,0:T(8,128)}) custom-call(s32[1]{0:T(128)} %bitcast.4.core_ref, bf16[256,832]{1,0:T(8,128)(2,1)} %copy.18.gate_ref, bf16[256,832]{1,0:T(8,128)(2,1)} %copy.19.up_ref), custom_call_target="tpu_custom_call" | custom-call | flops 10000000 | bytes 3145728 | tf_op jit(solution)/shard_map/pallas_call | solution.py:151
  47.4 2.5 %collective-permute-start.2 = (bf16[2,64,256]{2,1,0:T(8,128)(2,1)S(1)}, bf16[2,64,256]{2,1,0:T(8,128)(2,1)S(1)}, u32[]{:S(2)}, u32[]{:S(2)}) collective-permute-start(bf16[2,64,256]{2,1,0:T(8,128)(2,1)S(1)} %maximum_select_fusion.2), channel_id=1, source_target_pairs={{0,2},{2,0},{1,3},{3,1},{4,6},{6,4},{5,7},{7,5},{8,10},{10,8},{9,1... | collective-permute-start | bytes 196616 | tf_op jit(solution)/shard_map/ppermute | solution.py:70
  49.8 4.0 %collective-permute-done.2 = bf16[2,64,256]{2,1,0:T(8,128)(2,1)S(1)} collective-permute-done((bf16[2,64,256]{2,1,0:T(8,128)(2,1)S(1)}, bf16[2,64,256]{2,1,0:T(8,128)(2,1)S(1)}, u32[]{:S(2)}, u32[]{:S(2)}) %collective-permute-start.2) | collective-permute-done | bytes 65568 | tf_op jit(solution)/shard_map/ppermute | solution.py:70
  53.9 2.4 %collective-permute-start.3 = (bf16[4,64,256]{2,1,0:T(8,128)(2,1)S(1)}, bf16[4,64,256]{2,1,0:T(8,128)(2,1)S(1)}, u32[]{:S(2)}, u32[]{:S(2)}) collective-permute-start(bf16[4,64,256]{2,1,0:T(8,128)(2,1)S(1)} %maximum_select_fusion.1), channel_id=1, source_target_pairs={{0,4},{4,0},{1,5},{5,1},{2,6},{6,2},{3,7},{7,3},{8,12},{12,8},{9,1... | collective-permute-start | bytes 393224 | tf_op jit(solution)/shard_map/ppermute | solution.py:70
  57.8 6.6 %collective-permute-done.3 = bf16[4,64,256]{2,1,0:T(8,128)(2,1)S(1)} collective-permute-done((bf16[4,64,256]{2,1,0:T(8,128)(2,1)S(1)}, bf16[4,64,256]{2,1,0:T(8,128)(2,1)S(1)}, u32[]{:S(2)}, u32[]{:S(2)}) %collective-permute-start.3) | collective-permute-done | bytes 131104 | tf_op jit(solution)/shard_map/ppermute | solution.py:70
  64.8 9.9 %all-gather.2.cloned.1.call-done = bf16[4,128,2304]{2,1,0:T(8,128)(2,1)} async-done(((bf16[4,16,2304]{2,1,0:T(8,128)(2,1)}), bf16[4,128,2304]{2,1,0:T(8,128)(2,1)}) %all-gather.2.cloned.1.call-update) | async-done | bytes 2359312 | tf_op jit(solution)/shard_map/all_gather | solution.py:210
  84.2 6.6 %all-to-all-start.2 = ((bf16[4,832,128]{2,1,0:T(8,128)(2,1)}), bf16[4,832,128]{2,1,0:T(8,128)(2,1)S(1)}, u32[]{:S(2)}, u32[]{:S(2)}) async-start(bf16[4,832,128]{2,1,0:T(8,128)(2,1)} %bitcast.76), calls=%async_computation.2 | async-start | bytes 1703936 | tf_op jit(solution)/shard_map/all_to_all | solution.py:28
  96.9 4.8 %collective-permute-start.5 = (bf16[832,128]{1,0:T(8,128)(2,1)}, bf16[832,128]{1,0:T(8,128)(2,1)}, u32[]{:S(2)}, u32[]{:S(2)}) collective-permute-start(bf16[832,128]{1,0:T(8,128)(2,1)} %get-tuple-element.51), channel_id=1, source_target_pairs={{0,128},{128,256},{256,384},{384,0},{1,129},{129,257},{257,385},{3... | collective-permute-start | bytes 638984 | tf_op jit(solution)/shard_map/ppermute | solution.py:51
  101.7 5.5 %collective-permute-start.6 = (bf16[832,128]{1,0:T(8,128)(2,1)S(1)}, bf16[832,128]{1,0:T(8,128)(2,1)}, u32[]{:S(2)}, u32[]{:S(2)}) collective-permute-start(bf16[832,128]{1,0:T(8,128)(2,1)S(1)} %get-tuple-element.50), channel_id=1, source_target_pairs={{0,256},{128,384},{256,0},{384,128},{1,257},{129,385},{257,1},{385... | collective-permute-start | bytes 638984 | tf_op jit(solution)/shard_map/ppermute | solution.py:51
  107.2 5.5 %collective-permute-start.7 = (bf16[832,128]{1,0:T(8,128)(2,1)S(1)}, bf16[832,128]{1,0:T(8,128)(2,1)}, u32[]{:S(2)}, u32[]{:S(2)}) collective-permute-start(bf16[832,128]{1,0:T(8,128)(2,1)S(1)} %get-tuple-element.49), channel_id=1, source_target_pairs={{0,384},{128,0},{256,128},{384,256},{1,385},{129,1},{257,129},{385... | collective-permute-start | bytes 638984 | tf_op jit(solution)/shard_map/ppermute | solution.py:51
  113.4 2.7 %shard_map.122 = (bf16[128,128]{1,0:T(8,128)(2,1)}, bf16[128,128]{1,0:T(8,128)(2,1)}, bf16[64,256]{1,0:T(8,128)(2,1)}) custom-call(s32[3]{0:T(128)} %pad_add_fusion.place_ref, bf16[512,2304]{1,0:T(8,128)(2,1)} %bitcast.73, bf16[512,2304]{1,0:T(8,128)(2,1)} %collective-permute-done.4.other_band_ref.other_ranks_ref, bf16[512,2304]{1,0:T(8,128)(2,1)} %bitcast.74, ...), custom_call_target="tpu_custom_call" | custom-call | flops 33554432 | bytes 1048576 | tf_op jit(solution)/shard_map/pallas_call | solution.py:173
  117.5 3.8 %all-to-all-done.2.parts_ref = bf16[4,832,128]{2,1,0:T(8,128)(2,1)S(1)} async-done(((bf16[4,832,128]{2,1,0:T(8,128)(2,1)}), bf16[4,832,128]{2,1,0:T(8,128)(2,1)S(1)}, u32[]{:S(2)}, u32[]{:S(2)}) %all-to-all-start.2) | async-done | bytes 852000 | tf_op jit(solution)/shard_map/all_to_all | solution.py:28
  122.2 2.8 %shard_map.123 = (f32[128,128]{1,0:T(8,128)}, f32[128,832]{1,0:T(8,128)}) custom-call(bf16[4,832,128]{2,1,0:T(8,128)(2,1)} %copy-done.2, f32[832,128]{1,0:T(8,128)} %get-tuple-element.35.gate_ref, f32[832,128]{1,0:T(8,128)} %get-tuple-element.36.up_ref, bf16[128,128]{1,0:T(8,128)(2,1)} %get-tuple-element.38.saved_ref, ...), custom_call_target="tpu_custom_call" | custom-call | flops 100000000 | bytes 3145728 | tf_op jit(solution)/shard_map/pallas_call | solution.py:111
  125.0 6.7 %collective-permute-done.6.c_ref = bf16[832,128]{1,0:T(8,128)(2,1)} collective-permute-done((bf16[832,128]{1,0:T(8,128)(2,1)S(1)}, bf16[832,128]{1,0:T(8,128)(2,1)}, u32[]{:S(2)}, u32[]{:S(2)}) %collective-permute-start.6) | collective-permute-done | bytes 213024 | tf_op jit(solution)/shard_map/ppermute | solution.py:51
  131.7 3.0 %shard_map.124 = (f32[128,128]{1,0:T(8,128)}, bf16[128,960]{1,0:T(8,128)(2,1)}) custom-call(bf16[832,128]{1,0:T(8,128)(2,1)} %get-tuple-element.52.a_ref, bf16[832,128]{1,0:T(8,128)(2,1)} %collective-permute-done.5.b_ref, bf16[832,128]{1,0:T(8,128)(2,1)} %collective-permute-done.6.c_ref, bf16[832,128]{1,0:T(8,128)(2,1)} %collective-permute-done.7.d_ref, ...), custom_call_target="tpu_custom_call" | custom-call | flops 100000000 | bytes 3145728 | tf_op jit(solution)/shard_map/pallas_call | solution.py:122
  140.0 6.8 %all-to-all-start.3 = ((bf16[16,8,960]{2,1,0:T(8,128)(2,1)}), bf16[16,8,960]{2,1,0:T(8,128)(2,1)S(1)}, u32[]{:S(2)}, u32[]{:S(2)}) async-start(bf16[16,8,960]{2,1,0:T(8,128)(2,1)} %bitcast.86), calls=%async_computation.3 | async-start | bytes 524288 | tf_op jit(solution)/shard_map/all_to_all | solution.py:28
  146.8 4.2 %collective-permute-start.10 = (f32[4,8,128]{2,1,0:T(8,128)S(1)}, f32[4,8,128]{2,1,0:T(8,128)S(1)}, u32[]{:S(2)}, u32[]{:S(2)}) collective-permute-start(f32[4,8,128]{2,1,0:T(8,128)S(1)} %dynamic-slice_bitcast_fusion.1), channel_id=1, source_target_pairs={{0,4},{4,0},{1,5},{5,1},{2,6},{6,2},{3,7},{7,3},{8,12},{12,8},{9,1... | collective-permute-start | bytes 49160 | tf_op jit(solution)/shard_map/ppermute | solution.py:43
  152.7 3.8 %collective-permute-start.11 = (f32[2,8,128]{2,1,0:T(8,128)S(1)}, f32[2,8,128]{2,1,0:T(8,128)S(1)}, u32[]{:S(2)}, u32[]{:S(2)}) collective-permute-start(f32[2,8,128]{2,1,0:T(8,128)S(1)} %dynamic-slice_bitcast_fusion.2), channel_id=1, source_target_pairs={{0,8},{8,0},{16,24},{24,16},{1,9},{9,1},{17,25},{25,17},{2,10},{10... | collective-permute-start | bytes 24584 | tf_op jit(solution)/shard_map/ppermute | solution.py:43
  156.6 3.3 %all-to-all-done.3 = bf16[16,8,960]{2,1,0:T(8,128)(2,1)S(1)} async-done(((bf16[16,8,960]{2,1,0:T(8,128)(2,1)}), bf16[16,8,960]{2,1,0:T(8,128)(2,1)S(1)}, u32[]{:S(2)}, u32[]{:S(2)}) %all-to-all-start.3) | async-done | bytes 245792 | tf_op jit(solution)/shard_map/all_to_all | solution.py:28
  160.6 6.3 %all-to-all-start.4 = ((bf16[16,8,960]{2,1,0:T(8,128)(2,1)}), bf16[16,8,960]{2,1,0:T(8,128)(2,1)S(1)}, u32[]{:S(2)}, u32[]{:S(2)}) async-start(bf16[16,8,960]{2,1,0:T(8,128)(2,1)} %broadcast_in_dim.17), calls=%async_computation.4 | async-start | bytes 524288 | tf_op jit(solution)/shard_map/all_to_all | solution.py:28
  167.0 5.2 %collective-permute-start.12 = (f32[8,128]{1,0:T(8,128)S(1)}, f32[8,128]{1,0:T(8,128)S(1)}, u32[]{:S(2)}, u32[]{:S(2)}) collective-permute-start(f32[8,128]{1,0:T(8,128)S(1)} %dynamic-slice_bitcast_fusion.3), channel_id=1, source_target_pairs={{0,16},{8,24},{16,0},{24,8},{1,17},{9,25},{17,1},{25,9},{2,18},{10... | collective-permute-start | bytes 12296 | tf_op jit(solution)/shard_map/ppermute | solution.py:43
  172.3 4.2 %collective-permute-done.12 = f32[8,128]{1,0:T(8,128)S(1)} collective-permute-done((f32[8,128]{1,0:T(8,128)S(1)}, f32[8,128]{1,0:T(8,128)S(1)}, u32[]{:S(2)}, u32[]{:S(2)}) %collective-permute-start.12) | collective-permute-done | bytes 4128 | tf_op jit(solution)/shard_map/ppermute | solution.py:43
  (85 shorter events, 41.8 us)
Async XLA Ops:
  7.2 169.3 %copy-start = (bf16[8192,128]{1,0:T(8,128)(2,1)S(1)}, bf16[8192,128]{1,0:T(8,128)(2,1)}, u32[]{:S(2)}) copy-start(bf16[8192,128]{1,0:T(8,128)(2,1)} %param.19) | copy-start | bytes 6291460
  7.2 24.8 %copy-start.5 = (bf16[832,512]{1,0:T(8,128)(2,1)S(1)}, bf16[832,512]{1,0:T(8,128)(2,1)}, u32[]{:S(2)}) copy-start(bf16[832,512]{1,0:T(8,128)(2,1)} %param.11) | copy-start | bytes 2555908
  7.2 67.5 %all-gather.2.cloned.1.call-start = ((), (), s32[]{:S(2)}) async-start(), calls=%async_computation.5 | async-start | bytes 2654208 | tf_op jit(solution)/shard_map/all_gather | solution.py:210
  34.1 4.9 %copy-start.6 = (bf16[256,832]{0,1:T(8,128)(2,1)S(1)}, bf16[256,832]{0,1:T(8,128)(2,1)}, u32[]{:S(2)}) copy-start(bf16[256,832]{0,1:T(8,128)(2,1)} %param.12) | copy-start | bytes 1277956
  34.1 5.9 %copy-start.7 = (bf16[256,832]{0,1:T(8,128)(2,1)S(1)}, bf16[256,832]{0,1:T(8,128)(2,1)}, u32[]{:S(2)}) copy-start(bf16[256,832]{0,1:T(8,128)(2,1)} %param.13) | copy-start | bytes 1277956
  34.1 43.5 %all-to-all-start.1 = ((bf16[4,832,512]{2,1,0:T(8,128)(2,1)}), bf16[4,832,512]{2,1,0:T(8,128)(2,1)}, u32[]{:S(2)}, u32[]{:S(2)}) async-start(bf16[4,832,512]{2,1,0:T(8,128)(2,1)} %broadcast_in_dim.15), calls=%async_computation.1 | async-start | bytes 6815744 | tf_op jit(solution)/shard_map/all_to_all | solution.py:28
  38.9 17.4 %copy-start.8 = (bf16[2,64,832]{2,1,0:T(8,128)(2,1)S(1)}, bf16[2,64,832]{2,1,0:T(8,128)(2,1)}, u32[]{:S(2)}) copy-start(bf16[2,64,832]{2,1,0:T(8,128)(2,1)} %param.18) | copy-start | bytes 638980
  43.6 0.7 collective-permute-start
  44.2 3.1 %collective-permute-start.1 = (bf16[1,64,256]{2,1,0:T(8,128)(2,1)S(1)}, bf16[1,64,256]{2,1,0:T(8,128)(2,1)S(1)}, u32[]{:S(2)}, u32[]{:S(2)}) collective-permute-start(bf16[1,64,256]{2,1,0:T(8,128)(2,1)S(1)} %bitcast.92), channel_id=1, source_target_pairs={{0,1},{1,0},{2,3},{3,2},{4,5},{5,4},{6,7},{7,6},{8,9},{9,8},{10,11... | collective-permute-start | bytes 98312 | tf_op jit(solution)/shard_map/ppermute | solution.py:70
  47.4 6.5 %collective-permute-start.2 = (bf16[2,64,256]{2,1,0:T(8,128)(2,1)S(1)}, bf16[2,64,256]{2,1,0:T(8,128)(2,1)S(1)}, u32[]{:S(2)}, u32[]{:S(2)}) collective-permute-start(bf16[2,64,256]{2,1,0:T(8,128)(2,1)S(1)} %maximum_select_fusion.2), channel_id=1, source_target_pairs={{0,2},{2,0},{1,3},{3,1},{4,6},{6,4},{5,7},{7,5},{8,10},{10,8},{9,1... | collective-permute-start | bytes 196616 | tf_op jit(solution)/shard_map/ppermute | solution.py:70
  53.9 10.4 %collective-permute-start.3 = (bf16[4,64,256]{2,1,0:T(8,128)(2,1)S(1)}, bf16[4,64,256]{2,1,0:T(8,128)(2,1)S(1)}, u32[]{:S(2)}, u32[]{:S(2)}) collective-permute-start(bf16[4,64,256]{2,1,0:T(8,128)(2,1)S(1)} %maximum_select_fusion.1), channel_id=1, source_target_pairs={{0,4},{4,0},{1,5},{5,1},{2,6},{6,2},{3,7},{7,3},{8,12},{12,8},{9,1... | collective-permute-start | bytes 393224 | tf_op jit(solution)/shard_map/ppermute | solution.py:70
  74.7 16.1 %collective-permute-start.4 = (bf16[512,2304]{1,0:T(8,128)(2,1)}, bf16[512,2304]{1,0:T(8,128)(2,1)}, u32[]{:S(2)}, u32[]{:S(2)}) collective-permute-start(bf16[512,2304]{1,0:T(8,128)(2,1)} %bitcast.72), channel_id=1, source_target_pairs={{0,1},{1,0},{2,3},{3,2},{4,5},{5,4},{6,7},{7,6},{8,9},{9,8},{10,11... | collective-permute-start | bytes 7077896 | tf_op jit(solution)/shard_map/ppermute | solution.py:36
  84.2 37.1 %all-to-all-start.2 = ((bf16[4,832,128]{2,1,0:T(8,128)(2,1)}), bf16[4,832,128]{2,1,0:T(8,128)(2,1)S(1)}, u32[]{:S(2)}, u32[]{:S(2)}) async-start(bf16[4,832,128]{2,1,0:T(8,128)(2,1)} %bitcast.76), calls=%async_computation.2 | async-start | bytes 1703936 | tf_op jit(solution)/shard_map/all_to_all | solution.py:28
  96.9 28.1 %collective-permute-start.5 = (bf16[832,128]{1,0:T(8,128)(2,1)}, bf16[832,128]{1,0:T(8,128)(2,1)}, u32[]{:S(2)}, u32[]{:S(2)}) collective-permute-start(bf16[832,128]{1,0:T(8,128)(2,1)} %get-tuple-element.51), channel_id=1, source_target_pairs={{0,128},{128,256},{256,384},{384,0},{1,129},{129,257},{257,385},{3... | collective-permute-start | bytes 638984 | tf_op jit(solution)/shard_map/ppermute | solution.py:51
  101.7 30.0 %collective-permute-start.6 = (bf16[832,128]{1,0:T(8,128)(2,1)S(1)}, bf16[832,128]{1,0:T(8,128)(2,1)}, u32[]{:S(2)}, u32[]{:S(2)}) collective-permute-start(bf16[832,128]{1,0:T(8,128)(2,1)S(1)} %get-tuple-element.50), channel_id=1, source_target_pairs={{0,256},{128,384},{256,0},{384,128},{1,257},{129,385},{257,1},{385... | collective-permute-start | bytes 638984 | tf_op jit(solution)/shard_map/ppermute | solution.py:51
  107.2 24.5 %collective-permute-start.7 = (bf16[832,128]{1,0:T(8,128)(2,1)S(1)}, bf16[832,128]{1,0:T(8,128)(2,1)}, u32[]{:S(2)}, u32[]{:S(2)}) collective-permute-start(bf16[832,128]{1,0:T(8,128)(2,1)S(1)} %get-tuple-element.49), channel_id=1, source_target_pairs={{0,384},{128,0},{256,128},{384,256},{1,385},{129,1},{257,129},{385... | collective-permute-start | bytes 638984 | tf_op jit(solution)/shard_map/ppermute | solution.py:51
  125.0 13.0 %copy-start.10 = (f32[128,128]{1,0:T(8,128)S(1)}, f32[128,128]{1,0:T(8,128)}, u32[]{:S(2)}) copy-start(f32[128,128]{1,0:T(8,128)} %get-tuple-element.41) | copy-start | bytes 196612
  134.7 3.3 %collective-permute-start.8 = (f32[128,128]{1,0:T(8,128)}, f32[128,128]{1,0:T(8,128)S(1)}, u32[]{:S(2)}, u32[]{:S(2)}) collective-permute-start(f32[128,128]{1,0:T(8,128)} %get-tuple-element.47), channel_id=1, source_target_pairs={{0,1},{1,0},{2,3},{3,2},{4,5},{5,4},{6,7},{7,6},{8,9},{9,8},{10,11... | collective-permute-start | bytes 196616 | tf_op jit(solution)/shard_map/ppermute | solution.py:36
  138.1 8.7 %collective-permute-start.9 = (f32[8,8,128]{2,1,0:T(8,128)S(1)}, f32[8,8,128]{2,1,0:T(8,128)S(1)}, u32[]{:S(2)}, u32[]{:S(2)}) collective-permute-start(f32[8,8,128]{2,1,0:T(8,128)S(1)} %dynamic-slice_bitcast_fusion), channel_id=1, source_target_pairs={{0,2},{2,0},{1,3},{3,1},{4,6},{6,4},{5,7},{7,5},{8,10},{10,8},{9,1... | collective-permute-start | bytes 98312 | tf_op jit(solution)/shard_map/ppermute | solution.py:43
  140.0 19.9 %all-to-all-start.3 = ((bf16[16,8,960]{2,1,0:T(8,128)(2,1)}), bf16[16,8,960]{2,1,0:T(8,128)(2,1)S(1)}, u32[]{:S(2)}, u32[]{:S(2)}) async-start(bf16[16,8,960]{2,1,0:T(8,128)(2,1)} %bitcast.86), calls=%async_computation.3 | async-start | bytes 524288 | tf_op jit(solution)/shard_map/all_to_all | solution.py:28
  146.8 5.9 %collective-permute-start.10 = (f32[4,8,128]{2,1,0:T(8,128)S(1)}, f32[4,8,128]{2,1,0:T(8,128)S(1)}, u32[]{:S(2)}, u32[]{:S(2)}) collective-permute-start(f32[4,8,128]{2,1,0:T(8,128)S(1)} %dynamic-slice_bitcast_fusion.1), channel_id=1, source_target_pairs={{0,4},{4,0},{1,5},{5,1},{2,6},{6,2},{3,7},{7,3},{8,12},{12,8},{9,1... | collective-permute-start | bytes 49160 | tf_op jit(solution)/shard_map/ppermute | solution.py:43
  152.7 14.3 %collective-permute-start.11 = (f32[2,8,128]{2,1,0:T(8,128)S(1)}, f32[2,8,128]{2,1,0:T(8,128)S(1)}, u32[]{:S(2)}, u32[]{:S(2)}) collective-permute-start(f32[2,8,128]{2,1,0:T(8,128)S(1)} %dynamic-slice_bitcast_fusion.2), channel_id=1, source_target_pairs={{0,8},{8,0},{16,24},{24,16},{1,9},{9,1},{17,25},{25,17},{2,10},{10... | collective-permute-start | bytes 24584 | tf_op jit(solution)/shard_map/ppermute | solution.py:43
  160.6 18.3 %all-to-all-start.4 = ((bf16[16,8,960]{2,1,0:T(8,128)(2,1)}), bf16[16,8,960]{2,1,0:T(8,128)(2,1)S(1)}, u32[]{:S(2)}, u32[]{:S(2)}) async-start(bf16[16,8,960]{2,1,0:T(8,128)(2,1)} %broadcast_in_dim.17), calls=%async_computation.4 | async-start | bytes 524288 | tf_op jit(solution)/shard_map/all_to_all | solution.py:28
  167.0 9.4 %collective-permute-start.12 = (f32[8,128]{1,0:T(8,128)S(1)}, f32[8,128]{1,0:T(8,128)S(1)}, u32[]{:S(2)}, u32[]{:S(2)}) collective-permute-start(f32[8,128]{1,0:T(8,128)S(1)} %dynamic-slice_bitcast_fusion.3), channel_id=1, source_target_pairs={{0,16},{8,24},{16,0},{24,8},{1,17},{9,25},{17,1},{25,9},{2,18},{10... | collective-permute-start | bytes 12296 | tf_op jit(solution)/shard_map/ppermute | solution.py:43
  (6 other events, 15.2 us)
Sparse Core Ops, SparseCore 0:
  32.1 42.4 all-gather.1

commit v6 on v5

--- a/solution.py
+++ b/solution.py
@@ -231,11 +231,11 @@
         *other_parts, other_gate, other_up, other_saved, b_gate, b_up, first, partial_down
     )
     sums = jnp.sum(exchange(sums.reshape(16, 8, 960), DP).astype(F32), axis=0).astype(BF16)
-    rank_grad = (own_rank + swap_cores(other_rank)).reshape(8, 2, 8, 128)
-    rank_grad = halve(rank_grad, 1, "zl", 2, 1)
-    rank_grad = halve(rank_grad.reshape(4, 2, 8, 128), 1, "yl", 2, 1)
-    rank_grad = halve(rank_grad.reshape(2, 2, 8, 128), 1, "yh", 4, 1)
-    rank_grad = halve(rank_grad.reshape(2, 8, 128), 0, "yh", 4, 2)
+    rank_grad = (own_rank + swap_cores(other_rank)).reshape(2, 2, 2, 2, 8, 128)
+    rank_grad = halve(rank_grad, 0, "yh", 4, 2)
+    rank_grad = halve(rank_grad, 2, "zl", 2, 1)
+    rank_grad = halve(rank_grad, 0, "yh", 4, 1)
+    rank_grad = halve(rank_grad, 0, "yl", 2, 1)
     rank_grad = rank_grad.astype(BF16)
     sums = spread(sums, DP, 16).astype(F32)
     grad_b_in = sums[:, :, 128:].reshape(2, 64, 832)

time: 188 us -> 191 us (1.016)
  the two profiles are of different devices: /device:TPU:8 before, /device:TPU:16 now
where the time goes in v6:
time: 191 us; the launch traced here: 190 us
  starting transfers between devices  64.5 us (34%)
  waiting for transfers between devices  49.2 us (26%)
  blocking collectives  22.8 us (12%)
  local copies, waits for them, and re-layouts  19.3 us (10%)
  between operations  14.6 us (8%)
  Pallas kernels  11.1 us (6%)
  matrix products  6.3 us (3%)
  other arithmetic  2.48 us (1%)
    all_to_all x1, blocking collectives, exchange(): return lax.all_to_all(blocks, axes, 0, 0, tiled=True)  22.8 us
    all_to_all x4, starting transfers between devices, exchange(): return lax.all_to_all(blocks, axes, 0, 0, tiled=True)  21.8 us
    ppermute x3, starting transfers between devices, by_permutes(): lax.ppermute(block, 'zh', [(i, (i + step) % 4) for i in range(4)])  15.8 us
    all_to_all x4, waiting for transfers between devices, exchange(): return lax.all_to_all(blocks, axes, 0, 0, tiled=True)  15.4 us
    ppermute x4, starting transfers between devices, halve(): return kept + lax.ppermute(sent, axis, [(i, i ^ bit) for i in range(size)])  12.8 us
    ppermute x3, waiting for transfers between devices, join(): other = lax.ppermute(array, axis, [(0, 1), (1, 0)])  8.76 us
    ppermute x3, starting transfers between devices, join(): other = lax.ppermute(array, axis, [(0, 1), (1, 0)])  8.02 us
    ppermute x4, waiting for transfers between devices, halve(): return kept + lax.ppermute(sent, axis, [(i, i ^ bit) for i in range(size)])  7.84 us
  transfers between devices with their start and end apart: 18, of which 14 were waited for; matrix products, arithmetic and copies ran while one was open for 12% of the time, Pallas kernels for 4%

profile of v6, /device:TPU:16, one launch (start us, length us, event | category | flops | bytes accessed | tf_op | source)
XLA Modules:
  0.0 190.2 jit_solution(8959625567944821837)
XLA Ops:
  9.1 22.8 %all_to_all.26 = bf16[8,8,2304]{2,1,0:T(8,128)(2,1)} all-to-all(bf16[8,8,2304]{2,1,0:T(8,128)(2,1)S(1)} %bitcast.78), channel_id=1, replica_groups=mesh['zh'=4,'x'=4,'yh'=4,'yl'=2,'zl'=2,'c'=2] {'zh','zl'}, dimensions={0} | all-to-all | bytes 589824 | tf_op jit(solution)/shard_map/all_to_all | solution.py:28
  31.9 3.2 %broadcast_in_dim.15 = bf16[4,832,512]{2,1,0:T(8,128)(2,1)} broadcast(bf16[832,512]{1,0:T(8,128)(2,1)} %param.11), dimensions={1,2} | broadcast | bytes 4259840 | tf_op jit(solution)/shard_map/broadcast_in_dim | solution.py:208
  35.1 4.8 %all-to-all-start.1 = ((bf16[4,832,512]{2,1,0:T(8,128)(2,1)}), bf16[4,832,512]{2,1,0:T(8,128)(2,1)}, u32[]{:S(2)}, u32[]{:S(2)}) async-start(bf16[4,832,512]{2,1,0:T(8,128)(2,1)} %broadcast_in_dim.15), calls=%async_computation.1 | async-start | bytes 6815744 | tf_op jit(solution)/shard_map/all_to_all | solution.py:28
  46.8 6.6 %collective-permute-done = bf16[64,256]{1,0:T(8,128)(2,1)S(1)} collective-permute-done((bf16[64,256]{1,0:T(8,128)(2,1)S(1)}, bf16[64,256]{1,0:T(8,128)(2,1)S(1)}, u32[]{:S(2)}, u32[]{:S(2)}) %collective-permute-start) | collective-permute-done | bytes 32800 | tf_op jit(solution)/shard_map/ppermute | solution.py:213
  59.2 3.6 %collective-permute-done.2 = bf16[2,64,256]{2,1,0:T(8,128)(2,1)S(1)} collective-permute-done((bf16[2,64,256]{2,1,0:T(8,128)(2,1)S(1)}, bf16[2,64,256]{2,1,0:T(8,128)(2,1)S(1)}, u32[]{:S(2)}, u32[]{:S(2)}) %collective-permute-start.2) | collective-permute-done | bytes 65568 | tf_op jit(solution)/shard_map/ppermute | solution.py:70
  62.7 3.5 %collective-permute-start.3 = (bf16[4,64,256]{2,1,0:T(8,128)(2,1)S(1)}, bf16[4,64,256]{2,1,0:T(8,128)(2,1)S(1)}, u32[]{:S(2)}, u32[]{:S(2)}) collective-permute-start(bf16[4,64,256]{2,1,0:T(8,128)(2,1)S(1)} %maximum_select_fusion.1), channel_id=1, source_target_pairs={{0,4},{4,0},{1,5},{5,1},{2,6},{6,2},{3,7},{7,3},{8,12},{12,8},{9,1... | collective-permute-start | bytes 393224 | tf_op jit(solution)/shard_map/ppermute | solution.py:70
  67.7 4.0 %collective-permute-done.3 = bf16[4,64,256]{2,1,0:T(8,128)(2,1)S(1)} collective-permute-done((bf16[4,64,256]{2,1,0:T(8,128)(2,1)S(1)}, bf16[4,64,256]{2,1,0:T(8,128)(2,1)S(1)}, u32[]{:S(2)}, u32[]{:S(2)}) %collective-permute-start.3) | collective-permute-done | bytes 131104 | tf_op jit(solution)/shard_map/ppermute | solution.py:70
  75.6 3.1 %all-to-all-done.1 = bf16[4,832,512]{2,1,0:T(8,128)(2,1)} async-done(((bf16[4,832,512]{2,1,0:T(8,128)(2,1)}), bf16[4,832,512]{2,1,0:T(8,128)(2,1)}, u32[]{:S(2)}, u32[]{:S(2)}) %all-to-all-start.1) | async-done | bytes 3407904 | tf_op jit(solution)/shard_map/all_to_all | solution.py:28
  85.2 4.9 %all-to-all-start.2 = ((bf16[4,832,128]{2,1,0:T(8,128)(2,1)}), bf16[4,832,128]{2,1,0:T(8,128)(2,1)S(1)}, u32[]{:S(2)}, u32[]{:S(2)}) async-start(bf16[4,832,128]{2,1,0:T(8,128)(2,1)} %bitcast.74), calls=%async_computation.2 | async-start | bytes 1703936 | tf_op jit(solution)/shard_map/all_to_all | solution.py:28
  96.2 4.8 %collective-permute-start.5 = (bf16[832,128]{1,0:T(8,128)(2,1)}, bf16[832,128]{1,0:T(8,128)(2,1)}, u32[]{:S(2)}, u32[]{:S(2)}) collective-permute-start(bf16[832,128]{1,0:T(8,128)(2,1)} %get-tuple-element.51), channel_id=1, source_target_pairs={{0,128},{128,256},{256,384},{384,0},{1,129},{129,257},{257,385},{3... | collective-permute-start | bytes 638984 | tf_op jit(solution)/shard_map/ppermute | solution.py:51
  101.0 5.5 %collective-permute-start.6 = (bf16[832,128]{1,0:T(8,128)(2,1)S(1)}, bf16[832,128]{1,0:T(8,128)(2,1)}, u32[]{:S(2)}, u32[]{:S(2)}) collective-permute-start(bf16[832,128]{1,0:T(8,128)(2,1)S(1)} %get-tuple-element.50), channel_id=1, source_target_pairs={{0,256},{128,384},{256,0},{384,128},{1,257},{129,385},{257,1},{385... | collective-permute-start | bytes 638984 | tf_op jit(solution)/shard_map/ppermute | solution.py:51
  106.5 5.5 %collective-permute-start.7 = (bf16[832,128]{1,0:T(8,128)(2,1)S(1)}, bf16[832,128]{1,0:T(8,128)(2,1)}, u32[]{:S(2)}, u32[]{:S(2)}) collective-permute-start(bf16[832,128]{1,0:T(8,128)(2,1)S(1)} %get-tuple-element.49), channel_id=1, source_target_pairs={{0,384},{128,0},{256,128},{384,256},{1,385},{129,1},{257,129},{385... | collective-permute-start | bytes 638984 | tf_op jit(solution)/shard_map/ppermute | solution.py:51
  112.7 2.7 %shard_map.122 = (bf16[128,128]{1,0:T(8,128)(2,1)}, bf16[128,128]{1,0:T(8,128)(2,1)}, bf16[64,256]{1,0:T(8,128)(2,1)}) custom-call(s32[3]{0:T(128)} %pad_add_fusion.place_ref, bf16[512,2304]{1,0:T(8,128)(2,1)} %bitcast.71, bf16[512,2304]{1,0:T(8,128)(2,1)} %collective-permute-done.4.other_band_ref.other_ranks_ref, bf16[512,2304]{1,0:T(8,128)(2,1)} %bitcast.72, ...), custom_call_target="tpu_custom_call" | custom-call | flops 33554432 | bytes 1048576 | tf_op jit(solution)/shard_map/pallas_call | solution.py:173
  116.8 5.1 %all-to-all-done.2.parts_ref = bf16[4,832,128]{2,1,0:T(8,128)(2,1)S(1)} async-done(((bf16[4,832,128]{2,1,0:T(8,128)(2,1)}), bf16[4,832,128]{2,1,0:T(8,128)(2,1)S(1)}, u32[]{:S(2)}, u32[]{:S(2)}) %all-to-all-start.2) | async-done | bytes 852000 | tf_op jit(solution)/shard_map/all_to_all | solution.py:28
  122.8 2.8 %shard_map.123 = (f32[128,128]{1,0:T(8,128)}, f32[128,832]{1,0:T(8,128)}) custom-call(bf16[4,832,128]{2,1,0:T(8,128)(2,1)} %copy-done.2, f32[832,128]{1,0:T(8,128)} %get-tuple-element.35.gate_ref, f32[832,128]{1,0:T(8,128)} %get-tuple-element.36.up_ref, bf16[128,128]{1,0:T(8,128)(2,1)} %get-tuple-element.38.saved_ref, ...), custom_call_target="tpu_custom_call" | custom-call | flops 100000000 | bytes 3145728 | tf_op jit(solution)/shard_map/pallas_call | solution.py:111
  125.6 7.7 %collective-permute-done.6.c_ref = bf16[832,128]{1,0:T(8,128)(2,1)} collective-permute-done((bf16[832,128]{1,0:T(8,128)(2,1)S(1)}, bf16[832,128]{1,0:T(8,128)(2,1)}, u32[]{:S(2)}, u32[]{:S(2)}) %collective-permute-start.6) | collective-permute-done | bytes 213024 | tf_op jit(solution)/shard_map/ppermute | solution.py:51
  133.3 3.0 %shard_map.124 = (f32[128,128]{1,0:T(8,128)}, bf16[128,960]{1,0:T(8,128)(2,1)}) custom-call(bf16[832,128]{1,0:T(8,128)(2,1)} %get-tuple-element.52.a_ref, bf16[832,128]{1,0:T(8,128)(2,1)} %collective-permute-done.5.b_ref, bf16[832,128]{1,0:T(8,128)(2,1)} %collective-permute-done.6.c_ref, bf16[832,128]{1,0:T(8,128)(2,1)} %collective-permute-done.7.d_ref, ...), custom_call_target="tpu_custom_call" | custom-call | flops 100000000 | bytes 3145728 | tf_op jit(solution)/shard_map/pallas_call | solution.py:122
  139.6 4.6 %collective-permute-start.9 = (f32[2,2,2,8,128]{4,3,2,1,0:T(8,128)S(1)}, f32[2,2,2,8,128]{4,3,2,1,0:T(8,128)S(1)}, u32[]{:S(2)}, u32[]{:S(2)}) collective-permute-start(f32[2,2,2,8,128]{4,3,2,1,0:T(8,128)S(1)} %dynamic-slice_bitcast_fusion), channel_id=1, source_target_pairs={{0,16},{8,24},{16,0},{24,8},{1,17},{9,25},{17,1},{25,9},{2,18},{10... | collective-permute-start | bytes 98312 | tf_op jit(solution)/shard_map/ppermute | solution.py:43
  144.3 4.4 %all-to-all-start.3 = ((bf16[16,8,960]{2,1,0:T(8,128)(2,1)}), bf16[16,8,960]{2,1,0:T(8,128)(2,1)S(1)}, u32[]{:S(2)}, u32[]{:S(2)}) async-start(bf16[16,8,960]{2,1,0:T(8,128)(2,1)} %bitcast.84), calls=%async_computation.3 | async-start | bytes 524288 | tf_op jit(solution)/shard_map/all_to_all | solution.py:28
  152.1 4.5 %collective-permute-done.10 = f32[2,2,8,128]{3,2,1,0:T(8,128)S(1)} collective-permute-done((f32[2,2,8,128]{3,2,1,0:T(8,128)S(1)}, f32[2,2,8,128]{3,2,1,0:T(8,128)S(1)}, u32[]{:S(2)}, u32[]{:S(2)}) %collective-permute-start.10) | collective-permute-done | bytes 16416 | tf_op jit(solution)/shard_map/ppermute | solution.py:43
  159.3 2.7 %all-to-all-done.3 = bf16[16,8,960]{2,1,0:T(8,128)(2,1)S(1)} async-done(((bf16[16,8,960]{2,1,0:T(8,128)(2,1)}), bf16[16,8,960]{2,1,0:T(8,128)(2,1)S(1)}, u32[]{:S(2)}, u32[]{:S(2)}) %all-to-all-start.3) | async-done | bytes 245792 | tf_op jit(solution)/shard_map/all_to_all | solution.py:28
  162.8 7.7 %all-to-all-start.4 = ((bf16[16,8,960]{2,1,0:T(8,128)(2,1)}), bf16[16,8,960]{2,1,0:T(8,128)(2,1)S(1)}, u32[]{:S(2)}, u32[]{:S(2)}) async-start(bf16[16,8,960]{2,1,0:T(8,128)(2,1)} %broadcast_in_dim.17), calls=%async_computation.4 | async-start | bytes 524288 | tf_op jit(solution)/shard_map/all_to_all | solution.py:28
  170.5 2.8 %collective-permute-start.12 = (f32[8,128]{1,0:T(8,128)S(1)}, f32[8,128]{1,0:T(8,128)S(1)}, u32[]{:S(2)}, u32[]{:S(2)}) collective-permute-start(f32[8,128]{1,0:T(8,128)S(1)} %dynamic-slice_bitcast_fusion.3), channel_id=1, source_target_pairs={{0,4},{4,0},{1,5},{5,1},{2,6},{6,2},{3,7},{7,3},{8,12},{12,8},{9,1... | collective-permute-start | bytes 12296 | tf_op jit(solution)/shard_map/ppermute | solution.py:43
  177.4 4.6 %all-to-all-done.4 = bf16[16,8,960]{2,1,0:T(8,128)(2,1)S(1)} async-done(((bf16[16,8,960]{2,1,0:T(8,128)(2,1)}), bf16[16,8,960]{2,1,0:T(8,128)(2,1)S(1)}, u32[]{:S(2)}, u32[]{:S(2)}) %all-to-all-start.4) | async-done | bytes 245792 | tf_op jit(solution)/shard_map/all_to_all | solution.py:28
  (83 shorter events, 50.8 us)
Async XLA Ops:
  7.2 168.9 %copy-start = (bf16[8192,128]{1,0:T(8,128)(2,1)S(1)}, bf16[8192,128]{1,0:T(8,128)(2,1)}, u32[]{:S(2)}) copy-start(bf16[8192,128]{1,0:T(8,128)(2,1)} %param.19) | copy-start | bytes 6291460
  7.2 66.5 %all-gather.2.cloned.1.call-start = ((), (), s32[]{:S(2)}) async-start(), calls=%async_computation.5 | async-start | bytes 2654208 | tf_op jit(solution)/shard_map/all_gather | solution.py:210
  35.1 4.9 %copy-start.5 = (bf16[256,832]{0,1:T(8,128)(2,1)S(1)}, bf16[256,832]{0,1:T(8,128)(2,1)}, u32[]{:S(2)}) copy-start(bf16[256,832]{0,1:T(8,128)(2,1)} %param.12) | copy-start | bytes 1277956
  35.1 5.9 %copy-start.6 = (bf16[256,832]{0,1:T(8,128)(2,1)S(1)}, bf16[256,832]{0,1:T(8,128)(2,1)}, u32[]{:S(2)}) copy-start(bf16[256,832]{0,1:T(8,128)(2,1)} %param.13) | copy-start | bytes 1277956
  35.1 43.5 %all-to-all-start.1 = ((bf16[4,832,512]{2,1,0:T(8,128)(2,1)}), bf16[4,832,512]{2,1,0:T(8,128)(2,1)}, u32[]{:S(2)}, u32[]{:S(2)}) async-start(bf16[4,832,512]{2,1,0:T(8,128)(2,1)} %broadcast_in_dim.15), calls=%async_computation.1 | async-start | bytes 6815744 | tf_op jit(solution)/shard_map/all_to_all | solution.py:28
  39.9 4.7 %copy-start.10 = (bf16[64,256]{1,0:T(8,128)(2,1)S(1)}, bf16[64,256]{1,0:T(8,128)(2,1)}, u32[]{:S(2)}) copy-start(bf16[64,256]{1,0:T(8,128)(2,1)} %param.17) | copy-start | bytes 98308
  40.0 26.3 %copy-start.7 = (bf16[2,64,832]{2,1,0:T(8,128)(2,1)S(1)}, bf16[2,64,832]{2,1,0:T(8,128)(2,1)}, u32[]{:S(2)}) copy-start(bf16[2,64,832]{2,1,0:T(8,128)(2,1)} %param.18) | copy-start | bytes 638980
  44.6 8.8 %collective-permute-start = (bf16[64,256]{1,0:T(8,128)(2,1)S(1)}, bf16[64,256]{1,0:T(8,128)(2,1)S(1)}, u32[]{:S(2)}, u32[]{:S(2)}) collective-permute-start(bf16[64,256]{1,0:T(8,128)(2,1)S(1)} %copy-done.10), channel_id=1, source_target_pairs={{0,0},{1,1},{2,2},{3,3},{4,4},{5,5},{6,6},{7,7},{128,8},{129,9},{1... | collective-permute-start | bytes 98312 | tf_op jit(solution)/shard_map/ppermute | solution.py:213
  53.5 3.1 %collective-permute-start.1 = (bf16[1,64,256]{2,1,0:T(8,128)(2,1)S(1)}, bf16[1,64,256]{2,1,0:T(8,128)(2,1)S(1)}, u32[]{:S(2)}, u32[]{:S(2)}) collective-permute-start(bf16[1,64,256]{2,1,0:T(8,128)(2,1)S(1)} %bitcast.86), channel_id=1, source_target_pairs={{0,1},{1,0},{2,3},{3,2},{4,5},{5,4},{6,7},{7,6},{8,9},{9,8},{10,11... | collective-permute-start | bytes 98312 | tf_op jit(solution)/shard_map/ppermute | solution.py:70
  56.6 6.2 %collective-permute-start.2 = (bf16[2,64,256]{2,1,0:T(8,128)(2,1)S(1)}, bf16[2,64,256]{2,1,0:T(8,128)(2,1)S(1)}, u32[]{:S(2)}, u32[]{:S(2)}) collective-permute-start(bf16[2,64,256]{2,1,0:T(8,128)(2,1)S(1)} %maximum_select_fusion.2), channel_id=1, source_target_pairs={{0,2},{2,0},{1,3},{3,1},{4,6},{6,4},{5,7},{7,5},{8,10},{10,8},{9,1... | collective-permute-start | bytes 196616 | tf_op jit(solution)/shard_map/ppermute | solution.py:70
  62.7 9.0 %collective-permute-start.3 = (bf16[4,64,256]{2,1,0:T(8,128)(2,1)S(1)}, bf16[4,64,256]{2,1,0:T(8,128)(2,1)S(1)}, u32[]{:S(2)}, u32[]{:S(2)}) collective-permute-start(bf16[4,64,256]{2,1,0:T(8,128)(2,1)S(1)} %maximum_select_fusion.1), channel_id=1, source_target_pairs={{0,4},{4,0},{1,5},{5,1},{2,6},{6,2},{3,7},{7,3},{8,12},{12,8},{9,1... | collective-permute-start | bytes 393224 | tf_op jit(solution)/shard_map/ppermute | solution.py:70
  73.7 16.5 %collective-permute-start.4 = (bf16[512,2304]{1,0:T(8,128)(2,1)}, bf16[512,2304]{1,0:T(8,128)(2,1)}, u32[]{:S(2)}, u32[]{:S(2)}) collective-permute-start(bf16[512,2304]{1,0:T(8,128)(2,1)} %bitcast.70), channel_id=1, source_target_pairs={{0,1},{1,0},{2,3},{3,2},{4,5},{5,4},{6,7},{7,6},{8,9},{9,8},{10,11... | collective-permute-start | bytes 7077896 | tf_op jit(solution)/shard_map/ppermute | solution.py:36
  85.2 36.7 %all-to-all-start.2 = ((bf16[4,832,128]{2,1,0:T(8,128)(2,1)}), bf16[4,832,128]{2,1,0:T(8,128)(2,1)S(1)}, u32[]{:S(2)}, u32[]{:S(2)}) async-start(bf16[4,832,128]{2,1,0:T(8,128)(2,1)} %bitcast.74), calls=%async_computation.2 | async-start | bytes 1703936 | tf_op jit(solution)/shard_map/all_to_all | solution.py:28
  96.2 29.4 %collective-permute-start.5 = (bf16[832,128]{1,0:T(8,128)(2,1)}, bf16[832,128]{1,0:T(8,128)(2,1)}, u32[]{:S(2)}, u32[]{:S(2)}) collective-permute-start(bf16[832,128]{1,0:T(8,128)(2,1)} %get-tuple-element.51), channel_id=1, source_target_pairs={{0,128},{128,256},{256,384},{384,0},{1,129},{129,257},{257,385},{3... | collective-permute-start | bytes 638984 | tf_op jit(solution)/shard_map/ppermute | solution.py:51
  101.0 32.2 %collective-permute-start.6 = (bf16[832,128]{1,0:T(8,128)(2,1)S(1)}, bf16[832,128]{1,0:T(8,128)(2,1)}, u32[]{:S(2)}, u32[]{:S(2)}) collective-permute-start(bf16[832,128]{1,0:T(8,128)(2,1)S(1)} %get-tuple-element.50), channel_id=1, source_target_pairs={{0,256},{128,384},{256,0},{384,128},{1,257},{129,385},{257,1},{385... | collective-permute-start | bytes 638984 | tf_op jit(solution)/shard_map/ppermute | solution.py:51
  106.5 26.8 %collective-permute-start.7 = (bf16[832,128]{1,0:T(8,128)(2,1)S(1)}, bf16[832,128]{1,0:T(8,128)(2,1)}, u32[]{:S(2)}, u32[]{:S(2)}) collective-permute-start(bf16[832,128]{1,0:T(8,128)(2,1)S(1)} %get-tuple-element.49), channel_id=1, source_target_pairs={{0,384},{128,0},{256,128},{384,256},{1,385},{129,1},{257,129},{385... | collective-permute-start | bytes 638984 | tf_op jit(solution)/shard_map/ppermute | solution.py:51
  125.6 14.0 %copy-start.9 = (f32[128,128]{1,0:T(8,128)S(1)}, f32[128,128]{1,0:T(8,128)}, u32[]{:S(2)}) copy-start(f32[128,128]{1,0:T(8,128)} %get-tuple-element.41) | copy-start | bytes 196612
  136.2 3.3 %collective-permute-start.8 = (f32[128,128]{1,0:T(8,128)}, f32[128,128]{1,0:T(8,128)S(1)}, u32[]{:S(2)}, u32[]{:S(2)}) collective-permute-start(f32[128,128]{1,0:T(8,128)} %get-tuple-element.47), channel_id=1, source_target_pairs={{0,1},{1,0},{2,3},{3,2},{4,5},{5,4},{6,7},{7,6},{8,9},{9,8},{10,11... | collective-permute-start | bytes 196616 | tf_op jit(solution)/shard_map/ppermute | solution.py:36
  139.6 9.7 %collective-permute-start.9 = (f32[2,2,2,8,128]{4,3,2,1,0:T(8,128)S(1)}, f32[2,2,2,8,128]{4,3,2,1,0:T(8,128)S(1)}, u32[]{:S(2)}, u32[]{:S(2)}) collective-permute-start(f32[2,2,2,8,128]{4,3,2,1,0:T(8,128)S(1)} %dynamic-slice_bitcast_fusion), channel_id=1, source_target_pairs={{0,16},{8,24},{16,0},{24,8},{1,17},{9,25},{17,1},{25,9},{2,18},{10... | collective-permute-start | bytes 98312 | tf_op jit(solution)/shard_map/ppermute | solution.py:43
  144.3 17.8 %all-to-all-start.3 = ((bf16[16,8,960]{2,1,0:T(8,128)(2,1)}), bf16[16,8,960]{2,1,0:T(8,128)(2,1)S(1)}, u32[]{:S(2)}, u32[]{:S(2)}) async-start(bf16[16,8,960]{2,1,0:T(8,128)(2,1)} %bitcast.84), calls=%async_computation.3 | async-start | bytes 524288 | tf_op jit(solution)/shard_map/all_to_all | solution.py:28
  149.4 7.3 %collective-permute-start.10 = (f32[2,2,8,128]{3,2,1,0:T(8,128)S(1)}, f32[2,2,8,128]{3,2,1,0:T(8,128)S(1)}, u32[]{:S(2)}, u32[]{:S(2)}) collective-permute-start(f32[2,2,8,128]{3,2,1,0:T(8,128)S(1)} %dynamic-slice_bitcast_fusion.1), channel_id=1, source_target_pairs={{0,2},{2,0},{1,3},{3,1},{4,6},{6,4},{5,7},{7,5},{8,10},{10,8},{9,1... | collective-permute-start | bytes 49160 | tf_op jit(solution)/shard_map/ppermute | solution.py:43
  156.6 13.9 %collective-permute-start.11 = (f32[2,8,128]{2,1,0:T(8,128)S(1)}, f32[2,8,128]{2,1,0:T(8,128)S(1)}, u32[]{:S(2)}, u32[]{:S(2)}) collective-permute-start(f32[2,8,128]{2,1,0:T(8,128)S(1)} %dynamic-slice_bitcast_fusion.2), channel_id=1, source_target_pairs={{0,8},{8,0},{16,24},{24,16},{1,9},{9,1},{17,25},{25,17},{2,10},{10... | collective-permute-start | bytes 24584 | tf_op jit(solution)/shard_map/ppermute | solution.py:43
  162.8 19.1 %all-to-all-start.4 = ((bf16[16,8,960]{2,1,0:T(8,128)(2,1)}), bf16[16,8,960]{2,1,0:T(8,128)(2,1)S(1)}, u32[]{:S(2)}, u32[]{:S(2)}) async-start(bf16[16,8,960]{2,1,0:T(8,128)(2,1)} %broadcast_in_dim.17), calls=%async_computation.4 | async-start | bytes 524288 | tf_op jit(solution)/shard_map/all_to_all | solution.py:28
  170.5 5.5 %collective-permute-start.12 = (f32[8,128]{1,0:T(8,128)S(1)}, f32[8,128]{1,0:T(8,128)S(1)}, u32[]{:S(2)}, u32[]{:S(2)}) collective-permute-start(f32[8,128]{1,0:T(8,128)S(1)} %dynamic-slice_bitcast_fusion.3), channel_id=1, source_target_pairs={{0,4},{4,0},{1,5},{5,1},{2,6},{6,2},{3,7},{7,3},{8,12},{12,8},{9,1... | collective-permute-start | bytes 12296 | tf_op jit(solution)/shard_map/ppermute | solution.py:43
  (5 other events, 10.5 us)
Sparse Core Ops, SparseCore 0:
  32.0 41.5 all-gather.1
